TPU v7x, 32 devices: a whole 2x2x4 slice. The times are simulated.
32 devices in a mesh: pre: 4 (over x, core), seq: 8 (over z, y).
Axes of the slice: x: 2, y: 2, z: 4, core: 2. Of those that a mesh axis runs over, the one named last changes fastest.
Arguments:
- prefix_in: bfloat16 [8, 512, 2048], P('seq', 'pre'), may hold values from -13 to 13
- later_in: bfloat16 [8, 768, 2048], P('seq', 'pre'), may hold values from -13 to 13
- doc_lengths: int32 [8, 4], P('seq'), may hold values from 1 to 384, 768 in all within a row
- doc_exit: int32 [8, 4], P('seq'), may hold values from 1 to 24
- token_skip: int32 [8, 768], P('seq'), may hold values 0 or 1
- first_gain: bfloat16 [2048], P('seq'), may hold values from 0.5 to 1.5
- first_bias: bfloat16 [2048], P('seq'), may hold values from -1.25 to 1.25
- qkv_weight: bfloat16 [2048, 6144], P('seq'), may hold values from -0.125 to 0.125
- query_bias: bfloat16 [2048], P('seq'), may hold values from -3 to 3
- value_bias: bfloat16 [2048], P('seq'), may hold values from -1.75 to 1.75
- out_weight: bfloat16 [2048, 2048], P('seq'), may hold values from -1 to 1
- out_bias: bfloat16 [2048], P('seq'), may hold values from -1.25 to 1.25
- second_gain: bfloat16 [2048], P('seq'), may hold values from 0.5 to 1.5
- second_bias: bfloat16 [2048], P('seq'), may hold values from -1.25 to 1.25
- up_weight: bfloat16 [2048, 8192], P('seq'), may hold values from -0.125 to 0.125
- up_bias: bfloat16 [8192], P('seq'), may hold values from -1.75 to 1.75
- down_weight: bfloat16 [2048, 8192], P('seq'), may hold values from -0.0625 to 0.0625
- down_bias: bfloat16 [2048], P('seq'), may hold values from -1.25 to 1.25
- prefix_cot: bfloat16 [8, 512, 2048], P('seq', 'pre'), may hold values from -6 to 6
- later_cot: bfloat16 [8, 768, 2048], P('seq', 'pre'), may hold values from -6 to 6
Outputs:
- prefix_out: bfloat16 [8, 512, 2048], P('seq', 'pre')
- later_out: bfloat16 [8, 768, 2048], P('seq', 'pre')
- prefix_grad: bfloat16 [8, 512, 2048], P('seq', 'pre')
- later_grad: bfloat16 [8, 768, 2048], P('seq', 'pre')
- first_gain_grad: float32 [2048], P('seq')
- first_bias_grad: float32 [2048], P('seq')
- qkv_weight_grad: float32 [2048, 6144], P('seq')
- query_bias_grad: float32 [2048], P('seq')
- value_bias_grad: float32 [2048], P('seq')
- out_weight_grad: float32 [2048, 2048], P('seq')
- out_bias_grad: float32 [2048], P('seq')
- second_gain_grad: float32 [2048], P('seq')
- second_bias_grad: float32 [2048], P('seq')
- up_weight_grad: float32 [2048, 8192], P('seq')
- up_bias_grad: float32 [8192], P('seq')
- down_weight_grad: float32 [2048, 8192], P('seq')
- down_bias_grad: float32 [2048], P('seq')
- residual_rms: float32 [3], replicated
Inputs may be any that keep to these rules, and one draw needn't show every extreme that they name: `doc_lengths`: each row's 4 lengths sum to 768; the longest in each row is exactly 384.
All inputs are finite; a program needn't handle non-finite values. No bound on the sum of `token_skip` on one device may be relied on, other than what follows from the above.
Results may differ from a plain program's by a relative error of at most 0.018.
Values may be sent and summed in bfloat16 or wider, within the bound.
A program may use at most 768 MiB of HBM per device.

v0:
```python
from functools import reduce
import math

import jax
import jax.numpy as jnp
from jax import lax
from jax.sharding import PartitionSpec as P

D = 2048
HEADS = 32
HEAD_DIM = 64
FF = 8192
LAYER = 12
PRE = 512


EPS = 1e-05
NEG = -1e30


def layer_norm_parts(values, gain, bias):
    mean = jnp.mean(values, axis=-1, keepdims=True)
    centred = values - mean
    variance = jnp.mean(centred * centred, axis=-1, keepdims=True)
    scaling = lax.rsqrt(variance + EPS)
    normed = centred * scaling
    return (normed * gain + bias, normed, scaling)


def norm_back(grad, normed, scaling, gain):
    scaled = grad * gain
    inner = jnp.mean(scaled, axis=-1, keepdims=True)
    cross = jnp.mean(scaled * normed, axis=-1, keepdims=True)
    return scaling * (scaled - inner - normed * cross)


def gelu_slope(upper):
    cumulative = 0.5 * (1.0 + lax.erf(upper * (1.0 / math.sqrt(2.0))))
    density = jnp.exp(-0.5 * upper * upper) * (1.0 / math.sqrt(2.0 * math.pi))
    return cumulative + upper * density


def token_tables(doc_lengths, doc_exit, token_skip):
    ends = jnp.cumsum(doc_lengths, axis=-1, dtype=jnp.int32)
    starts = ends - doc_lengths
    places = jnp.arange(token_skip.shape[-1], dtype=jnp.int32)
    doc_id = (
        jnp.sum(
            (places[:, None] >= starts[..., None, :]).astype(jnp.int32), axis=-1, dtype=jnp.int32
        )
        - 1
    )
    kinds = jnp.arange(doc_lengths.shape[-1], dtype=jnp.int32)
    live_doc = doc_exit > LAYER
    live = jnp.any((doc_id[..., None] == kinds) & live_doc[..., None, :], axis=-1) & (
        token_skip == 0
    )
    return (doc_id, live)


def split_pairs(pairs):
    rows, count = (pairs.shape[0], pairs.shape[1])
    keys_h = pairs[..., :D].reshape(rows, count, HEADS, HEAD_DIM)
    values_h = pairs[..., D:].reshape(rows, count, HEADS, HEAD_DIM)
    return (keys_h, values_h)


def score_block(queries, keys_h, mask):
    scores = jnp.einsum("bqhd,bkhd->bhqk", queries, keys_h, preferred_element_type=jnp.float32)
    if mask is None:
        return scores
    return jnp.where(mask[:, None], scores, NEG)


def attend(queries, key_sets, masks):
    blocks = [
        score_block(queries, split_pairs(pairs)[0], mask) for pairs, mask in zip(key_sets, masks)
    ]
    top = reduce(jnp.maximum, [jnp.max(block, axis=-1) for block in blocks])
    powers = [jnp.exp(block - top[..., None]) for block in blocks]
    total = reduce(jnp.add, [jnp.sum(power, axis=-1) for power in powers])
    mixed = 0.0
    for power, pairs in zip(powers, key_sets):
        weights = (power / total[..., None]).astype(jnp.bfloat16)
        mixed = mixed + jnp.einsum(
            "bhqk,bkhd->bqhd", weights, split_pairs(pairs)[1], preferred_element_type=jnp.float32
        )
    return (mixed, top, total)


def attend_back(queries, key_sets, masks, top, total, grad_out):
    probs_all = []
    dprob_all = []
    for pairs, mask in zip(key_sets, masks):
        keys_h, values_h = split_pairs(pairs)
        block = score_block(queries, keys_h, mask)
        probs_all.append(jnp.exp(block - top[..., None]) / total[..., None])
        dprob_all.append(
            jnp.einsum("bqhd,bkhd->bhqk", grad_out, values_h, preferred_element_type=jnp.float32)
        )
    delta = reduce(
        jnp.add, [jnp.sum(probs * dprob, axis=-1) for probs, dprob in zip(probs_all, dprob_all)]
    )
    query_grad = 0.0
    parts = []
    for probs, dprob, pairs in zip(probs_all, dprob_all, key_sets):
        score_grad = (probs * (dprob - delta[..., None])).astype(jnp.bfloat16)
        query_grad = query_grad + jnp.einsum(
            "bhqk,bkhd->bqhd", score_grad, split_pairs(pairs)[0], preferred_element_type=jnp.float32
        )
        parts.append((score_grad, probs.astype(jnp.bfloat16)))
    return (query_grad, parts)


def pair_grads(score_grad, weights, queries, grad_out):
    key_grad = jnp.einsum(
        "bhqk,bqhd->bkhd", score_grad, queries, preferred_element_type=jnp.float32
    )
    value_grad = jnp.einsum(
        "bhqk,bqhd->bkhd", weights, grad_out, preferred_element_type=jnp.float32
    )
    count = key_grad.shape[1]
    return jnp.concatenate(
        [key_grad[0].reshape(count, D), value_grad[0].reshape(count, D)], axis=-1
    )


def terms_from(lefts, rights):
    sliced = [part for part in lefts]
    contract = (((0,), (0,)), ((), ()))
    return jnp.concatenate(
        [
            lax.dot_general(left, right, contract, preferred_element_type=jnp.float32)
            for left, right in zip(sliced, rights)
        ],
        axis=1,
    )


def on_device(
    prefix_in,
    later_in,
    doc_lengths,
    doc_exit,
    token_skip,
    first_gain,
    first_bias,
    qkv_weight,
    query_bias,
    value_bias,
    out_weight,
    out_bias,
    second_gain,
    second_bias,
    up_weight,
    up_bias,
    down_weight,
    down_bias,
    prefix_cot,
    later_cot,
):
    scale = 1.0 / math.sqrt(HEAD_DIM)
    pre_part = prefix_in.shape[1]
    later_part = later_in.shape[1]
    seq_count = lax.axis_size("seq")
    pre_count = lax.axis_size("pre")
    seq_place = lax.axis_index("seq")
    pre_place = lax.axis_index("pre")
    tokens = jnp.concatenate([prefix_in[0], later_in[0]], axis=0).astype(jnp.float32)
    (
        full_first_gain,
        full_first_bias,
        full_qkv,
        full_query_bias,
        full_value_bias,
        full_out,
        full_out_bias,
        full_second_gain,
        full_second_bias,
        full_up,
        full_up_bias,
        full_down,
        full_down_bias,
    ) = (
        lax.all_gather(first_gain, "seq", axis=0, tiled=True),
        lax.all_gather(first_bias, "seq", axis=0, tiled=True),
        lax.all_gather(qkv_weight, "seq", axis=0, tiled=True),
        lax.all_gather(query_bias, "seq", axis=0, tiled=True),
        lax.all_gather(value_bias, "seq", axis=0, tiled=True),
        lax.all_gather(out_weight, "seq", axis=0, tiled=True),
        lax.all_gather(out_bias, "seq", axis=0, tiled=True),
        lax.all_gather(second_gain, "seq", axis=0, tiled=True),
        lax.all_gather(second_bias, "seq", axis=0, tiled=True),
        lax.all_gather(up_weight, "seq", axis=0, tiled=True),
        lax.all_gather(up_bias, "seq", axis=0, tiled=True),
        lax.all_gather(down_weight, "seq", axis=0, tiled=True),
        lax.all_gather(down_bias, "seq", axis=0, tiled=True),
    )
    doc_id, live = token_tables(doc_lengths, doc_exit, token_skip)
    start_col = pre_place * later_part
    doc_here = lax.dynamic_slice_in_dim(doc_id, start_col, later_part, 1)
    live_here = lax.dynamic_slice_in_dim(live, start_col, later_part, 1)
    active = jnp.concatenate([jnp.ones((pre_part,), jnp.float32), live_here[0].astype(jnp.float32)])
    later_places = jnp.arange(token_skip.shape[1], dtype=jnp.int32)
    query_places = start_col + jnp.arange(later_part, dtype=jnp.int32)
    later_mask = (
        (later_places[None, :] <= query_places[:, None])
        & (doc_here[0][:, None] == doc_id[0][None, :])
        & live[0][None, :]
    )[None]
    prefix_places = pre_place * pre_part + jnp.arange(pre_part, dtype=jnp.int32)
    prefix_mask = (jnp.arange(PRE, dtype=jnp.int32)[None, :] <= prefix_places[:, None])[None]
    first_out, first_normed, first_scaling = layer_norm_parts(
        tokens, full_first_gain.astype(jnp.float32), full_first_bias.astype(jnp.float32)
    )
    first_h = first_out.astype(jnp.bfloat16)
    projected = jnp.dot(first_h, full_qkv, preferred_element_type=jnp.float32)
    queries = ((projected[:, :D] + full_query_bias.astype(jnp.float32)) * scale).astype(
        jnp.bfloat16
    )
    pairs = jnp.concatenate(
        [projected[:, D : 2 * D], projected[:, 2 * D :] + full_value_bias.astype(jnp.float32)],
        axis=1,
    ).astype(jnp.bfloat16)
    whole_prefix, whole_later = (
        lax.all_gather(pairs[:pre_part], "pre", axis=0, tiled=True),
        lax.all_gather(pairs[pre_part:], "pre", axis=0, tiled=True),
    )
    whole_prefix = whole_prefix[None]
    whole_later = whole_later[None]
    prefix_queries = queries[:pre_part].reshape(1, pre_part, HEADS, HEAD_DIM)
    later_queries = queries[pre_part:].reshape(1, later_part, HEADS, HEAD_DIM)
    prefix_mixed, prefix_top, prefix_total = attend(prefix_queries, [whole_prefix], [prefix_mask])
    later_mixed, later_top, later_total = attend(
        later_queries, [whole_prefix, whole_later], [None, later_mask]
    )
    mixed = jnp.concatenate(
        [prefix_mixed.reshape(pre_part, D), later_mixed.reshape(later_part, D)], axis=0
    ).astype(jnp.bfloat16)
    attn = jnp.dot(mixed, full_out, preferred_element_type=jnp.float32) + full_out_bias.astype(
        jnp.float32
    )
    middle = tokens + attn
    second_out, second_normed, second_scaling = layer_norm_parts(
        middle, full_second_gain.astype(jnp.float32), full_second_bias.astype(jnp.float32)
    )
    second_h = second_out.astype(jnp.bfloat16)
    upper = jnp.dot(second_h, full_up, preferred_element_type=jnp.float32) + full_up_bias.astype(
        jnp.float32
    )
    acted = jax.nn.gelu(upper, approximate=False).astype(jnp.bfloat16)
    ffn = lax.dot_general(
        acted, full_down, (((1,), (1,)), ((), ())), preferred_element_type=jnp.float32
    ) + full_down_bias.astype(jnp.float32)
    result = tokens + active[:, None] * (attn + ffn)
    square_sums = jnp.stack(
        [
            jnp.sum(active * jnp.sum(result * result, axis=-1)),
            jnp.sum(active * jnp.sum(attn * attn, axis=-1)),
            jnp.sum(active * jnp.sum(ffn * ffn, axis=-1)),
            jnp.sum(active),
        ]
    )
    cotangent = jnp.concatenate([prefix_cot[0], later_cot[0]], axis=0).astype(jnp.float32)
    ffn_grad = (active[:, None] * cotangent).astype(jnp.bfloat16)
    full_first_gain, full_qkv, full_out, full_second_gain, full_up, full_down = (
        lax.all_gather(first_gain, "seq", axis=0, tiled=True),
        lax.all_gather(qkv_weight, "seq", axis=0, tiled=True),
        lax.all_gather(out_weight, "seq", axis=0, tiled=True),
        lax.all_gather(second_gain, "seq", axis=0, tiled=True),
        lax.all_gather(up_weight, "seq", axis=0, tiled=True),
        lax.all_gather(down_weight, "seq", axis=0, tiled=True),
    )
    acted_grad = jnp.dot(ffn_grad, full_down, preferred_element_type=jnp.float32)
    upper_grad = (acted_grad * gelu_slope(upper)).astype(jnp.bfloat16)
    second_grad = jnp.dot(upper_grad, full_up.T, preferred_element_type=jnp.float32)
    middle_grad = norm_back(
        second_grad, second_normed, second_scaling, full_second_gain.astype(jnp.float32)
    )
    attn_grad = (active[:, None] * cotangent + middle_grad).astype(jnp.bfloat16)
    mixed_grad = jnp.dot(attn_grad, full_out.T, preferred_element_type=jnp.float32).astype(
        jnp.bfloat16
    )
    prefix_out_grad = mixed_grad[:pre_part].reshape(1, pre_part, HEADS, HEAD_DIM)
    later_out_grad = mixed_grad[pre_part:].reshape(1, later_part, HEADS, HEAD_DIM)
    prefix_query_grad, prefix_parts = attend_back(
        prefix_queries, [whole_prefix], [prefix_mask], prefix_top, prefix_total, prefix_out_grad
    )
    later_query_grad, later_parts = attend_back(
        later_queries,
        [whole_prefix, whole_later],
        [None, later_mask],
        later_top,
        later_total,
        later_out_grad,
    )
    prefix_term = pair_grads(
        prefix_parts[0][0], prefix_parts[0][1], prefix_queries, prefix_out_grad
    ) + pair_grads(later_parts[0][0], later_parts[0][1], later_queries, later_out_grad)
    later_term = pair_grads(later_parts[1][0], later_parts[1][1], later_queries, later_out_grad)
    prefix_pair_grads, later_pair_grads = (
        lax.psum_scatter(
            prefix_term.astype(jnp.bfloat16), "pre", scatter_dimension=0, tiled=True
        ).astype(jnp.float32),
        lax.psum_scatter(
            later_term.astype(jnp.bfloat16), "pre", scatter_dimension=0, tiled=True
        ).astype(jnp.float32),
    )
    rounded_query = jnp.concatenate(
        [prefix_query_grad.reshape(pre_part, D), later_query_grad.reshape(later_part, D)], axis=0
    ).astype(jnp.bfloat16)
    query_grad = (rounded_query.astype(jnp.float32) * scale).astype(jnp.bfloat16)
    pair_grad = jnp.concatenate([prefix_pair_grads, later_pair_grads], axis=0).astype(jnp.bfloat16)
    project_grad = jnp.concatenate([query_grad, pair_grad], axis=1)
    first_grad = jnp.dot(project_grad, full_qkv.T, preferred_element_type=jnp.float32)
    input_grad = (
        cotangent
        + middle_grad
        + norm_back(first_grad, first_normed, first_scaling, full_first_gain.astype(jnp.float32))
    )
    lefts = (first_h, mixed, second_h, ffn_grad)
    rights = (project_grad, attn_grad, upper_grad, acted)
    block_rows = qkv_weight.shape[0] // pre_count
    count_rows = first_h.shape[0]

    def reorder(left):
        return (
            left.reshape(count_rows, seq_count, pre_count, block_rows)
            .transpose(0, 2, 1, 3)
            .reshape(count_rows, D)
        )

    reordered = tuple((reorder(part) for part in lefts))
    own_block = lax.psum_scatter(
        terms_from(reordered, rights), ("pre", "seq"), scatter_dimension=0, tiled=True
    )
    weight_share = lax.all_gather(own_block.astype(jnp.bfloat16), "pre", axis=0, tiled=True).astype(
        own_block.dtype
    )
    totals = lax.psum(
        (
            square_sums,
            jnp.sum(first_grad * first_normed, axis=0),
            jnp.sum(first_grad, axis=0),
            jnp.sum(query_grad.astype(jnp.float32), axis=0),
            jnp.sum(pair_grad[:, D:].astype(jnp.float32), axis=0),
            jnp.sum(attn_grad.astype(jnp.float32), axis=0),
            jnp.sum(second_grad * second_normed, axis=0),
            jnp.sum(second_grad, axis=0),
            jnp.sum(upper_grad.astype(jnp.float32), axis=0),
            jnp.sum(ffn_grad.astype(jnp.float32), axis=0),
        ),
        ("pre", "seq"),
    )

    def own_share(vector):
        width = vector.shape[0] // seq_count
        return lax.dynamic_slice_in_dim(vector, seq_place * width, width, 0)

    residual_rms = jnp.sqrt(totals[0][:3] / (totals[0][3] * D))
    prefix_out = result[:pre_part][None].astype(jnp.bfloat16)
    later_out = result[pre_part:][None].astype(jnp.bfloat16)
    prefix_grad = input_grad[:pre_part][None].astype(jnp.bfloat16)
    later_grad = input_grad[pre_part:][None].astype(jnp.bfloat16)
    return (
        prefix_out,
        later_out,
        prefix_grad,
        later_grad,
        own_share(totals[1]),
        own_share(totals[2]),
        weight_share[:, : 3 * D],
        own_share(totals[3]),
        own_share(totals[4]),
        weight_share[:, 3 * D : 4 * D],
        own_share(totals[5]),
        own_share(totals[6]),
        own_share(totals[7]),
        weight_share[:, 4 * D : 4 * D + FF],
        own_share(totals[8]),
        weight_share[:, 4 * D + FF :],
        own_share(totals[9]),
        residual_rms,
    )


def solution(mesh):
    placed = (
        P("seq", "pre", None),
        P("seq", "pre", None),
        P("seq", None),
        P("seq", None),
        P("seq", None),
        P("seq"),
        P("seq"),
        P("seq", None),
        P("seq"),
        P("seq"),
        P("seq", None),
        P("seq"),
        P("seq"),
        P("seq"),
        P("seq", None),
        P("seq"),
        P("seq", None),
        P("seq"),
        P("seq", "pre", None),
        P("seq", "pre", None),
    )
    return jax.shard_map(
        on_device,
        mesh=mesh,
        in_specs=placed,
        out_specs=(
            P("seq", "pre", None),
            P("seq", "pre", None),
            P("seq", "pre", None),
            P("seq", "pre", None),
            P("seq"),
            P("seq"),
            P("seq", None),
            P("seq"),
            P("seq"),
            P("seq", None),
            P("seq"),
            P("seq"),
            P("seq"),
            P("seq", None),
            P("seq"),
            P("seq", None),
            P("seq"),
            P(),
        ),
        check_vma=False,
    )
```

profile of v0, /device:TPU:5, one launch (start us, length us, event | category | flops | bytes accessed | tf_op | source)
XLA Modules:
  0.0 4278.0 jit_solution(287303370636174228)
XLA Ops:
  10.6 43.1 %all-gather.2 = bf16[8,1,256]{2,1,0:T(2,128)(2,1)S(1)} all-gather(bf16[1,1,256]{2,1,0:T(2,128)(2,1)S(1)} %reshape.627), channel_id=1, replica_groups=mesh['pre'=4,'seq'=8] {'seq'}, dimensions={0}, use_global_device_ids=true | all-gather | bytes 4608 | tf_op jit(solution)/shard_map/all_gather | solution.py:189
  53.8 22.2 all-gather.3
  75.9 19.2 all-gather
  95.7 18.0 all-gather.1
  116.5 374.4 %all-gather.16.cloned.1.call-done = bf16[2048,6144]{1,0:T(8,128)(2,1)} async-done(((bf16[256,6144]{1,0:T(8,128)(2,1)}), bf16[2048,6144]{1,0:T(8,128)(2,1)}) %all-gather.16.cloned.1.call-update) | async-done | bytes 25165840 | tf_op jit(solution)/shard_map/all_gather | solution.py:187
  524.7 15.5 all-gather.5
  552.7 20.8 all_gather.66
  656.0 60.3 %all-gather.22.cloned.1.call-done = bf16[2048,2048]{1,0:T(8,128)(2,1)} async-done(((bf16[256,2048]{1,0:T(8,128)(2,1)}), bf16[2048,2048]{1,0:T(8,128)(2,1)}) %all-gather.22.cloned.1.call-update) | async-done | bytes 8388624 | tf_op jit(solution)/shard_map/all_gather | solution.py:190
  726.9 627.2 %all-gather.24.cloned.1.call-done = bf16[2048,8192]{1,0:T(8,128)(2,1)} async-done(((bf16[256,8192]{1,0:T(8,128)(2,1)}), bf16[2048,8192]{1,0:T(8,128)(2,1)}) %all-gather.24.cloned.1.call-update) | async-done | bytes 33554448 | tf_op jit(solution)/shard_map/all_gather | solution.py:194
  1354.0 39.7 fusion.8
  1393.7 599.4 %all-gather.26.cloned.1.call-done = bf16[2048,8192]{1,0:T(8,128)(2,1)} async-done(((bf16[256,8192]{1,0:T(8,128)(2,1)}), bf16[2048,8192]{1,0:T(8,128)(2,1)}) %all-gather.26.cloned.1.call-update) | async-done | bytes 33554448 | tf_op jit(solution)/shard_map/all_gather | solution.py:196
  1993.2 23.4 convert_reduce_fusion
  2016.6 20.3 multiply_reduce_fusion.6
  2076.4 16.0 multiply_reduce_fusion
  2126.4 16.7 multiply_convert_fusion
  2218.9 28.5 fusion.108
  2247.4 28.0 fusion.109
  2280.6 23.0 fusion.62
  2303.6 130.7 %pad_maximum_fusion = f32[2048,24576]{1,0:T(8,128)} fusion(f32[2048,8192]{1,0:T(8,128)} %fusion.109, f32[2048,8192]{1,0:T(8,128)} %fusion.108, f32[2048,2048]{1,0:T(8,128)} %fusion.107, f32[2048,6144]{1,0:T(8,128)} %fusion.62), kind=kLoop, calls=%fused_computation.1 | loop fusion | flops 150994944 | bytes 402653184 | tf_op jit(solution)/shard_map/concatenate | solution.py:131
  2448.5 25.8 convolution_add_fusion.1
  2476.4 24.7 fusion.49
  2505.1 1528.0 %reduce-scatter.8.cloned.1.call-done = f32[64,24576]{1,0:T(8,128)} async-done(((f32[2048,24576]{1,0:T(8,128)}), f32[64,24576]{1,0:T(8,128)}) %reduce-scatter.8.cloned.1.call-update) | async-done | bytes 6291472 | tf_op jit(solution)/shard_map/reduce_scatter | solution.py:334
  4046.5 118.1 %all-reduce.4.cloned.1.call-done = (f32[2048]{0:T(1024)}, f32[2048]{0:T(1024)}, f32[2048]{0:T(1024)}, f32[2048]{0:T(1024)}, f32[2048]{0:T(1024)}, /*index=5*/f32...) async-done(((f32[2048]{0:T(1024)}, f32[2048]{0:T(1024)}, f32[2048]{0:T(1024)}, f32[2048]{0:T(1024)}, f32[2048]{0:T(1024)}, ...) | async-done | bytes 98336 | tf_op jit(solution)/shard_map/psum | solution.py:340
  4179.4 71.7 %all-gather.28.cloned.1.call-done = bf16[256,24576]{1,0:T(8,128)(2,1)} async-done(((bf16[64,24576]{1,0:T(8,128)(2,1)}), bf16[256,24576]{1,0:T(8,128)(2,1)}) %all-gather.28.cloned.1.call-update) | async-done | bytes 12582928 | tf_op jit(solution)/shard_map/all_gather | solution.py:337
  (370 shorter events, 367.1 us)
Async XLA Ops:
  7.2 483.7 %all-gather.16.cloned.1.call-start = ((), (), s32[]{:S(2)}) async-start(), calls=%async_computation.3 | async-start | bytes 28311552 | tf_op jit(solution)/shard_map/all_gather | solution.py:187
  7.9 568.6 %all-gather.18.cloned.1.call-start = ((), (), s32[]{:S(2)}) async-start(), calls=%async_computation.4 | async-start | bytes 5242880 | tf_op jit(solution)/shard_map/all_gather | solution.py:226
  95.7 407.8 %copy-start.66 = (f32[8,1,256]{2,1,0:T(1,128)}, f32[8,1,256]{2,1,0:T(1,128)S(1)}, u32[]{:S(2)}) copy-start(f32[8,1,256]{2,1,0:T(1,128)S(1)} %convert_element_type.212) | copy-start | bytes 24580
  506.6 97.9 %all-gather.20.cloned.1.call-start = ((), (), s32[]{:S(2)}) async-start(), calls=%async_computation.5 | async-start | bytes 7864320 | tf_op jit(solution)/shard_map/all_gather | solution.py:227
  507.9 208.4 %all-gather.22.cloned.1.call-start = ((), (), s32[]{:S(2)}) async-start(), calls=%async_computation.6 | async-start | bytes 9437184 | tf_op jit(solution)/shard_map/all_gather | solution.py:190
  508.6 845.4 %all-gather.24.cloned.1.call-start = ((), (), s32[]{:S(2)}) async-start(), calls=%async_computation.7 | async-start | bytes 37748736 | tf_op jit(solution)/shard_map/all_gather | solution.py:194
  509.2 1484.0 %all-gather.26.cloned.1.call-start = ((), (), s32[]{:S(2)}) async-start(), calls=%async_computation.8 | async-start | bytes 37748736 | tf_op jit(solution)/shard_map/all_gather | solution.py:196
  509.8 1765.7 %reduce-scatter.10.cloned.1.call-start = ((), (), s32[]{:S(2)}) async-start(), calls=%async_computation.11 | async-start | bytes 5242880
  540.3 1496.6 %copy-start.53 = (f32[8,1,256]{2,1,0:T(1,128)}, f32[8,1,256]{2,1,0:T(1,128)S(1)}, u32[]{:S(2)}) copy-start(f32[8,1,256]{2,1,0:T(1,128)S(1)} %convert_element_type.217) | copy-start | bytes 24580
  724.8 1312.1 %copy-start.2 = (f32[320,2048]{1,0:T(8,128)}, f32[320,2048]{1,0:T(8,128)S(1)}, u32[]{:S(2)}) copy-start(f32[320,2048]{1,0:T(8,128)S(1)} %get-tuple-element.50) | copy-start | bytes 7864324
  724.8 1312.1 %copy-start.59 = (f32[320]{0:T(512)}, f32[320]{0:T(512)S(1)}, u32[]{:S(2)}) copy-start(f32[320]{0:T(512)S(1)} %broadcast_multiply_fusion.4) | copy-start | bytes 3844
  725.2 1311.7 %copy-start.64 = (f32[320]{0:T(512)}, f32[320]{0:T(512)S(1)}, u32[]{:S(2)}) copy-start(f32[320]{0:T(512)S(1)} %add_rsqrt_fusion) | copy-start | bytes 3844
  726.9 1266.3 %copy-start.26 = (bf16[1,192,2048]{2,1,0:T(8,128)(2,1)S(1)}, bf16[1,192,2048]{2,1,0:T(8,128)(2,1)}, u32[]{:S(2)}) copy-start(bf16[1,192,2048]{2,1,0:T(8,128)(2,1)} %param.39) | copy-start | bytes 2359300
  726.9 1266.3 %copy-start.75 = (f32[320]{0:T(512)S(1)}, f32[320]{0:T(512)}, u32[]{:S(2)}) copy-start(f32[320]{0:T(512)} %pad_convert_fusion) | copy-start | bytes 3844
  2126.4 150.7 %reduce-scatter.12.cloned.1.call-start = ((), (), s32[]{:S(2)}) async-start(), calls=%async_computation.12 | async-start | bytes 7864320
  2174.0 1859.1 %reduce-scatter.8.cloned.1.call-start = ((), (), s32[]{:S(2)}) async-start(), calls=%async_computation.9 | async-start | bytes 207618048 | tf_op jit(solution)/shard_map/reduce_scatter | solution.py:334
  2434.4 1730.2 %all-reduce.4.cloned.1.call-start = ((), (), s32[]{:S(2)}) async-start(), calls=%async_computation.13 | async-start | bytes 197632 | tf_op jit(solution)/shard_map/psum | solution.py:340
  2505.0 1532.9 %copy-start.3 = (f32[320,2048]{1,0:T(8,128)S(1)}, f32[320,2048]{1,0:T(8,128)}, u32[]{:S(2)}) copy-start(f32[320,2048]{1,0:T(8,128)} %copy-done.2) | copy-start | bytes 7864324
  2505.0 1532.9 %copy-start.54 = (f32[8,1,256]{2,1,0:T(1,128)S(1)}, f32[8,1,256]{2,1,0:T(1,128)}, u32[]{:S(2)}) copy-start(f32[8,1,256]{2,1,0:T(1,128)} %copy-done.53) | copy-start | bytes 24580
  2505.0 1532.9 %copy-start.60 = (f32[320]{0:T(512)S(1)}, f32[320]{0:T(512)}, u32[]{:S(2)}) copy-start(f32[320]{0:T(512)} %copy-done.59) | copy-start | bytes 3844
  2505.0 1532.9 %copy-start.65 = (f32[320]{0:T(512)S(1)}, f32[320]{0:T(512)}, u32[]{:S(2)}) copy-start(f32[320]{0:T(512)} %copy-done.64) | copy-start | bytes 3844
  2505.1 1532.9 %copy-start.72 = (f32[320]{0:T(512)S(1)}, f32[320]{0:T(512)}, u32[]{:S(2)}) copy-start(f32[320]{0:T(512)} %copy-done.71) | copy-start | bytes 3844
  2505.1 1532.9 %copy-start.74 = (f32[320]{0:T(512)S(1)}, f32[320]{0:T(512)}, u32[]{:S(2)}) copy-start(f32[320]{0:T(512)} %copy-done.73) | copy-start | bytes 3844
  2505.1 1746.0 %all-gather.28.cloned.1.call-start = ((), (), s32[]{:S(2)}) async-start(), calls=%async_computation.10 | async-start | bytes 15728640 | tf_op jit(solution)/shard_map/all_gather | solution.py:337
  (87 other events, 2188.8 us)
Sparse Core Ops, SparseCore 0:
  9.6 481.2 all-gather.15
  506.7 35.8 all-gather.17
  544.7 46.3 all-gather.19
  593.1 123.1 all-gather.21
  717.7 636.3 all-gather.23
  1355.4 637.7 all-gather.25
  2126.5 45.4 reduce-scatter.9
  2175.2 58.3 reduce-scatter.11
  2434.5 1598.5 reduce-scatter.7
  4040.0 124.5 all-reduce.3
  4166.8 84.2 all-gather.27
where the time goes:
time: 4280 us
  waiting for transfers between devices  3380 us (79%)
  matrix products  362 us (8%)
  other arithmetic  223 us (5%)
  blocking collectives  179 us (4%)
  local copies, waits for them, and re-layouts  116 us (3%)
    reduce_scatter x1, waiting for transfers between devices, on_device(): lax.psum_scatter(terms_from(reordered, rights), ('pre', 'seq'), scatter_d...  1530 us
    all_gather x1, waiting for transfers between devices, on_device(): lax.all_gather(up_weight, 'seq', axis=0, tiled=True)  627 us
    all_gather x1, waiting for transfers between devices, on_device(): lax.all_gather(down_weight, 'seq', axis=0, tiled=True)  599 us
    all_gather x1, waiting for transfers between devices, on_device(): lax.all_gather(qkv_weight, 'seq', axis=0, tiled=True)  374 us
    concatenate x1, other arithmetic, terms_from(): jnp.concatenate([lax.dot_general(left, right, contract, preferred_element...  131 us
    psum x1, waiting for transfers between devices, on_device(): lax.psum((square_sums, jnp.sum(first_grad * first_normed, axis=0), jnp.su...  118 us
    dot_general x4, matrix products, terms_from(): lax.dot_general(left, right, contract, preferred_element_type=jnp.float32)  89.2 us
  transfers between devices with their start and end apart: 11, of which 7 were waited for; matrix products, arithmetic and copies ran while one was open for 9% of the time, Pallas kernels for 0%

commit v1 on v0

v1 whole, which is shorter than its diff:
```python
import functools
import math

import jax
import jax.numpy as jnp
from jax import lax
from jax.experimental import pallas as pl
from jax.experimental.pallas import tpu as pltpu
from jax.sharding import PartitionSpec as P

D = 2048
HEADS = 32
HEAD_DIM = 64
FF = 8192
LAYER = 12
PRE = 512

EPS = 1e-05
NEG = -1e30
BF = jnp.bfloat16
F32 = jnp.float32
TILE = 256


def layer_norm_parts(values, gain, bias):
    mean = jnp.mean(values, axis=-1, keepdims=True)
    centred = values - mean
    variance = jnp.mean(centred * centred, axis=-1, keepdims=True)
    scaling = lax.rsqrt(variance + EPS)
    normed = centred * scaling
    return (normed * gain + bias, normed, scaling)


def norm_back(grad, normed, scaling, gain):
    scaled = grad * gain
    inner = jnp.mean(scaled, axis=-1, keepdims=True)
    cross = jnp.mean(scaled * normed, axis=-1, keepdims=True)
    return scaling * (scaled - inner - normed * cross)


def gelu_slope(upper):
    cumulative = 0.5 * (1.0 + lax.erf(upper * (1.0 / math.sqrt(2.0))))
    density = jnp.exp(-0.5 * upper * upper) * (1.0 / math.sqrt(2.0 * math.pi))
    return cumulative + upper * density


def token_tables(doc_lengths, doc_exit, token_skip):
    order = jnp.arange(doc_lengths.shape[-1], dtype=jnp.int32)
    earlier = order[None, :] < order[:, None]
    starts = jnp.sum(
        jnp.where(earlier, doc_lengths[..., None, :], 0), axis=-1, dtype=jnp.int32
    )
    places = jnp.arange(token_skip.shape[-1], dtype=jnp.int32)
    doc_id = (
        jnp.sum(
            (places[:, None] >= starts[..., None, :]).astype(jnp.int32), axis=-1, dtype=jnp.int32
        )
        - 1
    )
    live_doc = doc_exit > LAYER
    live = jnp.any((doc_id[..., None] == order) & live_doc[..., None, :], axis=-1) & (
        token_skip == 0
    )
    return (doc_id, live)


def dot_nt(a, b):
    return lax.dot_general(a, b, (((1,), (1,)), ((), ())), preferred_element_type=F32)


def dot_nn(a, b):
    return lax.dot_general(a, b, (((1,), (0,)), ((), ())), preferred_element_type=F32)


def dot_tn(a, b):
    return lax.dot_general(a, b, (((0,), (0,)), ((), ())), preferred_element_type=F32)


def gather_positions(place, ref, whole, pre_part, later_part):
    parts = ref.shape[0]
    for member in range(parts):
        source = jnp.bitwise_xor(place, member)
        whole[member * pre_part : (member + 1) * pre_part, :] = ref[source, :pre_part, :]
        start = parts * pre_part + member * later_part
        whole[start : start + later_part, :] = ref[source, pre_part:, :]


def scatter_positions(place, whole, ref, pre_part, later_part, lanes):
    parts = ref.shape[0]
    for member in range(parts):
        target = jnp.bitwise_xor(place, member)
        ref[target, :pre_part, lanes] = whole[
            member * pre_part : (member + 1) * pre_part, :
        ].astype(ref.dtype)
        start = parts * pre_part + member * later_part
        ref[target, pre_part:, lanes] = whole[start : start + later_part, :].astype(ref.dtype)


def masked_scores(block, scores, tile, codes_q, codes_k):
    rows = lax.broadcasted_iota(jnp.int32, (TILE, TILE), 0)
    cols = lax.broadcasted_iota(jnp.int32, (TILE, TILE), 1)
    allowed = None
    if tile == block:
        allowed = cols <= rows
    if tile * TILE >= PRE:
        same = (
            codes_q[block * TILE : (block + 1) * TILE, :]
            == codes_k[:, tile * TILE : (tile + 1) * TILE]
        )
        allowed = same if allowed is None else allowed & same
    if allowed is None:
        return scores
    return jnp.where(allowed, scores, NEG)


def attend_kernel(
    pre_part, later_part, place_ref, q_ref, k_ref, v_ref, cq_ref, ck_ref, o_ref, stat_ref, q_all, k_all, v_all, o_all
):
    place = place_ref[0]
    gather_positions(place, q_ref, q_all, pre_part, later_part)
    gather_positions(place, k_ref, k_all, pre_part, later_part)
    gather_positions(place, v_ref, v_all, pre_part, later_part)
    codes_q = cq_ref[...]
    codes_k = ck_ref[...]
    blocks = q_all.shape[0] // TILE
    for head in range(2):
        lanes = slice(head * HEAD_DIM, (head + 1) * HEAD_DIM)
        for block in range(blocks):
            rows = slice(block * TILE, (block + 1) * TILE)
            queries = q_all[rows, lanes]
            scores = [
                masked_scores(
                    block,
                    dot_nt(queries, k_all[tile * TILE : (tile + 1) * TILE, lanes]),
                    tile,
                    codes_q,
                    codes_k,
                )
                for tile in range(block + 1)
            ]
            top = functools.reduce(jnp.maximum, [jnp.max(s, axis=1, keepdims=True) for s in scores])
            powers = [jnp.exp(s - top) for s in scores]
            total = functools.reduce(jnp.add, [jnp.sum(e, axis=1, keepdims=True) for e in powers])
            share = 1.0 / total
            mixed = functools.reduce(
                jnp.add,
                [
                    dot_nn((e * share).astype(BF), v_all[tile * TILE : (tile + 1) * TILE, lanes])
                    for tile, e in enumerate(powers)
                ],
            )
            o_all[rows, lanes] = mixed
            stat_ref[0, rows, lanes] = jnp.broadcast_to(top + jnp.log(total), (TILE, HEAD_DIM))
    scatter_positions(place, o_all, o_ref, pre_part, later_part, slice(None))


def attend(place, qkv, codes_q, codes_k, pre_part, later_part):
    parts, part, width = qkv.shape
    pairs = width // 3 // 128
    length = parts * part
    block = (parts, part, 128)
    return pl.pallas_call(
        functools.partial(attend_kernel, pre_part, later_part),
        out_shape=(
            jax.ShapeDtypeStruct((parts, part, width // 3), BF),
            jax.ShapeDtypeStruct((pairs, length, 128), F32),
        ),
        grid_spec=pltpu.PrefetchScalarGridSpec(
            num_scalar_prefetch=1,
            grid=(pairs,),
            in_specs=[
                pl.BlockSpec(block, lambda i, _: (0, 0, i)),
                pl.BlockSpec(block, lambda i, _: (0, 0, pairs + i)),
                pl.BlockSpec(block, lambda i, _: (0, 0, 2 * pairs + i)),
                pl.BlockSpec((length, 1), lambda i, _: (0, 0)),
                pl.BlockSpec((1, length), lambda i, _: (0, 0)),
            ],
            out_specs=[
                pl.BlockSpec(block, lambda i, _: (0, 0, i)),
                pl.BlockSpec((1, length, 128), lambda i, _: (i, 0, 0)),
            ],
            scratch_shapes=[
                pltpu.VMEM((length, 128), BF),
                pltpu.VMEM((length, 128), BF),
                pltpu.VMEM((length, 128), BF),
                pltpu.VMEM((length, 128), F32),
            ],
        ),
        compiler_params=pltpu.CompilerParams(vmem_limit_bytes=48 * 2**20),
        cost_estimate=pl.CostEstimate(
            flops=pairs * 2 * 15 * 4 * 2 * TILE * TILE * 256,
            bytes_accessed=length * width * 3,
            transcendentals=pairs * 2 * 15 * TILE * TILE,
        ),
        name="attend",
    )(place, qkv, qkv, qkv, codes_q, codes_k)


def attend_back_kernel(
    pre_part,
    later_part,
    pairs,
    place_ref,
    q_ref,
    k_ref,
    v_ref,
    do_ref,
    stat_ref,
    cq_ref,
    ck_ref,
    grad_ref,
    q_all,
    k_all,
    v_all,
    do_all,
    dq_all,
    dk_all,
    dv_all,
):
    place = place_ref[0]
    step = pl.program_id(0)
    gather_positions(place, q_ref, q_all, pre_part, later_part)
    gather_positions(place, k_ref, k_all, pre_part, later_part)
    gather_positions(place, v_ref, v_all, pre_part, later_part)
    gather_positions(place, do_ref, do_all, pre_part, later_part)
    codes_q = cq_ref[...]
    codes_k = ck_ref[...]
    dk_all[...] = jnp.zeros_like(dk_all)
    dv_all[...] = jnp.zeros_like(dv_all)
    blocks = q_all.shape[0] // TILE
    for head in range(2):
        lanes = slice(head * HEAD_DIM, (head + 1) * HEAD_DIM)
        for block in range(blocks):
            rows = slice(block * TILE, (block + 1) * TILE)
            queries = q_all[rows, lanes]
            grads = do_all[rows, lanes]
            level = stat_ref[0, rows, head * HEAD_DIM : head * HEAD_DIM + 1]
            probs = []
            dprobs = []
            for tile in range(block + 1):
                cols = slice(tile * TILE, (tile + 1) * TILE)
                scores = masked_scores(
                    block, dot_nt(queries, k_all[cols, lanes]), tile, codes_q, codes_k
                )
                probs.append(jnp.exp(scores - level))
                dprobs.append(dot_nt(grads, v_all[cols, lanes]))
            delta = functools.reduce(
                jnp.add, [jnp.sum(a * b, axis=1, keepdims=True) for a, b in zip(probs, dprobs)]
            )
            dq = None
            for tile in range(block + 1):
                cols = slice(tile * TILE, (tile + 1) * TILE)
                ds = (probs[tile] * (dprobs[tile] - delta)).astype(BF)
                part = dot_nn(ds, k_all[cols, lanes])
                dq = part if dq is None else dq + part
                dk_all[cols, lanes] += dot_tn(ds, queries)
                dv_all[cols, lanes] += dot_tn(probs[tile].astype(BF), grads)
            dq_all[rows, lanes] = dq * (1.0 / math.sqrt(HEAD_DIM))
    for third, source in enumerate((dq_all, dk_all, dv_all)):
        start = pl.multiple_of((third * pairs + step) * 128, 128)
        scatter_positions(place, source, grad_ref, pre_part, later_part, pl.ds(start, 128))


def attend_back(place, qkv, grad_out, stats, codes_q, codes_k, pre_part, later_part):
    parts, part, width = qkv.shape
    pairs = width // 3 // 128
    length = parts * part
    block = (parts, part, 128)
    return pl.pallas_call(
        functools.partial(attend_back_kernel, pre_part, later_part, pairs),
        out_shape=jax.ShapeDtypeStruct((parts, part, width), BF),
        grid_spec=pltpu.PrefetchScalarGridSpec(
            num_scalar_prefetch=1,
            grid=(pairs,),
            in_specs=[
                pl.BlockSpec(block, lambda i, _: (0, 0, i)),
                pl.BlockSpec(block, lambda i, _: (0, 0, pairs + i)),
                pl.BlockSpec(block, lambda i, _: (0, 0, 2 * pairs + i)),
                pl.BlockSpec(block, lambda i, _: (0, 0, i)),
                pl.BlockSpec((1, length, 128), lambda i, _: (i, 0, 0)),
                pl.BlockSpec((length, 1), lambda i, _: (0, 0)),
                pl.BlockSpec((1, length), lambda i, _: (0, 0)),
            ],
            out_specs=pl.BlockSpec((parts, part, width), lambda i, _: (0, 0, 0)),
            scratch_shapes=[pltpu.VMEM((length, 128), BF)] * 4 + [pltpu.VMEM((length, 128), F32)] * 3,
        ),
        compiler_params=pltpu.CompilerParams(vmem_limit_bytes=56 * 2**20),
        cost_estimate=pl.CostEstimate(
            flops=pairs * 2 * 15 * 10 * TILE * TILE * 256,
            bytes_accessed=length * width * 6,
            transcendentals=pairs * 2 * 15 * TILE * TILE,
        ),
        name="attend_back",
    )(place, qkv, qkv, qkv, grad_out, stats, codes_q, codes_k)


class Seq:
    def __init__(self):
        self.size = lax.axis_size("seq")
        self.lines = self.size // 2
        place = lax.axis_index("seq")
        self.line = place // 2
        self.twin = place % 2

    def send(self, value, shift, valid):
        pairs = [
            (i, i + 2 * shift)
            for i in range(self.size)
            if valid(i // 2) and 0 <= i // 2 + shift < self.lines
        ]
        return lax.ppermute(value, "seq", pairs)

    def swap(self, value, valid=lambda line: True):
        return lax.ppermute(value, "seq", [(i, i ^ 1) for i in range(self.size) if valid(i // 2)])

    def gather(self, own):
        lines = self.lines
        below, above = {0: own}, {0: own}
        twin_below, twin_above = {}, {}
        twin_own = self.swap(own)
        for k in range(1, lines):
            below[k] = self.send(below[k - 1], 1, lambda line, k=k: line >= k - 1)
            above[k] = self.send(above[k - 1], -1, lambda line, k=k: line + k - 1 < lines)
            twin_below[k] = self.swap(below[k], lambda line, k=k: line >= k)
            twin_above[k] = self.swap(above[k], lambda line, k=k: line + k < lines)
        blocks = [own, twin_own]
        for m in range(1, lines):
            up = self.line + m < lines
            blocks.append(jnp.where(up, above[m], below[lines - m]))
            blocks.append(jnp.where(up, twin_above[m], twin_below[lines - m]))
        return blocks

    def reduce(self, blocks):
        lines = self.lines
        held = {}
        order = sorted(range(lines), key=lambda m: -min(m, lines - m) if m else 1)
        for m in order:
            other = self.swap(blocks[2 * m + 1])
            held[m] = blocks[2 * m].astype(F32) + other.astype(F32)
        up = down = None
        for k in range(lines - 1, 0, -1):
            going_up = held[k] if up is None else held[k] + up.astype(F32)
            up = self.send(going_up.astype(BF), 1, lambda line, k=k: line + k < lines)
            going_down = held[lines - k] if down is None else held[lines - k] + down.astype(F32)
            down = self.send(going_down.astype(BF), -1, lambda line, k=k: line - k >= 0)
        return held[0] + up.astype(F32) + down.astype(F32)

    def to_relative(self, value, axis):
        size = value.shape[axis]
        block = size // self.size
        twice = jnp.concatenate([value, value], axis=axis)
        rolled = lax.dynamic_slice_in_dim(twice, self.line * 2 * block, size, axis)
        return self.flip(rolled, axis)

    def flip(self, value, axis):
        shape = value.shape
        block = shape[axis] // self.size
        split = shape[:axis] + (self.lines, 2, block) + shape[axis + 1 :]
        swapped = lax.rev(value.reshape(split), (axis + 1,)).reshape(shape)
        return jnp.where(self.twin == 1, swapped, value)

    def to_absolute(self, value, axis):
        size = value.shape[axis]
        block = size // self.size
        flipped = self.flip(value, axis)
        twice = jnp.concatenate([flipped, flipped], axis=axis)
        start = lax.rem(self.lines - self.line, self.lines) * 2 * block
        return lax.dynamic_slice_in_dim(twice, start, size, axis)


def over_pre(value, mask):
    return lax.ppermute(value, "pre", [(i, i ^ mask) for i in range(lax.axis_size("pre"))])


def gather_pre(own):
    far = over_pre(own, 2)
    near = over_pre(own, 1)
    return [own, near, far, over_pre(far, 1)]


def scatter_pre(blocks):
    a = blocks[0] + over_pre(blocks[1].astype(BF), 1).astype(F32)
    b = blocks[2] + over_pre(blocks[3].astype(BF), 1).astype(F32)
    return a + over_pre(b.astype(BF), 2).astype(F32)


def sum_all(value):
    for mask in (1, 2):
        value = value + over_pre(value, mask)
    size = lax.axis_size("seq")
    mask = 1
    while mask < size:
        value = value + lax.ppermute(value, "seq", [(i, i ^ mask) for i in range(size)])
        mask *= 2
    return value


def absolute_pre(blocks, place):
    first = place % 2 == 0
    low = place < 2
    a = [jnp.where(first, blocks[0], blocks[1]), jnp.where(first, blocks[1], blocks[0])]
    b = [jnp.where(first, blocks[2], blocks[3]), jnp.where(first, blocks[3], blocks[2])]
    return [jnp.where(low, u, w) for u, w in zip(a, b)] + [jnp.where(low, w, u) for u, w in zip(a, b)]


def on_device(
    prefix_in,
    later_in,
    doc_lengths,
    doc_exit,
    token_skip,
    first_gain,
    first_bias,
    qkv_weight,
    query_bias,
    value_bias,
    out_weight,
    out_bias,
    second_gain,
    second_bias,
    up_weight,
    up_bias,
    down_weight,
    down_bias,
    prefix_cot,
    later_cot,
):
    scale = 1.0 / math.sqrt(HEAD_DIM)
    pre_part = prefix_in.shape[1]
    later_part = later_in.shape[1]
    part = pre_part + later_part
    parts = lax.axis_size("pre")
    place = lax.axis_index("pre")
    seq = Seq()
    seq_count = seq.size
    seq_place = lax.axis_index("seq")
    own_d = D // seq_count
    cols = D // parts
    ff_cols = FF // parts
    length = parts * part

    packed = jnp.concatenate(
        [
            first_gain,
            first_bias,
            query_bias,
            value_bias,
            out_bias,
            second_gain,
            second_bias,
            down_bias,
            up_bias,
        ]
    ).reshape(-1, 128)
    small = jnp.stack(seq.gather(packed)).reshape(seq_count, -1)
    small = seq.to_absolute(small, 0).astype(F32)
    vectors = [small[:, i * own_d : (i + 1) * own_d].reshape(D) for i in range(8)]
    full_up_bias = small[:, 8 * own_d :].reshape(FF)
    (gain1, bias1, qb, vb, ob, gain2, bias2, db) = vectors

    def section(weight, start, width):
        return lax.dynamic_slice_in_dim(weight, start + place * width, width, 1)

    own_qkv = jnp.concatenate([section(qkv_weight, i * D, cols) for i in range(3)], axis=1)
    block_rows = own_d // parts
    out_block = lax.dynamic_slice_in_dim(out_weight, place * block_rows, block_rows, 0)
    out_block = out_weight.reshape(parts, block_rows, D)
    out_block = lax.dynamic_index_in_dim(out_block, place, 0, keepdims=False)
    shuffle = [
        ((b % parts) * seq_count + b // parts, (b // seq_count) * seq_count + b % seq_count)
        for b in range(parts * seq_count)
    ]
    own_out = lax.ppermute(out_block, ("pre", "seq"), shuffle)
    w_qkv = jnp.concatenate(seq.gather(own_qkv), axis=0)
    w_out = seq.to_absolute(jnp.concatenate(seq.gather(own_out), axis=0), 0)
    w_up = jnp.concatenate(seq.gather(section(up_weight, 0, ff_cols)), axis=0)
    w_down = jnp.concatenate(seq.gather(section(down_weight, 0, ff_cols)), axis=0)

    doc_id, live = token_tables(doc_lengths, doc_exit, token_skip)
    live_here = lax.dynamic_slice_in_dim(live[0], place * later_part, later_part, 0)
    active = jnp.concatenate([jnp.ones((pre_part,), F32), live_here.astype(F32)])[:, None]
    codes_q = jnp.concatenate([jnp.full((PRE,), -1, jnp.int32), doc_id[0]])[:, None]
    codes_k = jnp.concatenate(
        [jnp.full((PRE,), -1, jnp.int32), jnp.where(live[0], doc_id[0], -2)]
    )[None, :]
    place_vec = place.reshape(1).astype(jnp.int32)

    tokens = jnp.concatenate([prefix_in[0], later_in[0]], axis=0).astype(F32)
    cotangent = jnp.concatenate([prefix_cot[0], later_cot[0]], axis=0).astype(F32)
    ffn_grad = (active * cotangent).astype(BF)

    first_out, first_normed, first_scaling = layer_norm_parts(tokens, gain1, bias1)
    h1 = jnp.concatenate(gather_pre(seq.to_relative(first_out.astype(BF), 1)), axis=0)
    df = jnp.concatenate(gather_pre(seq.to_relative(ffn_grad, 1)), axis=0)
    projected = jnp.dot(h1, w_qkv, preferred_element_type=F32)
    own_qb = lax.dynamic_slice_in_dim(qb, place * cols, cols, 0)
    own_vb = lax.dynamic_slice_in_dim(vb, place * cols, cols, 0)
    shift = jnp.concatenate([own_qb, jnp.zeros((cols,), F32), own_vb])
    factor = jnp.concatenate([jnp.full((cols,), scale, F32), jnp.ones((2 * cols,), F32)])
    qkv = ((projected + shift) * factor).astype(BF).reshape(parts, part, 3 * cols)
    mixed, stats = attend(place_vec, qkv, codes_q, codes_k, pre_part, later_part)
    mixed = mixed.reshape(length, cols)
    attn_terms = jnp.dot(mixed, w_out, preferred_element_type=F32)
    attn = scatter_pre([attn_terms[i * part : (i + 1) * part] for i in range(parts)]) + ob

    middle = tokens + attn
    second_out, second_normed, second_scaling = layer_norm_parts(middle, gain2, bias2)
    h2 = jnp.concatenate(gather_pre(seq.to_relative(second_out.astype(BF), 1)), axis=0)
    own_ub = lax.dynamic_slice_in_dim(full_up_bias, place * ff_cols, ff_cols, 0)
    upper = jnp.dot(h2, w_up, preferred_element_type=F32) + own_ub
    acted = jax.nn.gelu(upper, approximate=False).astype(BF)
    down_grad = lax.dot_general(df, acted, (((0,), (0,)), ((), ())), preferred_element_type=F32)
    down_grad = down_grad.astype(BF)
    ffn_terms = lax.dot_general(
        acted, w_down, (((1,), (1,)), ((), ())), preferred_element_type=F32
    )
    ffn = scatter_pre([ffn_terms[i * part : (i + 1) * part] for i in range(parts)])
    ffn = seq.to_absolute(ffn, 1) + db
    result = tokens + active * (attn + ffn)
    square_sums = jnp.stack(
        [
            jnp.sum(active * result * result),
            jnp.sum(active * attn * attn),
            jnp.sum(active * ffn * ffn),
            jnp.sum(active),
        ]
    )

    acted_grad = jnp.dot(df, w_down, preferred_element_type=F32)
    upper_grad = (acted_grad * gelu_slope(upper)).astype(BF)
    second_terms = lax.dot_general(
        upper_grad, w_up, (((1,), (1,)), ((), ())), preferred_element_type=F32
    )
    up_grad = lax.dot_general(h2, upper_grad, (((0,), (0,)), ((), ())), preferred_element_type=F32)
    up_grad = up_grad.astype(BF)
    second_grad = scatter_pre([second_terms[i * part : (i + 1) * part] for i in range(parts)])
    second_grad = seq.to_absolute(second_grad, 1)
    middle_grad = norm_back(second_grad, second_normed, second_scaling, gain2)
    attn_grad = (active * cotangent + middle_grad).astype(BF)

    dattn = jnp.concatenate(gather_pre(attn_grad), axis=0)
    mixed_grad = lax.dot_general(
        dattn, w_out, (((1,), (1,)), ((), ())), preferred_element_type=F32
    ).astype(BF)
    out_grad = lax.dot_general(mixed, dattn, (((0,), (0,)), ((), ())), preferred_element_type=F32)
    out_grad = seq.to_relative(out_grad.astype(BF), 0)
    project_grad = attend_back(
        place_vec,
        qkv,
        mixed_grad.reshape(parts, part, cols),
        stats,
        codes_q,
        codes_k,
        pre_part,
        later_part,
    ).reshape(length, 3 * cols)
    qkv_grad = lax.dot_general(
        h1, project_grad, (((0,), (0,)), ((), ())), preferred_element_type=F32
    ).astype(BF)
    first_terms = lax.dot_general(
        project_grad, w_qkv, (((1,), (1,)), ((), ())), preferred_element_type=F32
    )
    first_grad = scatter_pre([first_terms[i * part : (i + 1) * part] for i in range(parts)])
    first_grad = seq.to_absolute(first_grad, 1)
    input_grad = cotangent + middle_grad + norm_back(first_grad, first_normed, first_scaling, gain1)

    def spread(grad):
        rows = grad.shape[0] // seq_count
        return seq.reduce([grad[i * rows : (i + 1) * rows] for i in range(seq_count)]).astype(BF)

    def shared(block):
        return absolute_pre(gather_pre(block), place)

    down_full = jnp.concatenate(shared(spread(down_grad)), axis=1).astype(F32)
    up_full = jnp.concatenate(shared(spread(up_grad)), axis=1).astype(F32)
    out_own = lax.ppermute(spread(out_grad), ("pre", "seq"), [(b, a) for a, b in shuffle])
    out_full = jnp.concatenate(shared(out_own), axis=0).astype(F32)
    qkv_blocks = shared(spread(qkv_grad))
    qkv_full = jnp.concatenate(
        [block[:, i * cols : (i + 1) * cols] for i in range(3) for block in qkv_blocks], axis=1
    ).astype(F32)

    def placed(vector, width):
        zeros = jnp.zeros((width * parts,), F32)
        return lax.dynamic_update_slice_in_dim(zeros, vector, place * width, 0)

    column_sums = jnp.sum(project_grad.astype(F32), axis=0)
    sums = [
        jnp.sum(first_grad * first_normed, axis=0),
        jnp.sum(first_grad, axis=0),
        placed(column_sums[:cols], cols),
        placed(column_sums[2 * cols :], cols),
        jnp.sum(attn_grad.astype(F32), axis=0),
        jnp.sum(second_grad * second_normed, axis=0),
        jnp.sum(second_grad, axis=0),
        jnp.sum(ffn_grad.astype(F32), axis=0),
        placed(jnp.sum(upper_grad.astype(F32), axis=0), ff_cols),
        jnp.concatenate([square_sums, jnp.zeros((124,), F32)]),
    ]
    flat = sum_all(jnp.concatenate(sums).reshape(-1, 128)).reshape(-1)
    totals = [flat[i * D : (i + 1) * D] for i in range(8)]
    total_ub = flat[8 * D : 8 * D + FF]
    total_squares = flat[8 * D + FF : 8 * D + FF + 4]

    def own_share(vector):
        width = vector.shape[0] // seq_count
        return lax.dynamic_slice_in_dim(vector, seq_place * width, width, 0)

    residual_rms = jnp.sqrt(total_squares[:3] / (total_squares[3] * D))
    return (
        result[:pre_part][None].astype(BF),
        result[pre_part:][None].astype(BF),
        input_grad[:pre_part][None].astype(BF),
        input_grad[pre_part:][None].astype(BF),
        own_share(totals[0]),
        own_share(totals[1]),
        qkv_full,
        own_share(totals[2]),
        own_share(totals[3]),
        out_full,
        own_share(totals[4]),
        own_share(totals[5]),
        own_share(totals[6]),
        up_full,
        own_share(total_ub),
        down_full,
        own_share(totals[7]),
        residual_rms,
    )


def solution(mesh):
    placed = (
        P("seq", "pre", None),
        P("seq", "pre", None),
        P("seq", None),
        P("seq", None),
        P("seq", None),
        P("seq"),
        P("seq"),
        P("seq", None),
        P("seq"),
        P("seq"),
        P("seq", None),
        P("seq"),
        P("seq"),
        P("seq"),
        P("seq", None),
        P("seq"),
        P("seq", None),
        P("seq"),
        P("seq", "pre", None),
        P("seq", "pre", None),
    )
    return jax.shard_map(
        on_device,
        mesh=mesh,
        in_specs=placed,
        out_specs=(
            P("seq", "pre", None),
            P("seq", "pre", None),
            P("seq", "pre", None),
            P("seq", "pre", None),
            P("seq"),
            P("seq"),
            P("seq", None),
            P("seq"),
            P("seq"),
            P("seq", None),
            P("seq"),
            P("seq"),
            P("seq"),
            P("seq", None),
            P("seq"),
            P("seq", None),
            P("seq"),
            P(),
        ),
        check_vma=False,
    )
```

time: 4280 us -> 1350 us (0.32)
  waiting for transfers between devices: 3380 us -> 241 us
  starting transfers between devices: 0.44 us -> 428 us
  blocking collectives: 179 us -> 0 us
  matrix products: 362 us -> 186 us
  local copies, waits for them, and re-layouts: 116 us -> 243 us
  Pallas kernels: 0 us -> 74.3 us
  other arithmetic: 223 us -> 160 us
    all_gather x7 -> x0, waiting for transfers between devices: 1730 us -> none  [the longest x1 627 us: on_device(): lax.all_gather(up_weight, 'seq', axis=0, tiled=True)]
    reduce_scatter x1 -> x0, waiting for transfers between devices: 1530 us -> none  [on_device(): lax.psum_scatter(terms_from(reordered, rights), ('pre', 'seq'), scatter_d...]
    ppermute x0 -> x148, starting transfers between devices: none -> 428 us  [the longest x54 158 us: send(): return lax.ppermute(value, 'seq', pairs)]
    ppermute x0 -> x148, waiting for transfers between devices: none -> 241 us  [the longest x51 95.9 us: swap(): lax.ppermute(value, 'seq', [(i, i ^ 1) for i in range(self.size) if valid...]
    all_gather x9 -> x0, blocking collectives: 179 us -> none  [the longest x1 43.1 us: on_device(): lax.all_gather(value_bias, 'seq', axis=0, tiled=True)]
    dot_general x29 -> x12, matrix products: 354 us -> 186 us  [the longest x1 44 us: on_device(): upper = jnp.dot(h2, w_up, preferred_element_type=F32) + own_ub]
    concatenate x5 -> x10, other arithmetic: 140 us -> 14.1 us  [the longest x4 8.89 us: to_relative(): twice = jnp.concatenate([value, value], axis=axis)]
    psum x1 -> x0, waiting for transfers between devices: 118 us -> none  [on_device(): lax.psum((square_sums, jnp.sum(first_grad * first_normed, axis=0), jnp.su...]
  transfers between devices with their start and end apart: 11 -> 148, of which waited for: 7 -> 36; matrix products, arithmetic and copies ran while one was open for 9% -> 39% of each run, Pallas kernels for 0% -> 6%
where the time goes in v1:
time: 1350 us; the launch traced here: 1340 us
  starting transfers between devices  428 us (32%)
  local copies, waits for them, and re-layouts  243 us (18%)
  waiting for transfers between devices  241 us (18%)
  matrix products  186 us (14%)
  other arithmetic  160 us (12%)
  Pallas kernels  74.3 us (6%)
    ppermute x54, starting transfers between devices, send(): return lax.ppermute(value, 'seq', pairs)  158 us
    ppermute x38, starting transfers between devices, over_pre(): lax.ppermute(value, 'pre', [(i, i ^ mask) for i in range(lax.axis_size('p...  145 us
    ppermute x51, starting transfers between devices, swap(): lax.ppermute(value, 'seq', [(i, i ^ 1) for i in range(self.size) if valid...  100 us
    ppermute x51, waiting for transfers between devices, swap(): lax.ppermute(value, 'seq', [(i, i ^ 1) for i in range(self.size) if valid...  95.9 us
    rev x9, local copies, waits for them, and re-layouts, flip(): swapped = lax.rev(value.reshape(split), (axis + 1,)).reshape(shape)  94.6 us
    ppermute x54, waiting for transfers between devices, send(): return lax.ppermute(value, 'seq', pairs)  83.4 us
    unnamed x231, local copies, waits for them, and re-layouts  62 us
    reshape x13, local copies, waits for them, and re-layouts, flip(): swapped = lax.rev(value.reshape(split), (axis + 1,)).reshape(shape)  51.7 us
  transfers between devices with their start and end apart: 148, of which 36 were waited for; matrix products, arithmetic and copies ran while one was open for 39% of the time, Pallas kernels for 6%

profile of v1, /device:TPU:5, one launch (start us, length us, event | category | flops | bytes accessed | tf_op | source)
XLA Modules:
  0.0 1335.9 jit_solution(8124380602296496250)
XLA Ops:
  226.5 16.1 %collective-permute-start.51 = (bf16[256,2048]{1,0:T(8,128)(2,1)S(1)}, bf16[256,2048]{1,0:T(8,128)(2,1)S(1)}, u32[]{:S(2)}, u32[]{:S(2)}) collective-permute-start(bf16[256,2048]{1,0:T(8,128)(2,1)S(1)} %copy-done.47), channel_id=1, source_target_pairs={{0,2},{1,3},{2,4},{3,5},{4,6},{5,7},{8,10},{9,11},{10,12},{11,13},... | collective-permute-start | bytes 3145736 | tf_op jit(solution)/shard_map/ppermute | solution.py:311
  246.8 17.8 %collective-permute-done.51 = bf16[256,2048]{1,0:T(8,128)(2,1)S(1)} collective-permute-done((bf16[256,2048]{1,0:T(8,128)(2,1)S(1)}, bf16[256,2048]{1,0:T(8,128)(2,1)S(1)}, u32[]{:S(2)}, u32[]{:S(2)}) %collective-permute-start.51) | collective-permute-done | bytes 1048608 | tf_op jit(solution)/shard_map/ppermute | solution.py:311
  268.8 15.3 %fusion.17 = bf16[1280,1536]{1,0:T(8,128)(2,1)} fusion(bf16[2048,1536]{1,0:T(8,128)(2,1)} %select_dynamic-update-slice_fusion.12, f32[1536]{0:T(1024)S(1)} %copy-done.83, f32[1536]{0:T(1024)S(1)} %pad_maximum_fusion.15, bf16[320,2048]{1,0:T(8,128)(2,1)S(1)} %collective-permute-done.15, bf16[320,2048]{1,0:T(8,128)(2,1)} %collective-permute-done.14, ...), kind=kOutput, calls=%fused_computation.33 | convolution fusion | flops 8079933440 | bytes 15478784 | tf_op jit(solution)/shard_map/dot_general | solution.py:495
  284.2 27.2 %attend.1 = (bf16[4,320,512]{2,1,0:T(8,128)(2,1)S(1)}, f32[4,1280,128]{2,1,0:T(8,128)S(1)}) custom-call(s32[1]{0:T(128)} %bitcast.4.place_ref, bf16[4,320,1536]{2,1,0:T(8,128)(2,1)} %bitcast.217, bf16[4,320,1536]{2,1,0:T(8,128)(2,1)} %bitcast.218, bf16[4,320,1536]{2,1,0:T(8,128)(2,1)} %bitcast.219, s32[1280,1]{1,0:T(8,128)S(1)} %broadcast_in_dim.39.cq_ref, ...), custom_call_target="tpu_custom_call" | custom-call | flops 16106127360 | bytes 5898240 | tf_op jit(solution)/shard_map/attend/pallas_call | solution.py:162
  326.8 20.9 %collective-permute-done.50 = bf16[256,2048]{1,0:T(8,128)(2,1)} collective-permute-done((bf16[256,2048]{1,0:T(8,128)(2,1)S(1)}, bf16[256,2048]{1,0:T(8,128)(2,1)}, u32[]{:S(2)}, u32[]{:S(2)}) %collective-permute-start.50) | collective-permute-done | bytes 1048608 | tf_op jit(solution)/shard_map/ppermute | solution.py:311
  442.4 14.6 %collective-permute-done.57 = bf16[256,2048]{1,0:T(8,128)(2,1)S(1)} collective-permute-done((bf16[256,2048]{1,0:T(8,128)(2,1)}, bf16[256,2048]{1,0:T(8,128)(2,1)S(1)}, u32[]{:S(2)}, u32[]{:S(2)}) %collective-permute-start.57) | collective-permute-done | bytes 1048608 | tf_op jit(solution)/shard_map/ppermute | solution.py:314
  481.3 53.6 %collective-permute-start.80 = (bf16[320,2048]{1,0:T(8,128)(2,1)}, bf16[320,2048]{1,0:T(8,128)(2,1)S(1)}, u32[]{:S(2)}, u32[]{:S(2)}) collective-permute-start(bf16[320,2048]{1,0:T(8,128)(2,1)} %collective-permute-done.79), channel_id=1, source_target_pairs={{0,8},{8,0},{16,24},{24,16},{1,9},{9,1},{17,25},{25,17},{2,10},{10... | collective-permute-start | bytes 3932168 | tf_op jit(solution)/shard_map/ppermute | solution.py:372
  537.1 44.0 %fusion.2 = (bf16[1280,2048]{1,0:T(8,128)(2,1)}, f32[1280,2048]{1,0:T(8,128)}) fusion(f32[2048]{0:T(1024)S(1)} %dynamic_slice.97, bf16[2048,2048]{1,0:T(8,128)(2,1)} %get-tuple-element.189, bf16[320,2048]{1,0:T(8,128)(2,1)S(1)} %collective-permute-done.48, bf16[320,2048]{1,0:T(8,128)(2,1)S(1)} %collective-permute-done.47, ...), kind=kOutput, calls=%fused_computation.4 | convolution fusion | flops 10931404800 | bytes 29368320 | tf_op jit(solution)/shard_map/dot_general | solution.py:510
  581.2 24.6 %convert_reduce_fusion = (f32[2048]{0:T(1024)S(1)}, bf16[1280,2048]{1,0:T(8,128)(2,1)}) fusion(f32[1280,2048]{1,0:T(8,128)} %get-tuple-element.183, f32[2048]{0:T(1024)S(1)} %dynamic_slice.97, bf16[2048,2048]{1,0:T(8,128)(2,1)} %get-tuple-element.188, bf16[320,2048]{1,0:T(8,128)(2,1)S(1)} %collective-permute-done.80, ...), kind=kOutput, calls=%fused_computation.11 | convolution fusion | flops 10792466432 | bytes 29376512 | tf_op jit(solution)/shard_map/dot_general | solution.py:529
  605.8 14.9 %fusion.106 = (bf16[1280,2048]{1,0:T(8,128)(2,1)S(1)}, f32[1280,2048]{1,0:T(8,128)}) fusion(bf16[1280,2048]{1,0:T(8,128)(2,1)} %get-tuple-element.187, bf16[2048,2048]{1,0:T(8,128)(2,1)S(1)} %copy-done.56), kind=kOutput, calls=%fused_computation.364 | convolution fusion | flops 10740039680 | bytes 29360128 | tf_op jit(solution)/shard_map/dot_general | solution.py:531
  623.7 17.1 %fusion.108 = (bf16[1280,2048]{1,0:T(8,128)(2,1)}, f32[1280,2048]{1,0:T(8,128)}) fusion(bf16[1280,2048]{1,0:T(8,128)(2,1)S(1)} %copy-done.84, bf16[2048,2048]{1,0:T(8,128)(2,1)} %get-tuple-element.188), kind=kOutput, calls=%fused_computation.366 | convolution fusion | flops 10740039680 | bytes 29360128 | tf_op jit(solution)/shard_map/dot_general | solution.py:514
  640.8 14.6 %convolution_convert_fusion.1 = bf16[2048,2048]{0,1:T(8,128)(2,1)S(1)} fusion(bf16[1280,2048]{1,0:T(8,128)(2,1)} %get-tuple-element.187, bf16[320,2048]{1,0:T(8,128)(2,1)} %copy-done.78, bf16[320,2048]{1,0:T(8,128)(2,1)} %copy-done.76, bf16[320,2048]{1,0:T(8,128)(2,1)} %copy-done.77, bf16[320,2048]{1,0:T(8,128)(2,1)} %copy-done.45), kind=kOutput, calls=%fused_computation.31 | convolution fusion | flops 10762584064 | bytes 18874368 | tf_op jit(solution)/shard_map/dot_general | solution.py:534
  660.2 15.0 %convolution_convert_fusion = bf16[2048,2048]{0,1:T(8,128)(2,1)S(1)} fusion(bf16[1280,2048]{1,0:T(8,128)(2,1)} %get-tuple-element.182, bf16[320,2048]{1,0:T(8,128)(2,1)} %copy-done.80, bf16[320,2048]{1,0:T(8,128)(2,1)} %collective-permute-done.79, bf16[320,2048]{1,0:T(8,128)(2,1)} %copy-done.79, bf16[320,2048]{1,0:T(8,128)(2,1)} %broadcast_select_fusion.2), kind=kOutput, calls=%fused_computation.30 | convolution fusion | flops 10762584064 | bytes 18874368 | tf_op jit(solution)/shard_map/dot_general | solution.py:512
  687.2 19.9 %collective-permute-done.138 = bf16[256,2048]{0,1:T(8,128)(2,1)S(1)} collective-permute-done((bf16[256,2048]{0,1:T(8,128)(2,1)S(1)}, bf16[256,2048]{0,1:T(8,128)(2,1)S(1)}, u32[]{:S(2)}, u32[]{:S(2)}) %collective-permute-start.138) | collective-permute-done | bytes 1048608 | tf_op jit(solution)/shard_map/ppermute | solution.py:314
  712.9 16.8 %collective-permute-done.124 = bf16[256,2048]{0,1:T(8,128)(2,1)S(1)} collective-permute-done((bf16[256,2048]{0,1:T(8,128)(2,1)S(1)}, bf16[256,2048]{0,1:T(8,128)(2,1)S(1)}, u32[]{:S(2)}, u32[]{:S(2)}) %collective-permute-start.124) | collective-permute-done | bytes 1048608 | tf_op jit(solution)/shard_map/ppermute | solution.py:314
  770.4 15.6 %rev.33 = f32[320,4,2,256]{3,2,1,0:T(2,128)} reverse(f32[320,4,2,256]{3,2,1,0:T(2,128)} %reshape.388), dimensions={2} | reverse | bytes 5242880 | tf_op jit(solution)/shard_map/rev | solution.py:359
  834.4 15.7 %rev.31 = f32[320,4,2,256]{3,2,1,0:T(2,128)} reverse(f32[320,4,2,256]{3,2,1,0:T(2,128)} %reshape.384), dimensions={2} | reverse | bytes 5242880 | tf_op jit(solution)/shard_map/rev | solution.py:359
  869.4 23.0 %collective-permute-start.135 = (bf16[256,2048]{0,1:T(8,128)(2,1)}, bf16[256,2048]{0,1:T(8,128)(2,1)}, u32[]{:S(2)}, u32[]{:S(2)}) collective-permute-start(bf16[256,2048]{0,1:T(8,128)(2,1)} %get-tuple-element.107), channel_id=1, source_target_pairs={{0,1},{1,0},{2,3},{3,2},{4,5},{5,4},{6,7},{7,6},{8,9},{9,8},{10,11... | collective-permute-start | bytes 3145736 | tf_op jit(solution)/shard_map/ppermute | solution.py:314
  895.2 19.3 %collective-permute-start.128 = (bf16[256,2048]{0,1:T(8,128)(2,1)}, bf16[256,2048]{0,1:T(8,128)(2,1)}, u32[]{:S(2)}, u32[]{:S(2)}) collective-permute-start(bf16[256,2048]{0,1:T(8,128)(2,1)} %get-tuple-element.105), channel_id=1, source_target_pairs={{0,2},{1,3},{2,4},{3,5},{4,6},{5,7},{8,10},{9,11},{10,12},{11,13},... | collective-permute-start | bytes 3145736 | tf_op jit(solution)/shard_map/ppermute | solution.py:311
  923.7 47.1 %attend_back.1 = bf16[4,320,1536]{2,1,0:T(8,128)(2,1)} custom-call(s32[1]{0:T(128)} %bitcast.4.place_ref, bf16[4,320,1536]{2,1,0:T(8,128)(2,1)} %bitcast.220, bf16[4,320,1536]{2,1,0:T(8,128)(2,1)} %bitcast.221, bf16[4,320,1536]{2,1,0:T(8,128)(2,1)} %bitcast.222, bf16[4,320,512]{2,1,0:T(8,128)(2,1)} %bitcast.223, f32[4,1280,128]{2,1,0:T(8,128)} %copy-done.6, ...), custom_call_target="tpu_custom_call" | custom-call | flops 20132659200 | bytes 11796480 | tf_op jit(solution)/shard_map/attend_back/pallas_call | solution.py:269
  970.8 15.3 %fusion.107 = (bf16[1280,2048]{1,0:T(8,128)(2,1)}, f32[1280,2048]{1,0:T(8,128)}) fusion(bf16[1280,1536]{1,0:T(8,128)(2,1)} %bitcast.182, bf16[2048,1536]{1,0:T(8,128)(2,1)} %select_dynamic-update-slice_fusion.12), kind=kOutput, calls=%fused_computation.365 | convolution fusion | flops 8055685120 | bytes 25952256 | tf_op jit(solution)/shard_map/dot_general | solution.py:560
  1045.6 24.8 %collective-permute-start.141 = (bf16[256,2048]{0,1:T(8,128)(2,1)S(1)}, bf16[256,2048]{0,1:T(8,128)(2,1)S(1)}, u32[]{:S(2)}, u32[]{:S(2)}) collective-permute-start(bf16[256,2048]{0,1:T(8,128)(2,1)S(1)} %copy-done.46), channel_id=1, source_target_pairs={{0,2},{1,3},{2,4},{3,5},{4,6},{5,7},{8,10},{9,11},{10,12},{11,13},... | collective-permute-start | bytes 3145736 | tf_op jit(solution)/shard_map/ppermute | solution.py:311
  1142.9 18.7 %collective-permute-done.89 = bf16[320,2048]{1,0:T(8,128)(2,1)S(1)} collective-permute-done((bf16[320,2048]{1,0:T(8,128)(2,1)S(1)}, bf16[320,2048]{1,0:T(8,128)(2,1)S(1)}, u32[]{:S(2)}, u32[]{:S(2)}) %collective-permute-start.89) | collective-permute-done | bytes 1310752 | tf_op jit(solution)/shard_map/ppermute | solution.py:372
  1168.5 15.7 %rev.34 = f32[320,4,2,256]{3,2,1,0:T(2,128)} reverse(f32[320,4,2,256]{3,2,1,0:T(2,128)} %reshape.392), dimensions={2} | reverse | bytes 5242880 | tf_op jit(solution)/shard_map/rev | solution.py:359
  (714 shorter events, 804.1 us)
Async XLA Ops:
  8.2 57.8 %collective-permute-start.1 = (bf16[24,128]{1,0:T(8,128)(2,1)S(1)}, bf16[24,128]{1,0:T(8,128)(2,1)S(1)}, u32[]{:S(2)}, u32[]{:S(2)}) collective-permute-start(bf16[24,128]{1,0:T(8,128)(2,1)S(1)} %bitcast.212), channel_id=1, source_target_pairs={{2,0},{3,1},{4,2},{5,3},{6,4},{7,5},{10,8},{11,9},{12,10},{13,11},... | collective-permute-start | bytes 18440 | tf_op jit(solution)/shard_map/ppermute | solution.py:311
  16.1 127.1 %collective-permute-start.16 = (bf16[256,1536]{1,0:T(8,128)(2,1)}, bf16[256,1536]{1,0:T(8,128)(2,1)}, u32[]{:S(2)}, u32[]{:S(2)}) collective-permute-start(bf16[256,1536]{1,0:T(8,128)(2,1)} %get-tuple-element.158), channel_id=1, source_target_pairs={{0,1},{1,0},{2,3},{3,2},{4,5},{5,4},{6,7},{7,6},{8,9},{9,8},{10,11... | collective-permute-start | bytes 2359304 | tf_op jit(solution)/shard_map/ppermute | solution.py:314
  17.4 139.4 %collective-permute-start.17 = (bf16[256,1536]{1,0:T(8,128)(2,1)}, bf16[256,1536]{1,0:T(8,128)(2,1)}, u32[]{:S(2)}, u32[]{:S(2)}) collective-permute-start(bf16[256,1536]{1,0:T(8,128)(2,1)} %get-tuple-element.158), channel_id=1, source_target_pairs={{2,0},{3,1},{4,2},{5,3},{6,4},{7,5},{10,8},{11,9},{12,10},{13,11},... | collective-permute-start | bytes 2359304 | tf_op jit(solution)/shard_map/ppermute | solution.py:311
  58.4 65.6 %collective-permute-start.29 = (bf16[64,2048]{1,0:T(8,128)(2,1)S(1)}, bf16[64,2048]{1,0:T(8,128)(2,1)S(1)}, u32[]{:S(2)}, u32[]{:S(2)}) collective-permute-start(bf16[64,2048]{1,0:T(8,128)(2,1)S(1)} %dynamic-slice_bitcast_fusion), channel_id=1, source_target_pairs={{0,0},{8,1},{16,2},{24,3},{1,4},{9,5},{17,6},{25,7},{2,8},{10,9},{... | collective-permute-start | bytes 786440 | tf_op jit(solution)/shard_map/ppermute | solution.py:473
  243.8 70.9 %collective-permute-start.62 = (bf16[256,2048]{1,0:T(8,128)(2,1)}, bf16[256,2048]{1,0:T(8,128)(2,1)}, u32[]{:S(2)}, u32[]{:S(2)}) collective-permute-start(bf16[256,2048]{1,0:T(8,128)(2,1)} %get-tuple-element.95), channel_id=1, source_target_pairs={{0,1},{1,0},{2,3},{3,2},{4,5},{5,4},{6,7},{7,6},{8,9},{9,8},{10,11... | collective-permute-start | bytes 3145736 | tf_op jit(solution)/shard_map/ppermute | solution.py:314
  245.5 72.3 %collective-permute-start.63 = (bf16[256,2048]{1,0:T(8,128)(2,1)}, bf16[256,2048]{1,0:T(8,128)(2,1)}, u32[]{:S(2)}, u32[]{:S(2)}) collective-permute-start(bf16[256,2048]{1,0:T(8,128)(2,1)} %get-tuple-element.95), channel_id=1, source_target_pairs={{2,0},{3,1},{4,2},{5,3},{6,4},{7,5},{10,8},{11,9},{12,10},{13,11},... | collective-permute-start | bytes 3145736 | tf_op jit(solution)/shard_map/ppermute | solution.py:311
  372.8 58.1 %collective-permute-start.79 = (bf16[320,2048]{1,0:T(8,128)(2,1)}, bf16[320,2048]{1,0:T(8,128)(2,1)}, u32[]{:S(2)}, u32[]{:S(2)}) collective-permute-start(bf16[320,2048]{1,0:T(8,128)(2,1)} %broadcast_select_fusion.2), channel_id=1, source_target_pairs={{0,16},{8,24},{16,0},{24,8},{1,17},{9,25},{17,1},{25,9},{2,18},{10... | collective-permute-start | bytes 3932168 | tf_op jit(solution)/shard_map/ppermute | solution.py:372
  463.3 71.6 %collective-permute-start.60 = (bf16[256,2048]{1,0:T(8,128)(2,1)S(1)}, bf16[256,2048]{1,0:T(8,128)(2,1)S(1)}, u32[]{:S(2)}, u32[]{:S(2)}) collective-permute-start(bf16[256,2048]{1,0:T(8,128)(2,1)S(1)} %collective-permute-done.59), channel_id=1, source_target_pairs={{0,1},{1,0},{8,9},{9,8},{16,17},{17,16},{24,25},{25,24}} | collective-permute-start | bytes 3145736 | tf_op jit(solution)/shard_map/ppermute | solution.py:314
  466.0 71.1 %collective-permute-start.46 = (bf16[320,2048]{1,0:T(8,128)(2,1)S(1)}, bf16[320,2048]{1,0:T(8,128)(2,1)S(1)}, u32[]{:S(2)}, u32[]{:S(2)}) collective-permute-start(bf16[320,2048]{1,0:T(8,128)(2,1)S(1)} %broadcast_select_fusion.4), channel_id=1, source_target_pairs={{0,8},{8,0},{16,24},{24,16},{1,9},{9,1},{17,25},{25,17},{2,10},{10... | collective-permute-start | bytes 3932168 | tf_op jit(solution)/shard_map/ppermute | solution.py:372
  469.1 68.0 %collective-permute-start.48 = (bf16[320,2048]{1,0:T(8,128)(2,1)S(1)}, bf16[320,2048]{1,0:T(8,128)(2,1)S(1)}, u32[]{:S(2)}, u32[]{:S(2)}) collective-permute-start(bf16[320,2048]{1,0:T(8,128)(2,1)S(1)} %collective-permute-done.47), channel_id=1, source_target_pairs={{0,8},{8,0},{16,24},{24,16},{1,9},{9,1},{17,25},{25,17},{2,10},{10... | collective-permute-start | bytes 3932168 | tf_op jit(solution)/shard_map/ppermute | solution.py:372
  471.9 109.2 %collective-permute-start.78 = (bf16[320,2048]{1,0:T(8,128)(2,1)}, bf16[320,2048]{1,0:T(8,128)(2,1)S(1)}, u32[]{:S(2)}, u32[]{:S(2)}) collective-permute-start(bf16[320,2048]{1,0:T(8,128)(2,1)} %broadcast_select_fusion.2), channel_id=1, source_target_pairs={{0,8},{8,0},{16,24},{24,16},{1,9},{9,1},{17,25},{25,17},{2,10},{10... | collective-permute-start | bytes 3932168 | tf_op jit(solution)/shard_map/ppermute | solution.py:372
  481.3 99.8 %collective-permute-start.80 = (bf16[320,2048]{1,0:T(8,128)(2,1)}, bf16[320,2048]{1,0:T(8,128)(2,1)S(1)}, u32[]{:S(2)}, u32[]{:S(2)}) collective-permute-start(bf16[320,2048]{1,0:T(8,128)(2,1)} %collective-permute-done.79), channel_id=1, source_target_pairs={{0,8},{8,0},{16,24},{24,16},{1,9},{9,1},{17,25},{25,17},{2,10},{10... | collective-permute-start | bytes 3932168 | tf_op jit(solution)/shard_map/ppermute | solution.py:372
  621.9 86.0 %collective-permute-start.82 = (bf16[320,2048]{1,0:T(8,128)(2,1)}, bf16[320,2048]{1,0:T(8,128)(2,1)}, u32[]{:S(2)}, u32[]{:S(2)}) collective-permute-start(bf16[320,2048]{1,0:T(8,128)(2,1)} %get-tuple-element.124), channel_id=1, source_target_pairs={{0,8},{8,0},{16,24},{24,16},{1,9},{9,1},{17,25},{25,17},{2,10},{10... | collective-permute-start | bytes 3932168 | tf_op jit(solution)/shard_map/ppermute | solution.py:372
  622.3 135.3 %collective-permute-start.81 = (bf16[320,2048]{1,0:T(8,128)(2,1)S(1)}, bf16[320,2048]{1,0:T(8,128)(2,1)}, u32[]{:S(2)}, u32[]{:S(2)}) collective-permute-start(bf16[320,2048]{1,0:T(8,128)(2,1)S(1)} %get-tuple-element.123), channel_id=1, source_target_pairs={{0,8},{8,0},{16,24},{24,16},{1,9},{9,1},{17,25},{25,17},{2,10},{10... | collective-permute-start | bytes 3932168 | tf_op jit(solution)/shard_map/ppermute | solution.py:372
  737.3 77.6 %collective-permute-start.75 = (bf16[320,2048]{1,0:T(8,128)(2,1)}, bf16[320,2048]{1,0:T(8,128)(2,1)}, u32[]{:S(2)}, u32[]{:S(2)}) collective-permute-start(bf16[320,2048]{1,0:T(8,128)(2,1)} %get-tuple-element.125), channel_id=1, source_target_pairs={{0,8},{8,0},{16,24},{24,16},{1,9},{9,1},{17,25},{25,17},{2,10},{10... | collective-permute-start | bytes 3932168 | tf_op jit(solution)/shard_map/ppermute | solution.py:372
  804.0 266.5 %collective-permute-start.122 = (bf16[256,2048]{0,1:T(8,128)(2,1)}, bf16[256,2048]{0,1:T(8,128)(2,1)}, u32[]{:S(2)}, u32[]{:S(2)}) collective-permute-start(bf16[256,2048]{0,1:T(8,128)(2,1)} %get-tuple-element.111), channel_id=1, source_target_pairs={{0,1},{1,0},{2,3},{3,2},{4,5},{5,4},{6,7},{7,6},{8,9},{9,8},{10,11... | collective-permute-start | bytes 3145736 | tf_op jit(solution)/shard_map/ppermute | solution.py:314
  814.8 102.3 %collective-permute-start.84 = (bf16[320,2048]{1,0:T(8,128)(2,1)}, bf16[320,2048]{1,0:T(8,128)(2,1)}, u32[]{:S(2)}, u32[]{:S(2)}) collective-permute-start(bf16[320,2048]{1,0:T(8,128)(2,1)} %get-tuple-element.91), channel_id=1, source_target_pairs={{0,8},{8,0},{16,24},{24,16},{1,9},{9,1},{17,25},{25,17},{2,10},{10... | collective-permute-start | bytes 3932168 | tf_op jit(solution)/shard_map/ppermute | solution.py:372
  854.8 62.3 %collective-permute-start.86 = (bf16[320,2048]{1,0:T(8,128)(2,1)}, bf16[320,2048]{1,0:T(8,128)(2,1)S(1)}, u32[]{:S(2)}, u32[]{:S(2)}) collective-permute-start(bf16[320,2048]{1,0:T(8,128)(2,1)} %collective-permute-done.85), channel_id=1, source_target_pairs={{0,8},{8,0},{16,24},{24,16},{1,9},{9,1},{17,25},{25,17},{2,10},{10... | collective-permute-start | bytes 3932168 | tf_op jit(solution)/shard_map/ppermute | solution.py:372
  869.4 202.4 %collective-permute-start.135 = (bf16[256,2048]{0,1:T(8,128)(2,1)}, bf16[256,2048]{0,1:T(8,128)(2,1)}, u32[]{:S(2)}, u32[]{:S(2)}) collective-permute-start(bf16[256,2048]{0,1:T(8,128)(2,1)} %get-tuple-element.107), channel_id=1, source_target_pairs={{0,1},{1,0},{2,3},{3,2},{4,5},{5,4},{6,7},{7,6},{8,9},{9,8},{10,11... | collective-permute-start | bytes 3145736 | tf_op jit(solution)/shard_map/ppermute | solution.py:314
  895.2 177.0 %collective-permute-start.128 = (bf16[256,2048]{0,1:T(8,128)(2,1)}, bf16[256,2048]{0,1:T(8,128)(2,1)}, u32[]{:S(2)}, u32[]{:S(2)}) collective-permute-start(bf16[256,2048]{0,1:T(8,128)(2,1)} %get-tuple-element.105), channel_id=1, source_target_pairs={{0,2},{1,3},{2,4},{3,5},{4,6},{5,7},{8,10},{9,11},{10,12},{11,13},... | collective-permute-start | bytes 3145736 | tf_op jit(solution)/shard_map/ppermute | solution.py:311
  1131.0 140.5 %collective-permute-start.95 = (bf16[256,1536]{0,1:T(8,128)(2,1)}, bf16[256,1536]{0,1:T(8,128)(2,1)}, u32[]{:S(2)}, u32[]{:S(2)}) collective-permute-start(bf16[256,1536]{0,1:T(8,128)(2,1)} %get-tuple-element.117), channel_id=1, source_target_pairs={{0,1},{1,0},{2,3},{3,2},{4,5},{5,4},{6,7},{7,6},{8,9},{9,8},{10,11... | collective-permute-start | bytes 2359304 | tf_op jit(solution)/shard_map/ppermute | solution.py:314
  1134.6 131.3 %collective-permute-start.132 = (bf16[256,2048]{0,1:T(8,128)(2,1)}, bf16[256,2048]{0,1:T(8,128)(2,1)}, u32[]{:S(2)}, u32[]{:S(2)}) collective-permute-start(bf16[256,2048]{0,1:T(8,128)(2,1)} %add_convert_fusion.6), channel_id=1, source_target_pairs={{0,8},{8,0},{16,24},{24,16},{1,9},{9,1},{17,25},{25,17},{2,10},{10... | collective-permute-start | bytes 3145736 | tf_op jit(solution)/shard_map/ppermute | solution.py:372
  1136.7 104.7 %collective-permute-start.133 = (bf16[256,2048]{0,1:T(8,128)(2,1)}, bf16[256,2048]{0,1:T(8,128)(2,1)}, u32[]{:S(2)}, u32[]{:S(2)}) collective-permute-start(bf16[256,2048]{0,1:T(8,128)(2,1)} %add_convert_fusion.6), channel_id=1, source_target_pairs={{0,16},{8,24},{16,0},{24,8},{1,17},{9,25},{17,1},{25,9},{2,18},{10... | collective-permute-start | bytes 3145736 | tf_op jit(solution)/shard_map/ppermute | solution.py:372
  1141.2 96.9 %collective-permute-start.102 = (bf16[256,1536]{0,1:T(8,128)(2,1)}, bf16[256,1536]{0,1:T(8,128)(2,1)}, u32[]{:S(2)}, u32[]{:S(2)}) collective-permute-start(bf16[256,1536]{0,1:T(8,128)(2,1)} %get-tuple-element.116), channel_id=1, source_target_pairs={{6,4},{7,5},{14,12},{15,13},{22,20},{23,21},{30,28},{31,29}} | collective-permute-start | bytes 2359304 | tf_op jit(solution)/shard_map/ppermute | solution.py:311
  (215 other events, 5733.0 us)

commit v2 on v1

v2 whole, which is shorter than its diff:
```python
import functools
import math

import jax
import jax.numpy as jnp
from jax import lax
from jax.experimental import pallas as pl
from jax.experimental.pallas import tpu as pltpu
from jax.sharding import PartitionSpec as P

D = 2048
HEADS = 32
HEAD_DIM = 64
FF = 8192
LAYER = 12
PRE = 512

EPS = 1e-05
NEG = -1e30
BF = jnp.bfloat16
F32 = jnp.float32
TILE = 256


def layer_norm_parts(values, gain, bias):
    mean = jnp.mean(values, axis=-1, keepdims=True)
    centred = values - mean
    variance = jnp.mean(centred * centred, axis=-1, keepdims=True)
    scaling = lax.rsqrt(variance + EPS)
    normed = centred * scaling
    return (normed * gain + bias, normed, scaling)


def norm_back(grad, normed, scaling, gain):
    scaled = grad * gain
    inner = jnp.mean(scaled, axis=-1, keepdims=True)
    cross = jnp.mean(scaled * normed, axis=-1, keepdims=True)
    return scaling * (scaled - inner - normed * cross)


def token_tables(doc_lengths, doc_exit, token_skip):
    order = jnp.arange(doc_lengths.shape[-1], dtype=jnp.int32)
    earlier = order[None, :] < order[:, None]
    starts = jnp.sum(
        jnp.where(earlier, doc_lengths[..., None, :], 0), axis=-1, dtype=jnp.int32
    )
    places = jnp.arange(token_skip.shape[-1], dtype=jnp.int32)
    doc_id = (
        jnp.sum(
            (places[:, None] >= starts[..., None, :]).astype(jnp.int32), axis=-1, dtype=jnp.int32
        )
        - 1
    )
    live_doc = doc_exit > LAYER
    live = jnp.any((doc_id[..., None] == order) & live_doc[..., None, :], axis=-1) & (
        token_skip == 0
    )
    return (doc_id, live)


def dot_nt(a, b):
    return lax.dot_general(a, b, (((1,), (1,)), ((), ())), preferred_element_type=F32)


def dot_nn(a, b):
    return lax.dot_general(a, b, (((1,), (0,)), ((), ())), preferred_element_type=F32)


def dot_tn(a, b):
    return lax.dot_general(a, b, (((0,), (0,)), ((), ())), preferred_element_type=F32)


def masked_scores(block, scores, tile, codes_q, codes_k):
    rows = lax.broadcasted_iota(jnp.int32, (TILE, TILE), 0)
    cols = lax.broadcasted_iota(jnp.int32, (TILE, TILE), 1)
    allowed = None
    if tile == block:
        allowed = cols <= rows
    if tile * TILE >= PRE:
        same = (
            codes_q[block * TILE : (block + 1) * TILE, :]
            == codes_k[:, tile * TILE : (tile + 1) * TILE]
        )
        allowed = same if allowed is None else allowed & same
    if allowed is None:
        return scores
    return jnp.where(allowed, scores, NEG)


def attend_back_pair(qkv_lanes, do, level_of, codes_q, codes_k, dq_all, dk_all, dv_all, qkv):
    dk_all[...] = jnp.zeros_like(dk_all)
    dv_all[...] = jnp.zeros_like(dv_all)
    blocks = do.shape[0] // TILE
    for block in range(blocks):
        rows = slice(block * TILE, (block + 1) * TILE)
        both_q = qkv[0][rows, qkv_lanes[0]]
        both_do = do[rows, qkv_lanes[3]]
        parts = []
        for head in range(2):
            queries = head_lanes(both_q, head)
            grads = head_lanes(both_do, head)
            level = level_of(rows, head)
            probs = []
            dprobs = []
            for tile in range(block + 1):
                cols = slice(tile * TILE, (tile + 1) * TILE)
                scores = masked_scores(
                    block, dot_nt(queries, qkv[1][cols, qkv_lanes[1]]), tile, codes_q, codes_k
                )
                probs.append(jnp.exp(scores - level))
                dprobs.append(dot_nt(grads, qkv[2][cols, qkv_lanes[2]]))
            delta = functools.reduce(
                jnp.add, [jnp.sum(a * b, axis=1, keepdims=True) for a, b in zip(probs, dprobs)]
            )
            dq = None
            for tile in range(block + 1):
                cols = slice(tile * TILE, (tile + 1) * TILE)
                ds = (probs[tile] * (dprobs[tile] - delta)).astype(BF)
                part = dot_nn(ds, qkv[1][cols, qkv_lanes[1]])
                dq = part if dq is None else dq + part
                dk_all[cols, :] += dot_tn(ds, queries)
                dv_all[cols, :] += dot_tn(probs[tile].astype(BF), grads)
            parts.append(dq)
        dq_all[rows, :] = join_heads(*parts) * (1.0 / math.sqrt(HEAD_DIM))


def attend_back_kernel(q_ref, k_ref, v_ref, do_ref, stat_ref, cq_ref, ck_ref, dq_ref, dk_ref, dv_ref, dq, dk, dv):
    every = slice(None)
    attend_back_pair(
        [every] * 4,
        do_ref,
        lambda rows, head: stat_ref[rows, head * HEAD_DIM : head * HEAD_DIM + 1],
        cq_ref[...],
        ck_ref[...],
        dq,
        dk,
        dv,
        (q_ref, k_ref, v_ref),
    )
    dq_ref[...] = dq[...].astype(BF)
    dk_ref[...] = dk[...].astype(BF)
    dv_ref[...] = dv[...].astype(BF)


def attend_back(qkv, grad_out, stats, codes_q, codes_k):
    length, width = qkv.shape
    pairs = width // 3 // 128
    block = (length, 128)
    return pl.pallas_call(
        attend_back_kernel,
        out_shape=[jax.ShapeDtypeStruct((length, width // 3), BF)] * 3,
        grid=(pairs,),
        in_specs=[
            pl.BlockSpec(block, lambda i: (0, i)),
            pl.BlockSpec(block, lambda i: (0, pairs + i)),
            pl.BlockSpec(block, lambda i: (0, 2 * pairs + i)),
            pl.BlockSpec(block, lambda i: (0, i)),
            pl.BlockSpec(block, lambda i: (0, i)),
            pl.BlockSpec((length, 1), lambda i: (0, 0)),
            pl.BlockSpec((1, length), lambda i: (0, 0)),
        ],
        out_specs=[pl.BlockSpec(block, lambda i: (0, i))] * 3,
        scratch_shapes=[pltpu.VMEM((length, 128), F32)] * 3,
        compiler_params=pltpu.CompilerParams(vmem_limit_bytes=56 * 2**20),
        cost_estimate=pl.CostEstimate(
            flops=pairs * 2 * 15 * 10 * TILE * TILE * 256,
            bytes_accessed=length * width * 6,
            transcendentals=pairs * 2 * 15 * TILE * TILE,
        ),
        name="attend_back",
    )(qkv, qkv, qkv, grad_out, stats, codes_q, codes_k)


def xor(value, mask):
    bit = 1
    while bit <= mask:
        if mask & bit:
            value = value + bit * (1 - 2 * lax.rem(lax.div(value, jnp.int32(bit)), jnp.int32(2)))
        bit *= 2
    return value


def remote(src, dst, send_sem, recv_sem, **target):
    return pltpu.make_async_remote_copy(
        src_ref=src,
        dst_ref=dst,
        send_sem=send_sem,
        recv_sem=recv_sem,
        device_id=target,
        device_id_type=pl.DeviceIdType.MESH,
    )


def greet(wide):
    barrier = pltpu.get_barrier_semaphore()
    seq = lax.axis_index("seq")
    pre = lax.axis_index("pre")
    for mask in (1, *wide):
        pl.semaphore_signal(
            barrier, inc=1, device_id={"seq": xor(seq, mask)}, device_id_type=pl.DeviceIdType.MESH
        )
    for mask in (1, 2):
        pl.semaphore_signal(
            barrier, inc=1, device_id={"pre": xor(pre, mask)}, device_id_type=pl.DeviceIdType.MESH
        )
    pl.semaphore_wait(barrier, len(wide) + 3)


def rows_of(index, count):
    return pl.ds(pl.multiple_of(index * count, count), count)


class Gather:
    def __init__(self, own, land, rows, send_sem, recv_sem, local_sem):
        self.own, self.land, self.rows = own, land, rows
        self.send_sem, self.recv_sem, self.local_sem = send_sem, recv_sem, local_sem
        self.seq = lax.axis_index("seq")
        self.sent = []
        self.local = None

    def slot(self, place):
        return self.land.at[rows_of(place, self.rows), :]

    def begin(self, *masks):
        for mask in masks:
            copy = remote(
                self.own,
                self.slot(self.seq),
                self.send_sem.at[mask],
                self.recv_sem.at[mask],
                seq=xor(self.seq, mask),
            )
            copy.start()
            self.sent.append(copy)

    def keep(self):
        self.local = pltpu.make_async_copy(self.own, self.slot(self.seq), self.local_sem)
        self.local.start()

    def arrived(self, mask):
        here = self.slot(xor(self.seq, mask))
        remote(
            here, here, self.send_sem.at[mask], self.recv_sem.at[mask], seq=xor(self.seq, mask)
        ).wait_recv()

    def forward(self, mask):
        self.arrived(mask)
        here = self.slot(xor(self.seq, mask))
        copy = remote(
            here,
            here,
            self.send_sem.at[mask + 1],
            self.recv_sem.at[mask + 1],
            seq=xor(self.seq, 1),
        )
        copy.start()
        self.sent.append(copy)

    def finish(self, wide):
        self.local.wait()
        self.arrived(1)
        for mask in wide:
            self.arrived(mask + 1)

    def drain(self):
        for copy in self.sent:
            copy.wait_send()


class Spread:
    def __init__(self, own, land, rows, send_sem, recv_sem, local_sem):
        self.own, self.land, self.rows = own, land, rows
        self.send_sem, self.recv_sem, self.local_sem = send_sem, recv_sem, local_sem
        self.pre = lax.axis_index("pre")
        self.sent = []

    def slot(self, index):
        return self.land.at[index * self.rows : (index + 1) * self.rows, :]

    def copy(self, src, slot, mask):
        return remote(
            src, self.slot(slot), self.send_sem.at[slot], self.recv_sem.at[slot], pre=xor(self.pre, mask)
        )

    def begin(self):
        for mask in (2, 1):
            copy = self.copy(self.own, mask, mask)
            copy.start()
            self.sent.append(copy)
        self.local = pltpu.make_async_copy(self.own, self.slot(0), self.local_sem)
        self.local.start()

    def forward(self):
        self.copy(self.own, 2, 2).wait_recv()
        copy = self.copy(self.slot(2), 3, 1)
        copy.start()
        self.sent.append(copy)

    def finish(self):
        self.local.wait()
        self.copy(self.own, 1, 1).wait_recv()
        self.copy(self.own, 3, 1).wait_recv()

    def drain(self):
        for copy in self.sent:
            copy.wait_send()


def local_copies(pairs, sem):
    copies = [pltpu.make_async_copy(src, dst, sem.at[i]) for i, (src, dst) in enumerate(pairs)]
    for copy in copies:
        copy.start()
    for copy in copies:
        copy.wait()


def wide_masks(size):
    masks = list(range(2, size, 2))
    return sorted(masks, key=lambda m: (m != 2, -m))


def head_lanes(value, head):
    lane = lax.broadcasted_iota(jnp.int32, value.shape, 1)
    inside = (lane < HEAD_DIM) if head == 0 else (lane >= HEAD_DIM)
    return jnp.where(inside, value, jnp.zeros_like(value))


def join_heads(first, second):
    lane = lax.broadcasted_iota(jnp.int32, (first.shape[0], 2 * HEAD_DIM), 1)
    return jnp.where(lane < HEAD_DIM, first, second)


def attend_pair(pair, cols, qkv, codes_q, codes_k, mixed, stats):
    lanes = [pl.ds(pl.multiple_of(third * cols + pair * 128, 128), 128) for third in range(3)]
    blocks = qkv.shape[0] // TILE
    for block in range(blocks):
        rows = slice(block * TILE, (block + 1) * TILE)
        both = qkv[rows, lanes[0]]
        outs, levels = [], []
        for head in range(2):
            queries = head_lanes(both, head)
            scores = [
                masked_scores(
                    block,
                    dot_nt(queries, qkv[tile * TILE : (tile + 1) * TILE, lanes[1]]),
                    tile,
                    codes_q,
                    codes_k,
                )
                for tile in range(block + 1)
            ]
            top = functools.reduce(jnp.maximum, [jnp.max(x, axis=1, keepdims=True) for x in scores])
            powers = [jnp.exp(x - top) for x in scores]
            total = functools.reduce(jnp.add, [jnp.sum(e, axis=1, keepdims=True) for e in powers])
            share = 1.0 / total
            outs.append(
                functools.reduce(
                    jnp.add,
                    [
                        dot_nn((e * share).astype(BF), qkv[tile * TILE : (tile + 1) * TILE, lanes[2]])
                        for tile, e in enumerate(powers)
                    ],
                )
            )
            levels.append(top + jnp.log(total))
        mixed[rows, lanes_of(pair)] = join_heads(outs[0], outs[1]).astype(BF)
        stats[rows, lanes_of(pair)] = join_heads(levels[0], levels[1])


def lanes_of(pair):
    return pl.ds(pl.multiple_of(pair * 128, 128), 128)


def forward_kernel(
    sizes,
    own_qkv,
    own_out,
    own_up,
    own_down,
    prefix_in,
    later_in,
    prefix_cot,
    later_cot,
    active_ref,
    gain1,
    bias1,
    out_bias,
    gain2,
    bias2,
    shift,
    factor,
    up_bias,
    codes_q,
    codes_k,
    w_qkv,
    w_out,
    w_up,
    w_down,
    h1,
    df,
    h2,
    qkv,
    mixed,
    stats,
    attn,
    acted,
    slope,
    down_grad,
    wbuf,
    lhs,
    qkv_v,
    mixed_v,
    stats_v,
    x_v,
    cot_v,
    h1_v,
    df_v,
    h2_v,
    terms_v,
    near_v,
    pass_v,
    far_v,
    attn_v,
    acted_v,
    slope_v,
    grad_v,
    gather_send,
    gather_recv,
    spread_send,
    spread_recv,
    sum_send,
    sum_recv,
    local_sem,
):
    seq_size, pre_part, later_part = sizes
    part = pre_part + later_part
    cols = own_qkv.shape[1] // 3
    ff_cols = own_up.shape[1]
    wide = wide_masks(seq_size)
    pre = lax.axis_index("pre")
    near_id = {"pre": xor(pre, 1)}
    far_id = {"pre": xor(pre, 2)}

    def gather(i, own, land):
        return Gather(own, land, own.shape[0], gather_send.at[i], gather_recv.at[i], local_sem.at[i])

    get_qkv = gather(0, own_qkv, w_qkv)
    get_out = gather(1, own_out, w_out)
    get_up = gather(2, own_up, w_up)
    get_down = gather(3, own_down, w_down)
    get_h1 = Spread(h1_v, h1, part, spread_send.at[0], spread_recv.at[0], local_sem.at[4])
    get_df = Spread(df_v, df, part, spread_send.at[1], spread_recv.at[1], local_sem.at[5])
    get_h2 = Spread(h2_v, h2, part, spread_send.at[2], spread_recv.at[2], local_sem.at[6])

    greet(wide)
    get_qkv.begin(1, *wide)
    get_qkv.keep()
    get_out.begin(1, *wide)
    get_out.keep()
    local_copies(
        [
            (prefix_in, x_v.at[:pre_part, :]),
            (later_in, x_v.at[pre_part:, :]),
            (prefix_cot, cot_v.at[:pre_part, :]),
            (later_cot, cot_v.at[pre_part:, :]),
        ],
        local_sem.at[8:12],
    )
    chunk = 32

    @pl.loop(0, part // chunk)
    def _(i):
        rows = rows_of(i, chunk)
        value, _, _ = layer_norm_parts(x_v[rows, :].astype(F32), gain1[...], bias1[...])
        h1_v[rows, :] = value.astype(BF)

    get_h1.begin()

    @pl.loop(0, part // chunk)
    def _(i):
        rows = rows_of(i, chunk)
        df_v[rows, :] = (active_ref[rows, :] * cot_v[rows, :].astype(F32)).astype(BF)

    get_df.begin()
    get_qkv.forward(wide[0])
    get_h1.forward()
    for mask in wide[1:-1]:
        get_qkv.forward(mask)
    get_up.begin(1, *wide)
    get_up.keep()
    get_qkv.forward(wide[-1])
    get_h1.finish()
    get_df.forward()
    load = pltpu.make_async_copy(h1, lhs, local_sem.at[12])
    load.start()
    get_qkv.finish(wide)
    local_copies([(w_qkv, wbuf.at[:, : 3 * cols])], local_sem.at[8:9])
    load.wait()
    for mask in wide:
        get_out.forward(mask)

    @pl.loop(0, 4)
    def _(r):
        member = lax.rem(r, 2) * (xor(pre, 1) - pre) + lax.div(r, 2) * (xor(pre, 2) - pre) + pre
        head_rows = rows_of(member, pre_part)
        tail_rows = pl.ds(pl.multiple_of(4 * pre_part + member * later_part, 64), later_part)

        @pl.loop(0, 3)
        def _(j):
            lanes = pl.ds(pl.multiple_of(j * cols, cols), cols)
            value = dot_nn(lhs[rows_of(r, part), :], wbuf[:, lanes])
            value = ((value + shift[:, lanes]) * factor[:, lanes]).astype(BF)
            qkv_v[head_rows, lanes] = value[:pre_part]
            qkv_v[tail_rows, lanes] = value[pre_part:]

    save_qkv = pltpu.make_async_copy(qkv_v, qkv, local_sem.at[13])
    save_qkv.start()
    get_up.forward(wide[0])
    get_df.finish()
    pairs = cols // 128

    @pl.loop(0, pairs)
    def _(pair):
        attend_pair(pair, cols, qkv_v, codes_q[...], codes_k[...], mixed_v, stats_v)

    save_stats = pltpu.make_async_copy(stats_v, stats, local_sem.at[14])
    save_stats.start()
    for mask in wide[1:-1]:
        get_up.forward(mask)
    get_down.begin(1, *wide)
    get_down.keep()
    get_out.finish(wide)
    local_copies([(w_out, wbuf.at[:cols, :])], local_sem.at[8:9])

    def position_rows(r):
        member = xor(pre, r) if r else pre
        return (
            rows_of(member, pre_part),
            pl.ds(pl.multiple_of(4 * pre_part + member * later_part, 64), later_part),
        )

    def out_term(r, store):
        head_rows, tail_rows = position_rows(r)

        @pl.loop(0, D // 512)
        def _(j):
            lanes = rows_of(j, 512)
            store(
                lanes,
                dot_nn(mixed_v[head_rows, :], wbuf[:cols, lanes]),
                dot_nn(mixed_v[tail_rows, :], wbuf[:cols, lanes]),
            )

    def keep_term(slot):
        def store(lanes, head, tail):
            terms_v[slot, :pre_part, lanes] = head.astype(BF)
            terms_v[slot, pre_part:, lanes] = tail.astype(BF)

        return store

    near = [
        remote(terms_v.at[i], near_v.at[i], sum_send.at[i], sum_recv.at[i], **near_id)
        for i in range(2)
    ]
    far = remote(pass_v, far_v, sum_send.at[2], sum_recv.at[2], **far_id)
    out_term(3, keep_term(0))
    near[0].start()
    out_term(1, keep_term(1))
    near[1].start()
    near[0].wait_recv()

    def pass_term(lanes, head, tail):
        pass_v[:pre_part, lanes] = (head + near_v[0, :pre_part, lanes].astype(F32)).astype(BF)
        pass_v[pre_part:, lanes] = (tail + near_v[0, pre_part:, lanes].astype(F32)).astype(BF)

    out_term(2, pass_term)
    far.start()
    near[1].wait_recv()

    def own_term(lanes, head, tail):
        bias = out_bias[:, lanes]
        attn_v[:pre_part, lanes] = head + near_v[1, :pre_part, lanes].astype(F32) + bias
        attn_v[pre_part:, lanes] = tail + near_v[1, pre_part:, lanes].astype(F32) + bias

    out_term(0, own_term)
    moves = []
    for r in range(4):
        head_rows, tail_rows = position_rows(r)
        moves.append((mixed_v.at[head_rows, :], mixed.at[r * part : r * part + pre_part, :]))
        moves.append((mixed_v.at[tail_rows, :], mixed.at[r * part + pre_part : (r + 1) * part, :]))
    local_copies(moves, local_sem.at[16:24])
    get_up.forward(wide[-1])
    far.wait_recv()

    @pl.loop(0, part // chunk)
    def _(i):
        rows = rows_of(i, chunk)
        branch = attn_v[rows, :] + far_v[rows, :].astype(F32)
        attn_v[rows, :] = branch
        value, _, _ = layer_norm_parts(x_v[rows, :].astype(F32) + branch, gain2[...], bias2[...])
        h2_v[rows, :] = value.astype(BF)

    get_h2.begin()
    save_attn = pltpu.make_async_copy(attn_v, attn, local_sem.at[15])
    save_attn.start()
    get_down.forward(wide[0])
    get_up.finish(wide)
    load = pltpu.make_async_copy(w_up, wbuf, local_sem.at[12])
    load.start()
    get_h2.forward()
    get_h2.finish()
    local_copies([(h2, lhs)], local_sem.at[8:9])
    load.wait()

    @pl.loop(0, 4)
    def _(r):
        rows = rows_of(r, part)

        @pl.loop(0, ff_cols // 512)
        def _(j):
            lanes = rows_of(j, 512)
            upper = dot_nn(lhs[rows, :], wbuf[:, lanes]) + up_bias[:, lanes]
            cumulative = 0.5 * (1.0 + lax.erf(upper * (1.0 / math.sqrt(2.0))))
            density = jnp.exp(-0.5 * upper * upper) * (1.0 / math.sqrt(2.0 * math.pi))
            acted_v[rows, lanes] = (upper * cumulative).astype(BF)
            slope_v[rows, lanes] = (cumulative + upper * density).astype(BF)

    saves = [
        pltpu.make_async_copy(acted_v, acted, local_sem.at[12]),
        pltpu.make_async_copy(slope_v, slope, local_sem.at[8]),
    ]
    for save in saves:
        save.start()
    for mask in wide[1:-1]:
        get_down.forward(mask)
    local_copies([(df, lhs)], local_sem.at[9:10])

    @pl.loop(0, D // 256)
    def _(i):
        lanes = rows_of(i, 256)
        turned = lhs[:, lanes].T

        @pl.loop(0, ff_cols // 512)
        def _(j):
            grad_v[:, rows_of(j, 512)] = dot_nn(turned, acted_v[:, rows_of(j, 512)]).astype(BF)

        save = pltpu.make_async_copy(grad_v, down_grad.at[lanes, :], local_sem.at[9])
        save.start()
        save.wait()

    get_down.forward(wide[-1])
    get_down.finish(wide)
    for save in (*saves, save_qkv, save_stats, save_attn):
        save.wait()
    for item in (get_qkv, get_out, get_up, get_down, get_h1, get_df, get_h2):
        item.drain()
    for copy in (*near, far):
        copy.wait_send()


def forward_pass(seq_size, pre_part, later_part, *operands):
    own_qkv, own_out, own_up = operands[:3]
    part = pre_part + later_part
    length = 4 * part
    width = own_qkv.shape[1]
    cols = width // 3
    ff_cols = own_up.shape[1]
    hbm = pl.BlockSpec(memory_space=pl.ANY)
    vmem = pl.BlockSpec(memory_space=pltpu.VMEM)

    def out(shape, kind=BF):
        return jax.ShapeDtypeStruct(shape, kind)

    outs = (
        out((D, width)),
        out((cols, D)),
        out((D, ff_cols)),
        out((D, ff_cols)),
        out((length, D)),
        out((length, D)),
        out((length, D)),
        out((length, width)),
        out((length, cols)),
        out((length, cols), F32),
        out((part, D), F32),
        out((length, ff_cols)),
        out((length, ff_cols)),
        out((D, ff_cols)),
    )
    dma = pltpu.SemaphoreType.DMA
    return pl.pallas_call(
        functools.partial(forward_kernel, (seq_size, pre_part, later_part)),
        out_shape=outs,
        in_specs=[hbm] * 8 + [vmem] * (len(operands) - 8),
        out_specs=[hbm] * len(outs),
        scratch_shapes=[
            pltpu.VMEM((D, max(ff_cols, width)), BF),
            pltpu.VMEM((length, D), BF),
            pltpu.VMEM((length, width), BF),
            pltpu.VMEM((length, cols), BF),
            pltpu.VMEM((length, cols), F32),
            pltpu.VMEM((part, D), BF),
            pltpu.VMEM((part, D), BF),
            pltpu.VMEM((part, D), BF),
            pltpu.VMEM((part, D), BF),
            pltpu.VMEM((part, D), BF),
            pltpu.VMEM((2, part, D), BF),
            pltpu.VMEM((2, part, D), BF),
            pltpu.VMEM((part, D), BF),
            pltpu.VMEM((part, D), BF),
            pltpu.VMEM((part, D), F32),
            pltpu.VMEM((length, ff_cols), BF),
            pltpu.VMEM((length, ff_cols), BF),
            pltpu.VMEM((256, ff_cols), BF),
            dma((4, seq_size)),
            dma((4, seq_size)),
            dma((3, 4)),
            dma((3, 4)),
            dma((3,)),
            dma((3,)),
            dma((24,)),
        ],
        compiler_params=pltpu.CompilerParams(
            collective_id=0, has_side_effects=True, vmem_limit_bytes=62 * 2**20
        ),
        cost_estimate=pl.CostEstimate(
            flops=2 * length * D * (width + cols + 2 * ff_cols),
            bytes_accessed=8 * D * ff_cols,
            transcendentals=length * ff_cols,
        ),
        name="forward_pass",
    )(*operands)


class Seq:
    def __init__(self):
        self.size = lax.axis_size("seq")
        self.place = lax.axis_index("seq")

    def swap(self, value, mask):
        return lax.ppermute(value, "seq", [(i, i ^ mask) for i in range(self.size)])

    def gather(self, own):
        blocks = [own, self.swap(own, 1)]
        for mask in range(2, self.size, 2):
            blocks.append(self.swap(own, mask))
            blocks.append(self.swap(blocks[-1], 1))
        return blocks

    def reduce(self, blocks):
        total = None
        masks = [mask for mask in range(2, self.size, 2)][::-1] + [0]
        for mask in masks:
            other = self.swap(blocks[mask + 1], 1)
            part = blocks[mask].astype(F32) + other.astype(F32)
            if mask:
                part = self.swap(part.astype(BF), mask).astype(F32)
            total = part if total is None else total + part
        return total

    def reorder(self, value, axis):
        block = value.shape[axis] // self.size
        return jnp.concatenate(
            [
                lax.dynamic_slice_in_dim(value, jnp.bitwise_xor(self.place, i) * block, block, axis)
                for i in range(self.size)
            ],
            axis=axis,
        )


def over_pre(value, mask):
    return lax.ppermute(value, "pre", [(i, i ^ mask) for i in range(lax.axis_size("pre"))])


def gather_pre(own):
    far = over_pre(own, 2)
    near = over_pre(own, 1)
    return [own, near, far, over_pre(far, 1)]


def scatter_pre(blocks):
    a = blocks[0] + over_pre(blocks[1].astype(BF), 1).astype(F32)
    b = blocks[2] + over_pre(blocks[3].astype(BF), 1).astype(F32)
    return a + over_pre(b.astype(BF), 2).astype(F32)


def sum_all(value):
    for mask in (1, 2):
        value = value + over_pre(value, mask)
    size = lax.axis_size("seq")
    mask = 1
    while mask < size:
        value = value + lax.ppermute(value, "seq", [(i, i ^ mask) for i in range(size)])
        mask *= 2
    return value


def absolute_pre(blocks, place):
    first = place % 2 == 0
    low = place < 2
    a = [jnp.where(first, blocks[0], blocks[1]), jnp.where(first, blocks[1], blocks[0])]
    b = [jnp.where(first, blocks[2], blocks[3]), jnp.where(first, blocks[3], blocks[2])]
    return [jnp.where(low, u, w) for u, w in zip(a, b)] + [jnp.where(low, w, u) for u, w in zip(a, b)]


def on_device(
    prefix_in,
    later_in,
    doc_lengths,
    doc_exit,
    token_skip,
    first_gain,
    first_bias,
    qkv_weight,
    query_bias,
    value_bias,
    out_weight,
    out_bias,
    second_gain,
    second_bias,
    up_weight,
    up_bias,
    down_weight,
    down_bias,
    prefix_cot,
    later_cot,
):
    scale = 1.0 / math.sqrt(HEAD_DIM)
    pre_part = prefix_in.shape[1]
    later_part = later_in.shape[1]
    part = pre_part + later_part
    parts = lax.axis_size("pre")
    place = lax.axis_index("pre")
    seq = Seq()
    seq_count = seq.size
    seq_place = seq.place
    own_d = D // seq_count
    cols = D // parts
    ff_cols = FF // parts
    length = parts * part

    packed = jnp.concatenate(
        [
            first_gain,
            first_bias,
            query_bias,
            value_bias,
            out_bias,
            second_gain,
            second_bias,
            down_bias,
            up_bias,
        ]
    ).reshape(-1, 128)
    small = seq.reorder(jnp.stack(seq.gather(packed)).reshape(seq_count, -1), 0).astype(F32)
    vectors = [small[:, i * own_d : (i + 1) * own_d].reshape(1, D) for i in range(8)]
    full_up_bias = small[:, 8 * own_d :].reshape(1, FF)
    (gain1, bias1, qb, vb, ob, gain2, bias2, db) = vectors

    def section(weight, start, width):
        return lax.dynamic_slice_in_dim(weight, start + place * width, width, 1)

    own_qkv = jnp.concatenate([section(qkv_weight, i * D, cols) for i in range(3)], axis=1)
    block_rows = own_d // parts
    out_block = lax.dynamic_slice_in_dim(out_weight, place * block_rows, block_rows, 0)
    shuffle = [
        ((b % parts) * seq_count + b // parts, (b // seq_count) * seq_count + b % seq_count)
        for b in range(parts * seq_count)
    ]
    own_out = lax.ppermute(out_block, ("pre", "seq"), shuffle)
    doc_id, live = token_tables(doc_lengths, doc_exit, token_skip)
    live_here = lax.dynamic_slice_in_dim(live[0], place * later_part, later_part, 0)
    active = jnp.concatenate([jnp.ones((pre_part,), F32), live_here.astype(F32)])[:, None]
    codes_q = jnp.concatenate([jnp.full((PRE,), -1, jnp.int32), doc_id[0]])[:, None]
    codes_k = jnp.concatenate(
        [jnp.full((PRE,), -1, jnp.int32), jnp.where(live[0], doc_id[0], -2)]
    )[None, :]

    def own_columns(vector, width):
        return lax.dynamic_slice_in_dim(vector, place * width, width, 1)

    shift = jnp.concatenate(
        [own_columns(qb, cols), jnp.zeros((1, cols), F32), own_columns(vb, cols)], axis=1
    )
    factor = jnp.concatenate([jnp.full((1, cols), scale, F32), jnp.ones((1, 2 * cols), F32)], axis=1)
    (w_qkv, w_out, w_up, w_down, h1, df, h2, qkv, mixed, stats, attn, acted, slope, down_grad) = forward_pass(
        seq_count,
        pre_part,
        later_part,
        own_qkv,
        own_out,
        section(up_weight, 0, ff_cols),
        section(down_weight, 0, ff_cols),
        prefix_in[0],
        later_in[0],
        prefix_cot[0],
        later_cot[0],
        active,
        gain1,
        bias1,
        ob,
        gain2,
        bias2,
        shift,
        factor,
        own_columns(full_up_bias, ff_cols),
        codes_q,
        codes_k,
    )

    tokens = jnp.concatenate([prefix_in[0], later_in[0]], axis=0).astype(F32)
    cotangent = jnp.concatenate([prefix_cot[0], later_cot[0]], axis=0).astype(F32)
    ffn_grad = (active * cotangent).astype(BF)
    _, first_normed, first_scaling = layer_norm_parts(tokens, gain1, bias1)
    _, second_normed, second_scaling = layer_norm_parts(tokens + attn, gain2, bias2)
    ffn_terms = lax.dot_general(
        acted, w_down, (((1,), (1,)), ((), ())), preferred_element_type=F32
    )
    ffn = scatter_pre([ffn_terms[i * part : (i + 1) * part] for i in range(parts)]) + db
    result = tokens + active * (attn + ffn)
    square_sums = jnp.stack(
        [
            jnp.sum(active * result * result),
            jnp.sum(active * attn * attn),
            jnp.sum(active * ffn * ffn),
            jnp.sum(active),
        ]
    )

    acted_grad = jnp.dot(df, w_down, preferred_element_type=F32)
    upper_grad = (acted_grad * slope.astype(F32)).astype(BF)
    second_terms = lax.dot_general(
        upper_grad, w_up, (((1,), (1,)), ((), ())), preferred_element_type=F32
    )
    up_grad = lax.dot_general(h2, upper_grad, (((0,), (0,)), ((), ())), preferred_element_type=F32)
    up_grad = up_grad.astype(BF)
    second_grad = scatter_pre([second_terms[i * part : (i + 1) * part] for i in range(parts)])
    middle_grad = norm_back(second_grad, second_normed, second_scaling, gain2)
    attn_grad = (active * cotangent + middle_grad).astype(BF)

    dattn = jnp.concatenate(gather_pre(attn_grad), axis=0)
    mixed_grad = lax.dot_general(
        dattn, w_out, (((1,), (1,)), ((), ())), preferred_element_type=F32
    ).astype(BF)
    out_grad = lax.dot_general(mixed, dattn, (((0,), (0,)), ((), ())), preferred_element_type=F32)
    out_grad = out_grad.astype(BF)

    def by_member(blocks):
        return absolute_pre(blocks, place)

    do_blocks = by_member([mixed_grad[i * part : (i + 1) * part] for i in range(parts)])
    do = jnp.concatenate([b[:pre_part] for b in do_blocks] + [b[pre_part:] for b in do_blocks], axis=0)
    grads = jnp.concatenate(attend_back(qkv, do, stats, codes_q, codes_k), axis=1)
    blocks = [
        jnp.concatenate(
            [
                grads[i * pre_part : (i + 1) * pre_part],
                grads[PRE + i * later_part : PRE + (i + 1) * later_part],
            ],
            axis=0,
        )
        for i in range(parts)
    ]
    project_grad = jnp.concatenate(by_member(blocks), axis=0)
    qkv_grad = lax.dot_general(
        h1, project_grad, (((0,), (0,)), ((), ())), preferred_element_type=F32
    ).astype(BF)
    first_terms = lax.dot_general(
        project_grad, w_qkv, (((1,), (1,)), ((), ())), preferred_element_type=F32
    )
    first_grad = scatter_pre([first_terms[i * part : (i + 1) * part] for i in range(parts)])
    input_grad = cotangent + middle_grad + norm_back(first_grad, first_normed, first_scaling, gain1)

    def spread(grad):
        rows = grad.shape[0] // seq_count
        return seq.reduce(
            [
                lax.dynamic_slice_in_dim(grad, jnp.bitwise_xor(seq_place, i) * rows, rows, 0)
                for i in range(seq_count)
            ]
        ).astype(BF)

    def shared(block):
        return absolute_pre(gather_pre(block), place)

    down_full = jnp.concatenate(shared(spread(down_grad)), axis=1).astype(F32)
    up_full = jnp.concatenate(shared(spread(up_grad)), axis=1).astype(F32)
    out_own = lax.ppermute(spread(out_grad), ("pre", "seq"), [(b, a) for a, b in shuffle])
    out_full = jnp.concatenate(shared(out_own), axis=0).astype(F32)
    qkv_blocks = shared(spread(qkv_grad))
    qkv_full = jnp.concatenate(
        [block[:, i * cols : (i + 1) * cols] for i in range(3) for block in qkv_blocks], axis=1
    ).astype(F32)

    def placed(vector, width):
        zeros = jnp.zeros((width * parts,), F32)
        return lax.dynamic_update_slice_in_dim(zeros, vector, place * width, 0)

    column_sums = jnp.sum(project_grad.astype(F32), axis=0)
    feature_sums = jnp.stack(
        [
            jnp.sum(first_grad * first_normed, axis=0),
            jnp.sum(first_grad, axis=0),
            jnp.sum(attn_grad.astype(F32), axis=0),
            jnp.sum(second_grad * second_normed, axis=0),
            jnp.sum(second_grad, axis=0),
            jnp.sum(ffn_grad.astype(F32), axis=0),
        ]
    )
    sums = [
        feature_sums[0],
        feature_sums[1],
        placed(column_sums[:cols], cols),
        placed(column_sums[2 * cols :], cols),
        feature_sums[2],
        feature_sums[3],
        feature_sums[4],
        feature_sums[5],
        placed(jnp.sum(upper_grad.astype(F32), axis=0), ff_cols),
        jnp.concatenate([square_sums, jnp.zeros((124,), F32)]),
    ]
    flat = sum_all(jnp.concatenate(sums).reshape(-1, 128)).reshape(-1)
    totals = [flat[i * D : (i + 1) * D] for i in range(8)]
    total_ub = flat[8 * D : 8 * D + FF]
    total_squares = flat[8 * D + FF : 8 * D + FF + 4]

    def own_share(vector):
        width = vector.shape[0] // seq_count
        return lax.dynamic_slice_in_dim(vector, seq_place * width, width, 0)

    residual_rms = jnp.sqrt(total_squares[:3] / (total_squares[3] * D))
    result = result.astype(BF)
    input_grad = input_grad.astype(BF)
    return (
        result[:pre_part][None],
        result[pre_part:][None],
        input_grad[:pre_part][None],
        input_grad[pre_part:][None],
        own_share(totals[0]),
        own_share(totals[1]),
        qkv_full,
        own_share(totals[2]),
        own_share(totals[3]),
        out_full,
        own_share(totals[4]),
        own_share(totals[5]),
        own_share(totals[6]),
        up_full,
        own_share(total_ub),
        down_full,
        own_share(totals[7]),
        residual_rms,
    )


def solution(mesh):
    placed = (
        P("seq", "pre", None),
        P("seq", "pre", None),
        P("seq", None),
        P("seq", None),
        P("seq", None),
        P("seq"),
        P("seq"),
        P("seq", None),
        P("seq"),
        P("seq"),
        P("seq", None),
        P("seq"),
        P("seq"),
        P("seq"),
        P("seq", None),
        P("seq"),
        P("seq", None),
        P("seq"),
        P("seq", "pre", None),
        P("seq", "pre", None),
    )
    return jax.shard_map(
        on_device,
        mesh=mesh,
        in_specs=placed,
        out_specs=(
            P("seq", "pre", None),
            P("seq", "pre", None),
            P("seq", "pre", None),
            P("seq", "pre", None),
            P("seq"),
            P("seq"),
            P("seq", None),
            P("seq"),
            P("seq"),
            P("seq", None),
            P("seq"),
            P("seq"),
            P("seq"),
            P("seq", None),
            P("seq"),
            P("seq", None),
            P("seq"),
            P(),
        ),
        check_vma=False,
    )
```

time: 1350 us -> 1020 us (0.76)
  starting transfers between devices: 428 us -> 75.6 us
  Pallas kernels: 74.3 us -> 377 us
  local copies, waits for them, and re-layouts: 243 us -> 74.2 us
  other arithmetic: 160 us -> 66.2 us
  matrix products: 186 us -> 101 us
  waiting for transfers between devices: 241 us -> 305 us
    pallas_call x2, Pallas kernels: 74.3 us -> 377 us  [the longest x1 341 us: forward_pass(): pl.pallas_call(functools.partial(forward_kernel, (seq_size, pre_part, lat...]
    ppermute x105 -> x35, starting transfers between devices: 258 us -> 26.9 us  [swap(): return lax.ppermute(value, 'seq', [(i, i ^ mask) for i in range(self.size)])]
    ppermute x38 -> x26, starting transfers between devices: 145 us -> 41.2 us  [over_pre(): lax.ppermute(value, 'pre', [(i, i ^ mask) for i in range(lax.axis_size('p...]
    rev x9 -> x0, local copies, waits for them, and re-layouts: 94.6 us -> none  [flip(): swapped = lax.rev(value.reshape(split), (axis + 1,)).reshape(shape)]
    dot_general x4 -> x0, matrix products: 77.5 us -> none  [the longest x1 44 us: on_device(): upper = jnp.dot(h2, w_up, preferred_element_type=F32) + own_ub]
    ppermute x105 -> x35, waiting for transfers between devices: 179 us -> 250 us  [swap(): return lax.ppermute(value, 'seq', [(i, i ^ mask) for i in range(self.size)])]
    reshape x13 -> x0, local copies, waits for them, and re-layouts: 51.7 us -> none  [flip(): swapped = lax.rev(value.reshape(split), (axis + 1,)).reshape(shape)]
    unnamed x34 -> x3, other arithmetic: 33.3 us -> 0.01 us
  transfers between devices with their start and end apart: 148 -> 66, of which waited for: 36 -> 21; matrix products, arithmetic and copies ran while one was open for 39% -> 19% of each run, Pallas kernels for 6% -> 0%
where the time goes in v2:
time: 1020 us; the launch traced here: 1000 us
  Pallas kernels  377 us (37%)
  waiting for transfers between devices  305 us (30%)
  matrix products  101 us (10%)
  starting transfers between devices  75.6 us (7%)
  local copies, waits for them, and re-layouts  74.2 us (7%)
  other arithmetic  66.2 us (6%)
    pallas_call x1, Pallas kernels, forward_pass(): pl.pallas_call(functools.partial(forward_kernel, (seq_size, pre_part, lat...  341 us
    ppermute x35, waiting for transfers between devices, swap(): return lax.ppermute(value, 'seq', [(i, i ^ mask) for i in range(self.size)])  250 us
    ppermute x26, waiting for transfers between devices, over_pre(): lax.ppermute(value, 'pre', [(i, i ^ mask) for i in range(lax.axis_size('p...  47.8 us
    ppermute x26, starting transfers between devices, over_pre(): lax.ppermute(value, 'pre', [(i, i ^ mask) for i in range(lax.axis_size('p...  41.2 us
    pallas_call x1, Pallas kernels, attend_back(): pl.pallas_call(attend_back_kernel, out_shape=[jax.ShapeDtypeStruct((lengt...  36 us
    unnamed x149, local copies, waits for them, and re-layouts  33.5 us
    ppermute x35, starting transfers between devices, swap(): return lax.ppermute(value, 'seq', [(i, i ^ mask) for i in range(self.size)])  26.9 us
  transfers between devices with their start and end apart: 66, of which 21 were waited for; matrix products, arithmetic and copies ran while one was open for 19% of the time, Pallas kernels for 0%

profile of v2, /device:TPU:5, one launch (start us, length us, event | category | flops | bytes accessed | tf_op | source)
XLA Modules:
  0.0 1001.6 jit_solution(12956472121989689967)
XLA Ops:
  37.4 341.2 %forward_pass.1 = (bf16[2048,1536]{1,0:T(8,128)(2,1)}, bf16[512,2048]{1,0:T(8,128)(2,1)}, bf16[2048,2048]{1,0:T(8,128)(2,1)}, bf16[2048,2048]{1,0:T(8,128)(2,1)}...) custom-call(bf16[256,1536]{1,0:T(8,128)(2,1)} %pad_maximum_fusion.10, ...), custom_call_target="tpu_custom_call" | custom-call | flops 32212254720 | bytes 33554432 | tf_op jit(solution)/shard_map/forward_pass/pallas_call | solution.py:691
  384.9 15.1 %fusion.44 = (bf16[1280,2048]{1,0:T(8,128)(2,1)S(1)}, f32[1280,2048]{1,0:T(8,128)}) fusion(bf16[1280,2048]{1,0:T(8,128)(2,1)} %get-tuple-element.36, bf16[2048,2048]{1,0:T(8,128)(2,1)S(1)} %copy-done.41), kind=kOutput, calls=%fused_computation.260 | convolution fusion | flops 10740039680 | bytes 29360128 | tf_op jit(solution)/shard_map/dot_general | solution.py:917
  401.2 15.9 %convert_reduce_fusion = (f32[2048]{0:T(1024)S(1)}, bf16[1280,2048]{1,0:T(8,128)(2,1)S(1)}) fusion(bf16[1280,2048]{1,0:T(8,128)(2,1)} %get-tuple-element.39, bf16[1280,2048]{1,0:T(8,128)(2,1)} %get-tuple-element.38, bf16[2048,2048]{1,0:T(8,128)(2,1)} %get-tuple-element.37), kind=kOutput, calls=%fused_computation | convolution fusion | flops 10750523392 | bytes 24125440 | tf_op jit(solution)/shard_map/dot_general | solution.py:931
  417.1 15.3 %convolution_convert_fusion = bf16[2048,2048]{1,0:T(8,128)(2,1)S(1)} fusion(bf16[1280,2048]{1,0:T(8,128)(2,1)} %get-tuple-element.50, bf16[1280,2048]{1,0:T(8,128)(2,1)S(1)} %get-tuple-element.233), kind=kOutput, calls=%fused_computation.3 | convolution fusion | flops 10741612544 | bytes 18874368 | tf_op jit(solution)/shard_map/dot_general | solution.py:936
  432.4 18.3 %fusion.45 = (bf16[1280,2048]{1,0:T(8,128)(2,1)}, f32[1280,2048]{1,0:T(8,128)}) fusion(bf16[1280,2048]{1,0:T(8,128)(2,1)} %copy-done.43, bf16[2048,2048]{1,0:T(8,128)(2,1)} %get-tuple-element.40), kind=kOutput, calls=%fused_computation.261 | convolution fusion | flops 10740039680 | bytes 29360128 | tf_op jit(solution)/shard_map/dot_general | solution.py:933
  468.2 13.4 %collective-permute-done.62 = bf16[256,2048]{1,0:T(8,128)(2,1)S(1)} collective-permute-done((bf16[256,2048]{1,0:T(8,128)(2,1)S(1)}, bf16[256,2048]{1,0:T(8,128)(2,1)S(1)}, u32[]{:S(2)}, u32[]{:S(2)}) %collective-permute-start.62) | collective-permute-done | bytes 1048608 | tf_op jit(solution)/shard_map/ppermute | solution.py:741
  483.1 20.9 %collective-permute-done.46 = bf16[256,2048]{1,0:T(8,128)(2,1)S(1)} collective-permute-done((bf16[256,2048]{1,0:T(8,128)(2,1)}, bf16[256,2048]{1,0:T(8,128)(2,1)S(1)}, u32[]{:S(2)}, u32[]{:S(2)}) %collective-permute-start.46) | collective-permute-done | bytes 1048608 | tf_op jit(solution)/shard_map/ppermute | solution.py:741
  504.9 21.7 %collective-permute-done.50 = bf16[256,2048]{1,0:T(8,128)(2,1)} collective-permute-done((bf16[256,2048]{1,0:T(8,128)(2,1)S(1)}, bf16[256,2048]{1,0:T(8,128)(2,1)}, u32[]{:S(2)}, u32[]{:S(2)}) %collective-permute-start.50) | collective-permute-done | bytes 1048608 | tf_op jit(solution)/shard_map/ppermute | solution.py:741
  527.3 21.8 %collective-permute-done.48 = bf16[256,2048]{1,0:T(8,128)(2,1)} collective-permute-done((bf16[256,2048]{1,0:T(8,128)(2,1)S(1)}, bf16[256,2048]{1,0:T(8,128)(2,1)}, u32[]{:S(2)}, u32[]{:S(2)}) %collective-permute-start.48) | collective-permute-done | bytes 1048608 | tf_op jit(solution)/shard_map/ppermute | solution.py:741
  558.5 38.5 %collective-permute-done.59 = bf16[256,2048]{1,0:T(8,128)(2,1)} collective-permute-done((bf16[256,2048]{1,0:T(8,128)(2,1)}, bf16[256,2048]{1,0:T(8,128)(2,1)}, u32[]{:S(2)}, u32[]{:S(2)}) %collective-permute-start.59) | collective-permute-done | bytes 1048608 | tf_op jit(solution)/shard_map/ppermute | solution.py:741
  611.2 15.1 %collective-permute-done.13 = bf16[320,2048]{1,0:T(8,128)(2,1)S(1)} collective-permute-done((bf16[320,2048]{1,0:T(8,128)(2,1)S(1)}, bf16[320,2048]{1,0:T(8,128)(2,1)S(1)}, u32[]{:S(2)}, u32[]{:S(2)}) %collective-permute-start.13) | collective-permute-done | bytes 1310752 | tf_op jit(solution)/shard_map/ppermute | solution.py:773
  637.4 16.8 %collective-permute-done.51 = bf16[256,2048]{1,0:T(8,128)(2,1)} collective-permute-done((bf16[256,2048]{1,0:T(8,128)(2,1)S(1)}, bf16[256,2048]{1,0:T(8,128)(2,1)}, u32[]{:S(2)}, u32[]{:S(2)}) %collective-permute-start.51) | collective-permute-done | bytes 1048608 | tf_op jit(solution)/shard_map/ppermute | solution.py:741
  654.2 36.5 %collective-permute-done.49 = bf16[256,2048]{1,0:T(8,128)(2,1)S(1)} collective-permute-done((bf16[256,2048]{1,0:T(8,128)(2,1)S(1)}, bf16[256,2048]{1,0:T(8,128)(2,1)S(1)}, u32[]{:S(2)}, u32[]{:S(2)}) %collective-permute-start.49) | collective-permute-done | bytes 1048608 | tf_op jit(solution)/shard_map/ppermute | solution.py:741
  698.7 16.8 %collective-permute-done.54 = bf16[256,2048]{1,0:T(8,128)(2,1)S(1)} collective-permute-done((bf16[256,2048]{1,0:T(8,128)(2,1)S(1)}, bf16[256,2048]{1,0:T(8,128)(2,1)S(1)}, u32[]{:S(2)}, u32[]{:S(2)}) %collective-permute-start.54) | collective-permute-done | bytes 1048608 | tf_op jit(solution)/shard_map/ppermute | solution.py:773
  727.7 6.5 convolution_convert_fusion.3
  735.6 36.0 %attend_back.1 = (bf16[1280,512]{1,0:T(8,128)(2,1)}, bf16[1280,512]{1,0:T(8,128)(2,1)}, bf16[1280,512]{1,0:T(8,128)(2,1)}) custom-call(bf16[1280,1536]{1,0:T(8,128)(2,1)} %get-tuple-element.41.q_ref.k_ref.v_ref, bf16[1280,1536]{1,0:T(8,128)(2,1)} %get-tuple-element.41.q_ref.k_ref.v_ref, bf16[1280,1536]{1,0:T(8,128)(2,1)} %get-tuple-element.41.q_ref.k_ref.v_ref, ...), custom_call_target="tpu_custom_call" | custom-call | flops 20132659200 | bytes 11796480 | tf_op jit(solution)/shard_map/attend_back/pallas_call | solution.py:149
  784.4 9.5 convolution_convert_fusion.1
  796.0 17.0 %fusion.46 = (bf16[1280,2048]{1,0:T(8,128)(2,1)}, f32[1280,2048]{1,0:T(8,128)}) fusion(bf16[2048,1536]{1,0:T(8,128)(2,1)} %get-tuple-element.47, bf16[320,1536]{1,0:T(8,128)(2,1)S(1)} %get-tuple-element.169, bf16[320,1536]{1,0:T(8,128)(2,1)S(1)} %get-tuple-element.168, bf16[320,1536]{1,0:T(8,128)(2,1)S(1)} %get-tuple-element.167, ...), kind=kOutput, calls=%fused_computation.262 | convolution fusion | flops 8071413760 | bytes 25952256 | tf_op jit(solution)/shard_map/dot_general | solution.py:969
  824.1 8.4 collective-permute-done.40
  843.8 15.6 %collective-permute-done.27 = bf16[256,1536]{0,1:T(8,128)(2,1)S(1)} collective-permute-done((bf16[256,1536]{0,1:T(8,128)(2,1)}, bf16[256,1536]{0,1:T(8,128)(2,1)S(1)}, u32[]{:S(2)}, u32[]{:S(2)}) %collective-permute-start.27) | collective-permute-done | bytes 786464 | tf_op jit(solution)/shard_map/ppermute | solution.py:741
  866.2 10.1 %collective-permute-done.31 = bf16[256,1536]{0,1:T(8,128)(2,1)S(1)} collective-permute-done((bf16[256,1536]{0,1:T(8,128)(2,1)S(1)}, bf16[256,1536]{0,1:T(8,128)(2,1)S(1)}, u32[]{:S(2)}, u32[]{:S(2)}) %collective-permute-start.31) | collective-permute-done | bytes 786464 | tf_op jit(solution)/shard_map/ppermute | solution.py:741
  886.0 16.8 %collective-permute-done.30 = bf16[256,1536]{0,1:T(8,128)(2,1)S(1)} collective-permute-done((bf16[256,1536]{0,1:T(8,128)(2,1)S(1)}, bf16[256,1536]{0,1:T(8,128)(2,1)S(1)}, u32[]{:S(2)}, u32[]{:S(2)}) %collective-permute-start.30) | collective-permute-done | bytes 786464 | tf_op jit(solution)/shard_map/ppermute | solution.py:741
  902.7 25.1 %collective-permute-done.28 = bf16[256,1536]{0,1:T(8,128)(2,1)S(1)} collective-permute-done((bf16[256,1536]{0,1:T(8,128)(2,1)S(1)}, bf16[256,1536]{0,1:T(8,128)(2,1)S(1)}, u32[]{:S(2)}, u32[]{:S(2)}) %collective-permute-start.28) | collective-permute-done | bytes 786464 | tf_op jit(solution)/shard_map/ppermute | solution.py:741
  936.5 11.6 %collective-permute-done.33 = bf16[256,1536]{0,1:T(8,128)(2,1)} collective-permute-done((bf16[256,1536]{0,1:T(8,128)(2,1)}, bf16[256,1536]{0,1:T(8,128)(2,1)}, u32[]{:S(2)}, u32[]{:S(2)}) %collective-permute-start.33) | collective-permute-done | bytes 786464 | tf_op jit(solution)/shard_map/ppermute | solution.py:773
  (378 shorter events, 235.0 us)
Async XLA Ops:
  383.2 72.8 %collective-permute-start.56 = (bf16[256,2048]{1,0:T(8,128)(2,1)}, bf16[256,2048]{1,0:T(8,128)(2,1)S(1)}, u32[]{:S(2)}, u32[]{:S(2)}) collective-permute-start(bf16[256,2048]{1,0:T(8,128)(2,1)} %get-tuple-element.134), channel_id=1, source_target_pairs={{0,1},{1,0},{2,3},{3,2},{4,5},{5,4},{6,7},{7,6},{8,9},{9,8},{10,11... | collective-permute-start | bytes 3145736 | tf_op jit(solution)/shard_map/ppermute | solution.py:741
  383.4 74.8 %collective-permute-start.60 = (bf16[256,2048]{1,0:T(8,128)(2,1)}, bf16[256,2048]{1,0:T(8,128)(2,1)}, u32[]{:S(2)}, u32[]{:S(2)}) collective-permute-start(bf16[256,2048]{1,0:T(8,128)(2,1)} %get-tuple-element.136), channel_id=1, source_target_pairs={{0,1},{1,0},{2,3},{3,2},{4,5},{5,4},{6,7},{7,6},{8,9},{9,8},{10,11... | collective-permute-start | bytes 3145736 | tf_op jit(solution)/shard_map/ppermute | solution.py:741
  384.6 73.8 %collective-permute-start.58 = (bf16[256,2048]{1,0:T(8,128)(2,1)}, bf16[256,2048]{1,0:T(8,128)(2,1)}, u32[]{:S(2)}, u32[]{:S(2)}) collective-permute-start(bf16[256,2048]{1,0:T(8,128)(2,1)} %get-tuple-element.137), channel_id=1, source_target_pairs={{0,1},{1,0},{2,3},{3,2},{4,5},{5,4},{6,7},{7,6},{8,9},{9,8},{10,11... | collective-permute-start | bytes 3145736 | tf_op jit(solution)/shard_map/ppermute | solution.py:741
  401.2 58.5 %collective-permute-start.9 = (bf16[320,2048]{1,0:T(8,128)(2,1)}, bf16[320,2048]{1,0:T(8,128)(2,1)}, u32[]{:S(2)}, u32[]{:S(2)}) collective-permute-start(bf16[320,2048]{1,0:T(8,128)(2,1)} %get-tuple-element.157), channel_id=1, source_target_pairs={{0,8},{8,0},{16,24},{24,16},{1,9},{9,1},{17,25},{25,17},{2,10},{10... | collective-permute-start | bytes 3932168 | tf_op jit(solution)/shard_map/ppermute | solution.py:773
  452.9 96.4 %collective-permute-start.12 = (bf16[320,2048]{1,0:T(8,128)(2,1)S(1)}, bf16[320,2048]{1,0:T(8,128)(2,1)S(1)}, u32[]{:S(2)}, u32[]{:S(2)}) collective-permute-start(bf16[320,2048]{1,0:T(8,128)(2,1)S(1)} %get-tuple-element.155), channel_id=1, source_target_pairs={{0,8},{8,0},{16,24},{24,16},{1,9},{9,1},{17,25},{25,17},{2,10},{10... | collective-permute-start | bytes 3932168 | tf_op jit(solution)/shard_map/ppermute | solution.py:773
  458.4 68.2 %collective-permute-start.50 = (bf16[256,2048]{1,0:T(8,128)(2,1)S(1)}, bf16[256,2048]{1,0:T(8,128)(2,1)}, u32[]{:S(2)}, u32[]{:S(2)}) collective-permute-start(bf16[256,2048]{1,0:T(8,128)(2,1)S(1)} %get-tuple-element.143), channel_id=1, source_target_pairs={{0,1},{1,0},{2,3},{3,2},{4,5},{5,4},{6,7},{7,6},{8,9},{9,8},{10,11... | collective-permute-start | bytes 3145736 | tf_op jit(solution)/shard_map/ppermute | solution.py:741
  459.7 89.4 %collective-permute-start.48 = (bf16[256,2048]{1,0:T(8,128)(2,1)S(1)}, bf16[256,2048]{1,0:T(8,128)(2,1)}, u32[]{:S(2)}, u32[]{:S(2)}) collective-permute-start(bf16[256,2048]{1,0:T(8,128)(2,1)S(1)} %get-tuple-element.144), channel_id=1, source_target_pairs={{0,1},{1,0},{2,3},{3,2},{4,5},{5,4},{6,7},{7,6},{8,9},{9,8},{10,11... | collective-permute-start | bytes 3145736 | tf_op jit(solution)/shard_map/ppermute | solution.py:741
  481.6 120.5 %collective-permute-start.8 = (bf16[320,2048]{1,0:T(8,128)(2,1)S(1)}, bf16[320,2048]{1,0:T(8,128)(2,1)S(1)}, u32[]{:S(2)}, u32[]{:S(2)}) collective-permute-start(bf16[320,2048]{1,0:T(8,128)(2,1)S(1)} %get-tuple-element.156), channel_id=1, source_target_pairs={{0,8},{8,0},{16,24},{24,16},{1,9},{9,1},{17,25},{25,17},{2,10},{10... | collective-permute-start | bytes 3932168 | tf_op jit(solution)/shard_map/ppermute | solution.py:773
  504.0 52.3 %collective-permute-start.57 = (bf16[256,2048]{1,0:T(8,128)(2,1)}, bf16[256,2048]{1,0:T(8,128)(2,1)}, u32[]{:S(2)}, u32[]{:S(2)}) collective-permute-start(bf16[256,2048]{1,0:T(8,128)(2,1)} %get-tuple-element.131), channel_id=1, source_target_pairs={{0,6},{1,7},{2,4},{3,5},{4,2},{5,3},{6,0},{7,1},{8,14},{9,15},{10,... | collective-permute-start | bytes 3145736 | tf_op jit(solution)/shard_map/ppermute | solution.py:741
  549.1 47.9 %collective-permute-start.59 = (bf16[256,2048]{1,0:T(8,128)(2,1)}, bf16[256,2048]{1,0:T(8,128)(2,1)}, u32[]{:S(2)}, u32[]{:S(2)}) collective-permute-start(bf16[256,2048]{1,0:T(8,128)(2,1)} %get-tuple-element.133), channel_id=1, source_target_pairs={{0,4},{1,5},{2,6},{3,7},{4,0},{5,1},{6,2},{7,3},{8,12},{9,13},{10,... | collective-permute-start | bytes 3145736 | tf_op jit(solution)/shard_map/ppermute | solution.py:741
  549.3 54.1 %collective-permute-start.10 = (bf16[320,2048]{1,0:T(8,128)(2,1)S(1)}, bf16[320,2048]{1,0:T(8,128)(2,1)S(1)}, u32[]{:S(2)}, u32[]{:S(2)}) collective-permute-start(bf16[320,2048]{1,0:T(8,128)(2,1)S(1)} %fusion.22), channel_id=1, source_target_pairs={{0,16},{8,24},{16,0},{24,8},{1,17},{9,25},{17,1},{25,9},{2,18},{10... | collective-permute-start | bytes 3932168 | tf_op jit(solution)/shard_map/ppermute | solution.py:773
  556.3 52.5 %collective-permute-start.11 = (bf16[320,2048]{1,0:T(8,128)(2,1)S(1)}, bf16[320,2048]{1,0:T(8,128)(2,1)S(1)}, u32[]{:S(2)}, u32[]{:S(2)}) collective-permute-start(bf16[320,2048]{1,0:T(8,128)(2,1)S(1)} %get-tuple-element.154), channel_id=1, source_target_pairs={{0,8},{8,0},{16,24},{24,16},{1,9},{9,1},{17,25},{25,17},{2,10},{10... | collective-permute-start | bytes 3932168 | tf_op jit(solution)/shard_map/ppermute | solution.py:773
  558.2 76.6 %collective-permute-start.52 = (bf16[256,2048]{1,0:T(8,128)(2,1)S(1)}, bf16[256,2048]{1,0:T(8,128)(2,1)}, u32[]{:S(2)}, u32[]{:S(2)}) collective-permute-start(bf16[256,2048]{1,0:T(8,128)(2,1)S(1)} %copy-done.14), channel_id=1, source_target_pairs={{0,1},{1,0},{2,3},{3,2},{4,5},{5,4},{6,7},{7,6},{8,9},{9,8},{10,11... | collective-permute-start | bytes 3145736 | tf_op jit(solution)/shard_map/ppermute | solution.py:741
  603.4 50.8 %collective-permute-start.51 = (bf16[256,2048]{1,0:T(8,128)(2,1)S(1)}, bf16[256,2048]{1,0:T(8,128)(2,1)}, u32[]{:S(2)}, u32[]{:S(2)}) collective-permute-start(bf16[256,2048]{1,0:T(8,128)(2,1)S(1)} %copy-done.16), channel_id=1, source_target_pairs={{0,2},{1,3},{2,0},{3,1},{4,6},{5,7},{6,4},{7,5},{8,10},{9,11},{10,... | collective-permute-start | bytes 3145736 | tf_op jit(solution)/shard_map/ppermute | solution.py:741
  608.9 81.8 %collective-permute-start.49 = (bf16[256,2048]{1,0:T(8,128)(2,1)S(1)}, bf16[256,2048]{1,0:T(8,128)(2,1)S(1)}, u32[]{:S(2)}, u32[]{:S(2)}) collective-permute-start(bf16[256,2048]{1,0:T(8,128)(2,1)S(1)} %copy-done.15), channel_id=1, source_target_pairs={{0,4},{1,5},{2,6},{3,7},{4,0},{5,1},{6,2},{7,3},{8,12},{9,13},{10,... | collective-permute-start | bytes 3145736 | tf_op jit(solution)/shard_map/ppermute | solution.py:741
  626.3 70.1 %collective-permute-start.64 = (bf16[256,2048]{1,0:T(8,128)(2,1)S(1)}, bf16[256,2048]{1,0:T(8,128)(2,1)S(1)}, u32[]{:S(2)}, u32[]{:S(2)}) collective-permute-start(bf16[256,2048]{1,0:T(8,128)(2,1)S(1)} %add_convert_fusion), channel_id=1, source_target_pairs={{0,16},{8,24},{16,0},{24,8},{1,17},{9,25},{17,1},{25,9},{2,18},{10... | collective-permute-start | bytes 3145736 | tf_op jit(solution)/shard_map/ppermute | solution.py:773
  634.9 63.4 %collective-permute-start.63 = (bf16[256,2048]{1,0:T(8,128)(2,1)S(1)}, bf16[256,2048]{1,0:T(8,128)(2,1)S(1)}, u32[]{:S(2)}, u32[]{:S(2)}) collective-permute-start(bf16[256,2048]{1,0:T(8,128)(2,1)S(1)} %add_convert_fusion), channel_id=1, source_target_pairs={{0,8},{8,0},{16,24},{24,16},{1,9},{9,1},{17,25},{25,17},{2,10},{10... | collective-permute-start | bytes 3145736 | tf_op jit(solution)/shard_map/ppermute | solution.py:773
  637.4 81.7 %collective-permute-start.15 = (bf16[320,2048]{1,0:T(8,128)(2,1)S(1)}, bf16[320,2048]{1,0:T(8,128)(2,1)S(1)}, u32[]{:S(2)}, u32[]{:S(2)}) collective-permute-start(bf16[320,2048]{1,0:T(8,128)(2,1)S(1)} %get-tuple-element.125), channel_id=1, source_target_pairs={{0,16},{8,24},{16,0},{24,8},{1,17},{9,25},{17,1},{25,9},{2,18},{10... | collective-permute-start | bytes 3932168 | tf_op jit(solution)/shard_map/ppermute | solution.py:773
  863.6 64.3 %collective-permute-start.28 = (bf16[256,1536]{0,1:T(8,128)(2,1)S(1)}, bf16[256,1536]{0,1:T(8,128)(2,1)S(1)}, u32[]{:S(2)}, u32[]{:S(2)}) collective-permute-start(bf16[256,1536]{0,1:T(8,128)(2,1)S(1)} %get-tuple-element.147), channel_id=1, source_target_pairs={{0,4},{1,5},{2,6},{3,7},{4,0},{5,1},{6,2},{7,3},{8,12},{9,13},{10,... | collective-permute-start | bytes 2359304 | tf_op jit(solution)/shard_map/ppermute | solution.py:741
  876.2 74.7 %collective-permute-start.17 = (bf16[320,2048]{1,0:T(8,128)(2,1)S(1)}, bf16[320,2048]{1,0:T(8,128)(2,1)S(1)}, u32[]{:S(2)}, u32[]{:S(2)}) collective-permute-start(bf16[320,2048]{1,0:T(8,128)(2,1)S(1)} %get-tuple-element.152), channel_id=1, source_target_pairs={{0,8},{8,0},{16,24},{24,16},{1,9},{9,1},{17,25},{25,17},{2,10},{10... | collective-permute-start | bytes 3932168 | tf_op jit(solution)/shard_map/ppermute | solution.py:773
  877.5 54.0 %collective-permute-start.43 = (bf16[64,2048]{1,0:T(8,128)(2,1)S(1)}, bf16[64,2048]{1,0:T(8,128)(2,1)S(1)}, u32[]{:S(2)}, u32[]{:S(2)}) collective-permute-start(bf16[64,2048]{1,0:T(8,128)(2,1)S(1)} %collective-permute-done.42), channel_id=1, source_target_pairs={{0,8},{8,0},{16,24},{24,16},{1,9},{9,1},{17,25},{25,17},{2,10},{10... | collective-permute-start | bytes 786440 | tf_op jit(solution)/shard_map/ppermute | solution.py:773
  882.3 49.2 %collective-permute-start.45 = (bf16[64,2048]{1,0:T(8,128)(2,1)S(1)}, bf16[64,2048]{1,0:T(8,128)(2,1)S(1)}, u32[]{:S(2)}, u32[]{:S(2)}) collective-permute-start(bf16[64,2048]{1,0:T(8,128)(2,1)S(1)} %collective-permute-done.44), channel_id=1, source_target_pairs={{0,8},{8,0},{16,24},{24,16},{1,9},{9,1},{17,25},{25,17},{2,10},{10... | collective-permute-start | bytes 786440 | tf_op jit(solution)/shard_map/ppermute | solution.py:773
  902.7 48.2 %collective-permute-start.19 = (bf16[320,2048]{1,0:T(8,128)(2,1)S(1)}, bf16[320,2048]{1,0:T(8,128)(2,1)S(1)}, u32[]{:S(2)}, u32[]{:S(2)}) collective-permute-start(bf16[320,2048]{1,0:T(8,128)(2,1)S(1)} %fusion.18), channel_id=1, source_target_pairs={{0,16},{8,24},{16,0},{24,8},{1,17},{9,25},{17,1},{25,9},{2,18},{10... | collective-permute-start | bytes 3932168 | tf_op jit(solution)/shard_map/ppermute | solution.py:773
  933.2 52.0 %collective-permute-start.32 = (bf16[256,1536]{0,1:T(8,128)(2,1)}, bf16[256,1536]{0,1:T(8,128)(2,1)}, u32[]{:S(2)}, u32[]{:S(2)}) collective-permute-start(bf16[256,1536]{0,1:T(8,128)(2,1)} %add_convert_fusion.8), channel_id=1, source_target_pairs={{0,8},{8,0},{16,24},{24,16},{1,9},{9,1},{17,25},{25,17},{2,10},{10... | collective-permute-start | bytes 2359304 | tf_op jit(solution)/shard_map/ppermute | solution.py:773
  (92 other events, 2407.3 us)

commit v3 on v2

--- a/solution.py
+++ b/solution.py
@@ -85,90 +85,6 @@
     if allowed is None:
         return scores
     return jnp.where(allowed, scores, NEG)
-
-
-def attend_back_pair(qkv_lanes, do, level_of, codes_q, codes_k, dq_all, dk_all, dv_all, qkv):
-    dk_all[...] = jnp.zeros_like(dk_all)
-    dv_all[...] = jnp.zeros_like(dv_all)
-    blocks = do.shape[0] // TILE
-    for block in range(blocks):
-        rows = slice(block * TILE, (block + 1) * TILE)
-        both_q = qkv[0][rows, qkv_lanes[0]]
-        both_do = do[rows, qkv_lanes[3]]
-        parts = []
-        for head in range(2):
-            queries = head_lanes(both_q, head)
-            grads = head_lanes(both_do, head)
-            level = level_of(rows, head)
-            probs = []
-            dprobs = []
-            for tile in range(block + 1):
-                cols = slice(tile * TILE, (tile + 1) * TILE)
-                scores = masked_scores(
-                    block, dot_nt(queries, qkv[1][cols, qkv_lanes[1]]), tile, codes_q, codes_k
-                )
-                probs.append(jnp.exp(scores - level))
-                dprobs.append(dot_nt(grads, qkv[2][cols, qkv_lanes[2]]))
-            delta = functools.reduce(
-                jnp.add, [jnp.sum(a * b, axis=1, keepdims=True) for a, b in zip(probs, dprobs)]
-            )
-            dq = None
-            for tile in range(block + 1):
-                cols = slice(tile * TILE, (tile + 1) * TILE)
-                ds = (probs[tile] * (dprobs[tile] - delta)).astype(BF)
-                part = dot_nn(ds, qkv[1][cols, qkv_lanes[1]])
-                dq = part if dq is None else dq + part
-                dk_all[cols, :] += dot_tn(ds, queries)
-                dv_all[cols, :] += dot_tn(probs[tile].astype(BF), grads)
-            parts.append(dq)
-        dq_all[rows, :] = join_heads(*parts) * (1.0 / math.sqrt(HEAD_DIM))
-
-
-def attend_back_kernel(q_ref, k_ref, v_ref, do_ref, stat_ref, cq_ref, ck_ref, dq_ref, dk_ref, dv_ref, dq, dk, dv):
-    every = slice(None)
-    attend_back_pair(
-        [every] * 4,
-        do_ref,
-        lambda rows, head: stat_ref[rows, head * HEAD_DIM : head * HEAD_DIM + 1],
-        cq_ref[...],
-        ck_ref[...],
-        dq,
-        dk,
-        dv,
-        (q_ref, k_ref, v_ref),
-    )
-    dq_ref[...] = dq[...].astype(BF)
-    dk_ref[...] = dk[...].astype(BF)
-    dv_ref[...] = dv[...].astype(BF)
-
-
-def attend_back(qkv, grad_out, stats, codes_q, codes_k):
-    length, width = qkv.shape
-    pairs = width // 3 // 128
-    block = (length, 128)
-    return pl.pallas_call(
-        attend_back_kernel,
-        out_shape=[jax.ShapeDtypeStruct((length, width // 3), BF)] * 3,
-        grid=(pairs,),
-        in_specs=[
-            pl.BlockSpec(block, lambda i: (0, i)),
-            pl.BlockSpec(block, lambda i: (0, pairs + i)),
-            pl.BlockSpec(block, lambda i: (0, 2 * pairs + i)),
-            pl.BlockSpec(block, lambda i: (0, i)),
-            pl.BlockSpec(block, lambda i: (0, i)),
-            pl.BlockSpec((length, 1), lambda i: (0, 0)),
-            pl.BlockSpec((1, length), lambda i: (0, 0)),
-        ],
-        out_specs=[pl.BlockSpec(block, lambda i: (0, i))] * 3,
-        scratch_shapes=[pltpu.VMEM((length, 128), F32)] * 3,
-        compiler_params=pltpu.CompilerParams(vmem_limit_bytes=56 * 2**20),
-        cost_estimate=pl.CostEstimate(
-            flops=pairs * 2 * 15 * 10 * TILE * TILE * 256,
-            bytes_accessed=length * width * 6,
-            transcendentals=pairs * 2 * 15 * TILE * TILE,
-        ),
-        name="attend_back",
-    )(qkv, qkv, qkv, grad_out, stats, codes_q, codes_k)
 
 
 def xor(value, mask):
@@ -732,6 +648,877 @@
     )(*operands)
 
 
+class Pool:
+    def __init__(self, buffers, count):
+        self.buffers, self.count = buffers, count
+        self.pending = [None] * count
+        self.turn = 0
+
+    def take(self):
+        index = self.turn % self.count
+        self.turn += 1
+        if self.pending[index] is not None:
+            self.pending[index].wait_send()
+            self.pending[index] = None
+        return index
+
+    def drain(self):
+        for copy in self.pending:
+            if copy is not None:
+                copy.wait_send()
+
+
+class Reduce:
+    def __init__(self, grad, near, wide_land, rows, width, sems, work):
+        self.grad, self.near, self.wide_land = grad, near, wide_land
+        self.rows, self.width = rows, width
+        self.near_send, self.near_recv, self.wide_send, self.wide_recv = sems
+        self.left, self.right, self.total, self.out, self.pool, self.sem = work
+        self.seq = lax.axis_index("seq")
+        self.sent = []
+
+    def block(self, mask):
+        return self.grad.at[rows_of(xor(self.seq, mask), self.rows), :]
+
+    def near_slot(self, mask):
+        return self.near.at[mask // 2 * self.rows : (mask // 2 + 1) * self.rows, :]
+
+    def wide_slot(self, mask):
+        return self.wide_land.at[mask // 2 * self.rows : (mask // 2 + 1) * self.rows, :]
+
+    def near_copy(self, mask):
+        return remote(
+            self.block(mask + 1),
+            self.near_slot(mask),
+            self.near_send.at[mask // 2],
+            self.near_recv.at[mask // 2],
+            seq=xor(self.seq, 1),
+        )
+
+    def wide_copy(self, src, mask):
+        return remote(
+            src,
+            self.wide_slot(mask),
+            self.wide_send.at[mask // 2],
+            self.wide_recv.at[mask // 2],
+            seq=xor(self.seq, mask),
+        )
+
+    def begin(self, *masks):
+        for mask in masks:
+            copy = self.near_copy(mask)
+            copy.start()
+            self.sent.append(copy)
+
+    def views(self, index=None):
+        left = self.left.at[: self.rows, : self.width]
+        right = self.right.at[: self.rows, : self.width]
+        return left, right
+
+    def step(self, mask):
+        left, right = self.views()
+        own = pltpu.make_async_copy(self.block(mask), left, self.sem.at[0])
+        own.start()
+        self.near_copy(mask).wait_recv()
+        other = pltpu.make_async_copy(self.near_slot(mask), right, self.sem.at[1])
+        other.start()
+        index = self.pool.take()
+        own.wait()
+        other.wait()
+        chunk = min(32, self.rows)
+
+        @pl.loop(0, self.rows // chunk)
+        def _(i):
+            at = (rows_of(i, chunk), slice(0, self.width))
+            value = self.left[at].astype(F32) + self.right[at].astype(F32)
+            self.out[index, at[0], at[1]] = value.astype(BF)
+
+        copy = self.wide_copy(self.out.at[index, : self.rows, : self.width], mask)
+        copy.start()
+        self.pool.pending[index] = copy
+
+    def settle(self, wide):
+        self.near_copy(0).wait_recv()
+        for mask in wide:
+            self.wide_copy(self.out.at[0, : self.rows, : self.width], mask).wait_recv()
+
+    def final(self, wide, result):
+        left, right = self.views()
+        chunk = min(32, self.rows)
+        local_copies([(self.block(0), left), (self.near_slot(0), right)], self.sem)
+        masks = list(wide)
+
+        @pl.loop(0, self.rows // chunk)
+        def _(i):
+            at = (rows_of(i, chunk), slice(0, self.width))
+            self.total[at] = self.left[at].astype(F32) + self.right[at].astype(F32)
+
+        while masks:
+            now, masks = masks[:2], masks[2:]
+            views = [(self.wide_slot(mask), view) for mask, view in zip(now, (left, right))]
+            local_copies(views, self.sem)
+            refs = (self.left, self.right)[: len(now)]
+            last = not masks
+
+            @pl.loop(0, self.rows // chunk)
+            def _(i):
+                at = (rows_of(i, chunk), slice(0, self.width))
+                value = self.total[at]
+                for ref in refs:
+                    value = value + ref[at].astype(F32)
+                if last:
+                    result[at] = value.astype(BF)
+                else:
+                    self.total[at] = value
+
+    def drain(self):
+        for copy in self.sent:
+            copy.wait_send()
+
+
+class Sum:
+    def __init__(self, terms, near, passed, far, send_sem, recv_sem):
+        pre = lax.axis_index("pre")
+        near_id, far_id = {"pre": xor(pre, 1)}, {"pre": xor(pre, 2)}
+        self.terms, self.near, self.passed = terms, near, passed
+        self.near_copies = [
+            remote(terms.at[i], near.at[i], send_sem.at[i], recv_sem.at[i], **near_id)
+            for i in range(2)
+        ]
+        self.far_copy = remote(passed, far, send_sem.at[2], recv_sem.at[2], **far_id)
+
+    def run(self, term, keep):
+        def store_in(slot):
+            def store(rows, lanes, value):
+                self.terms[slot, rows, lanes] = value.astype(BF)
+
+            return store
+
+        term(3, store_in(0))
+        self.near_copies[0].start()
+        term(1, store_in(1))
+        self.near_copies[1].start()
+        self.near_copies[0].wait_recv()
+
+        def store(rows, lanes, value):
+            self.passed[rows, lanes] = (value + self.near[0, rows, lanes].astype(F32)).astype(BF)
+
+        term(2, store)
+        self.far_copy.start()
+        self.near_copies[1].wait_recv()
+
+        def store(rows, lanes, value):
+            keep(rows, lanes, value + self.near[1, rows, lanes].astype(F32))
+
+        term(0, store)
+
+    def drain(self):
+        for copy in (*self.near_copies, self.far_copy):
+            copy.wait_send()
+
+
+def columns_grad(left, right, rows, width, tile, save):
+    @pl.loop(0, rows // 256)
+    def _(i):
+        turned = left[:, rows_of(i, 256)].T
+
+        @pl.loop(0, width // 512)
+        def _(j):
+            tile[:, rows_of(j, 512)] = dot_nn(turned, right[:, rows_of(j, 512)]).astype(BF)
+
+        copy = save(rows_of(i, 256))
+        copy.start()
+        copy.wait()
+
+
+def add_rows(target, index, value):
+    target[index : index + 1, : value.shape[1]] += jnp.sum(value, axis=0, keepdims=True)
+
+
+def feed_back_kernel(
+    sizes,
+    w_down,
+    w_up,
+    df,
+    h2,
+    slope,
+    attn,
+    down_grad,
+    prefix_in,
+    later_in,
+    prefix_cot,
+    later_cot,
+    active_ref,
+    gain2,
+    near_down,
+    wide_down,
+    up_grad,
+    dattn,
+    middle_grad,
+    sums,
+    up_sums,
+    wbuf,
+    lhs,
+    slope_v,
+    du_v,
+    x_v,
+    cot_v,
+    attn_v,
+    acc_v,
+    dattn_v,
+    terms_v,
+    near_v,
+    pass_v,
+    far_v,
+    left_v,
+    right_v,
+    total_v,
+    out_v,
+    grad_v,
+    twin_send,
+    twin_recv,
+    wide_send,
+    wide_recv,
+    spread_send,
+    spread_recv,
+    sum_send,
+    sum_recv,
+    local_sem,
+):
+    seq_size, pre_part, later_part = sizes
+    part = pre_part + later_part
+    length = 4 * part
+    ff_cols = w_up.shape[1]
+    wide = wide_masks(seq_size)
+    late = sorted(wide, key=lambda m: (m == 2, m))
+    pool = Pool(out_v, 3)
+    work = (left_v, right_v, total_v, out_v, pool, local_sem.at[0:2])
+    put_down = Reduce(
+        down_grad,
+        near_down,
+        wide_down,
+        D // seq_size,
+        ff_cols,
+        (twin_send, twin_recv, wide_send, wide_recv),
+        work,
+    )
+    get_dattn = Spread(dattn_v, dattn, part, spread_send, spread_recv, local_sem.at[2])
+    sum_dh2 = Sum(terms_v, near_v, pass_v, far_v, sum_send, sum_recv)
+
+    greet(wide)
+    put_down.begin(*late, 0)
+    loads = [
+        pltpu.make_async_copy(src, dst, local_sem.at[3 + i])
+        for i, (src, dst) in enumerate(
+            [
+                (w_down, wbuf),
+                (df, lhs),
+                (slope, slope_v),
+                (prefix_in, x_v.at[:pre_part, :]),
+                (later_in, x_v.at[pre_part:, :]),
+                (prefix_cot, cot_v.at[:pre_part, :]),
+                (later_cot, cot_v.at[pre_part:, :]),
+                (attn, attn_v),
+            ]
+        )
+    ]
+    for load in loads:
+        load.start()
+    for load in loads:
+        load.wait()
+
+    @pl.loop(0, 4)
+    def _(r):
+        rows = rows_of(r, part)
+
+        @pl.loop(0, ff_cols // 512)
+        def _(j):
+            lanes = rows_of(j, 512)
+            value = dot_nn(lhs[rows, :], wbuf[:, lanes])
+            du_v[rows, lanes] = (value * slope_v[rows, lanes].astype(F32)).astype(BF)
+
+    load = pltpu.make_async_copy(w_up, wbuf, local_sem.at[3])
+    load.start()
+    load_h2 = pltpu.make_async_copy(h2, lhs, local_sem.at[4])
+    load_h2.start()
+    put_down.step(late[0])
+    load.wait()
+
+    def dh2_term(r, store):
+        @pl.loop(0, D // 512)
+        def _(j):
+            store(
+                slice(0, part),
+                rows_of(j, 512),
+                dot_nt(du_v[r * part : (r + 1) * part, :], wbuf[rows_of(j, 512), :]),
+            )
+
+    def keep_dh2(rows, lanes, value):
+        acc_v[rows, lanes] = value
+
+    sum_dh2.run(dh2_term, keep_dh2)
+    for mask in late[1:-1]:
+        put_down.step(mask)
+    load_h2.wait()
+    columns_grad(
+        lhs,
+        du_v,
+        D,
+        ff_cols,
+        grad_v,
+        lambda rows: pltpu.make_async_copy(grad_v, up_grad.at[rows, :], local_sem.at[3]),
+    )
+    sums[...] = jnp.zeros_like(sums)
+    up_sums[...] = jnp.zeros_like(up_sums)
+    if len(late) > 1:
+        put_down.step(late[-1])
+    sum_dh2.far_copy.wait_recv()
+    chunk = 32
+
+    @pl.loop(0, part // chunk)
+    def _(i):
+        rows = rows_of(i, chunk)
+        grad = acc_v[rows, :] + far_v[rows, :].astype(F32)
+        middle = x_v[rows, :].astype(F32) + attn_v[rows, :]
+        _, normed, scaling = layer_norm_parts(middle, gain2[...], 0.0)
+        back = norm_back(grad, normed, scaling, gain2[...])
+        acc_v[rows, :] = back
+        direct = active_ref[rows, :] * cot_v[rows, :].astype(F32)
+        value = (direct + back).astype(BF)
+        dattn_v[rows, :] = value
+        add_rows(sums, 0, value.astype(F32))
+        add_rows(sums, 1, grad * normed)
+        add_rows(sums, 2, grad)
+        add_rows(sums, 3, direct)
+
+    get_dattn.begin()
+    save = pltpu.make_async_copy(acc_v, middle_grad, local_sem.at[3])
+    save.start()
+
+    @pl.loop(0, length // chunk)
+    def _(i):
+        add_rows(up_sums, 0, du_v[rows_of(i, chunk), :].astype(F32))
+
+    get_dattn.forward()
+    put_down.settle(wide)
+    get_dattn.finish()
+    save.wait()
+    for item in (put_down, get_dattn, sum_dh2, pool):
+        item.drain()
+
+
+def feed_back(seq_size, pre_part, later_part, *operands):
+    part = pre_part + later_part
+    length = 4 * part
+    w_up = operands[1]
+    ff_cols = w_up.shape[1]
+    own_d = D // seq_size
+    hbm = pl.BlockSpec(memory_space=pl.ANY)
+    vmem = pl.BlockSpec(memory_space=pltpu.VMEM)
+
+    def out(shape, kind=BF):
+        return jax.ShapeDtypeStruct(shape, kind)
+
+    half = seq_size // 2
+    outs = (
+        out((half * own_d, ff_cols)),
+        out((half * own_d, ff_cols)),
+        out((D, ff_cols)),
+        out((length, D)),
+        out((part, D), F32),
+        out((8, D), F32),
+        out((8, ff_cols), F32),
+    )
+    dma = pltpu.SemaphoreType.DMA
+    return pl.pallas_call(
+        functools.partial(feed_back_kernel, (seq_size, pre_part, later_part)),
+        out_shape=outs,
+        in_specs=[hbm] * 11 + [vmem] * (len(operands) - 11),
+        out_specs=[hbm] * 5 + [vmem] * 2,
+        scratch_shapes=[
+            pltpu.VMEM((D, ff_cols), BF),
+            pltpu.VMEM((length, D), BF),
+            pltpu.VMEM((length, ff_cols), BF),
+            pltpu.VMEM((length, ff_cols), BF),
+            pltpu.VMEM((part, D), BF),
+            pltpu.VMEM((part, D), BF),
+            pltpu.VMEM((part, D), F32),
+            pltpu.VMEM((part, D), F32),
+            pltpu.VMEM((part, D), BF),
+            pltpu.VMEM((2, part, D), BF),
+            pltpu.VMEM((2, part, D), BF),
+            pltpu.VMEM((part, D), BF),
+            pltpu.VMEM((part, D), BF),
+            pltpu.VMEM((own_d, ff_cols), BF),
+            pltpu.VMEM((own_d, ff_cols), BF),
+            pltpu.VMEM((own_d, ff_cols), F32),
+            pltpu.VMEM((3, own_d, ff_cols), BF),
+            pltpu.VMEM((256, ff_cols), BF),
+            dma((half,)),
+            dma((half,)),
+            dma((half,)),
+            dma((half,)),
+            dma((4,)),
+            dma((4,)),
+            dma((3,)),
+            dma((3,)),
+            dma((12,)),
+        ],
+        compiler_params=pltpu.CompilerParams(
+            collective_id=1, has_side_effects=True, vmem_limit_bytes=62 * 2**20
+        ),
+        cost_estimate=pl.CostEstimate(
+            flops=2 * length * D * 3 * ff_cols,
+            bytes_accessed=8 * D * ff_cols,
+            transcendentals=length,
+        ),
+        name="feed_back",
+    )(*operands)
+
+
+def attend_back_pair(pair, cols, qkv, do, stats, codes_q, codes_k, dq_all, dk_all, dv_all, dqkv):
+    lanes = [pl.ds(pl.multiple_of(third * cols + pair * 128, 128), 128) for third in range(3)]
+    dk_all[...] = jnp.zeros_like(dk_all)
+    dv_all[...] = jnp.zeros_like(dv_all)
+    blocks = qkv.shape[0] // TILE
+    for block in range(blocks):
+        rows = slice(block * TILE, (block + 1) * TILE)
+        both_q = qkv[rows, lanes[0]]
+        both_do = do[rows, lanes_of(pair)]
+        both_levels = stats[rows, lanes_of(pair)]
+        parts = []
+        for head in range(2):
+            queries = head_lanes(both_q, head)
+            grads = head_lanes(both_do, head)
+            level = both_levels[:, head * HEAD_DIM : head * HEAD_DIM + 1]
+            probs = []
+            dprobs = []
+            for tile in range(block + 1):
+                keys = slice(tile * TILE, (tile + 1) * TILE)
+                scores = masked_scores(
+                    block, dot_nt(queries, qkv[keys, lanes[1]]), tile, codes_q, codes_k
+                )
+                probs.append(jnp.exp(scores - level))
+                dprobs.append(dot_nt(grads, qkv[keys, lanes[2]]))
+            delta = functools.reduce(
+                jnp.add, [jnp.sum(a * b, axis=1, keepdims=True) for a, b in zip(probs, dprobs)]
+            )
+            dq = None
+            for tile in range(block + 1):
+                keys = slice(tile * TILE, (tile + 1) * TILE)
+                ds = (probs[tile] * (dprobs[tile] - delta)).astype(BF)
+                part = dot_nn(ds, qkv[keys, lanes[1]])
+                dq = part if dq is None else dq + part
+                dk_all[keys, :] += dot_tn(ds, queries)
+                dv_all[keys, :] += dot_tn(probs[tile].astype(BF), grads)
+            parts.append(dq)
+        dq_all[rows, :] = join_heads(*parts) * (1.0 / math.sqrt(HEAD_DIM))
+    for lane, source in zip(lanes, (dq_all, dk_all, dv_all)):
+        dqkv[:, lane] = source[...].astype(BF)
+
+
+def attend_back_kernel(
+    sizes,
+    w_qkv,
+    w_out,
+    w_down,
+    h1,
+    qkv,
+    stats,
+    mixed,
+    acted,
+    dattn,
+    middle_grad,
+    attn,
+    up_grad,
+    down_grad,
+    near_down,
+    wide_down,
+    prefix_in,
+    later_in,
+    prefix_cot,
+    later_cot,
+    active_ref,
+    gain1,
+    down_bias,
+    codes_q,
+    codes_k,
+    fin_down,
+    fin_up,
+    fin_qkv,
+    fin_out,
+    near_up,
+    wide_up,
+    near_out,
+    wide_out,
+    near_qkv,
+    wide_qkv,
+    out_grad,
+    qkv_grad,
+    prefix_out,
+    later_out,
+    prefix_grad,
+    later_grad,
+    sums,
+    qkv_sums,
+    wbuf,
+    lhs,
+    qkv_v,
+    stats_v,
+    do_v,
+    mixed_v,
+    dqkv_v,
+    dq_v,
+    dk_v,
+    dv_v,
+    x_v,
+    cot_v,
+    attn_v,
+    middle_v,
+    acc_v,
+    terms_v,
+    near_v,
+    pass_v,
+    far_v,
+    left_v,
+    right_v,
+    total_v,
+    out_v,
+    grad_v,
+    res_down,
+    res_up,
+    res_qkv,
+    res_out,
+    twin_send,
+    twin_recv,
+    wide_send,
+    wide_recv,
+    spread_send,
+    spread_recv,
+    sum_send,
+    sum_recv,
+    local_sem,
+):
+    seq_size, pre_part, later_part = sizes
+    part = pre_part + later_part
+    length = 4 * part
+    width = w_qkv.shape[1]
+    cols = width // 3
+    ff_cols = w_down.shape[1]
+    own_d = D // seq_size
+    own_o = cols // seq_size
+    pre = lax.axis_index("pre")
+    wide = wide_masks(seq_size)
+    late = sorted(wide, key=lambda m: (m == 2, m))
+    pool = Pool(out_v, 3)
+    work = (left_v, right_v, total_v, out_v, pool, local_sem.at[0:2])
+
+    def reduce_of(i, grad, near, wide_land, rows, columns):
+        sems = (twin_send.at[i], twin_recv.at[i], wide_send.at[i], wide_recv.at[i])
+        return Reduce(grad, near, wide_land, rows, columns, sems, work)
+
+    put_down = reduce_of(0, down_grad, near_down, wide_down, own_d, ff_cols)
+    put_up = reduce_of(0, up_grad, near_up, wide_up, own_d, ff_cols)
+    put_out = reduce_of(1, out_grad, near_out, wide_out, own_o, D)
+    put_qkv = reduce_of(2, qkv_grad, near_qkv, wide_qkv, own_d, width)
+
+    def spread_of(i, own, land):
+        return Spread(own, land, own_d, spread_send.at[i], spread_recv.at[i], local_sem.at[2 + i])
+
+    get_down = spread_of(0, res_down, fin_down)
+    get_up = spread_of(1, res_up, fin_up)
+    get_qkv = spread_of(2, res_qkv, fin_qkv)
+    sum_f = Sum(terms_v, near_v, pass_v, far_v, sum_send.at[0], sum_recv.at[0])
+    sum_dh1 = Sum(terms_v, near_v, pass_v, far_v, sum_send.at[1], sum_recv.at[1])
+    chunk = 32
+
+    greet(wide)
+    put_up.begin(*late, 0)
+
+    def load_all(first, *pairs):
+        copies = [
+            pltpu.make_async_copy(src, dst, local_sem.at[first + i])
+            for i, (src, dst) in enumerate(pairs)
+        ]
+        for copy in copies:
+            copy.start()
+        return copies
+
+    def wait_all(copies):
+        for copy in copies:
+            copy.wait()
+
+    loads = load_all(5, (w_down, wbuf), (acted, lhs))
+    more = load_all(
+        8,
+        (prefix_in, x_v.at[:pre_part, :]),
+        (later_in, x_v.at[pre_part:, :]),
+        (prefix_cot, cot_v.at[:pre_part, :]),
+        (later_cot, cot_v.at[pre_part:, :]),
+        (attn, attn_v),
+        (middle_grad, middle_v),
+        (qkv, qkv_v),
+        (stats, stats_v),
+        (mixed, mixed_v),
+    )
+    sums[...] = jnp.zeros_like(sums)
+    qkv_sums[...] = jnp.zeros_like(qkv_sums)
+    wait_all(loads)
+
+    def f_term(r, store):
+        @pl.loop(0, D // 512)
+        def _(j):
+            store(
+                slice(0, part),
+                rows_of(j, 512),
+                dot_nt(lhs[r * part : (r + 1) * part, :], wbuf[rows_of(j, 512), :]),
+            )
+
+    def keep(rows, lanes, value):
+        acc_v[rows, lanes] = value
+
+    sum_f.run(f_term, keep)
+    loads = load_all(5, (w_out, wbuf.at[:cols, :]), (dattn, lhs))
+    wait_all(more)
+    put_up.step(late[0])
+    wait_all(loads)
+
+    def position_rows(r):
+        member = lax.rem(r, 2) * (xor(pre, 1) - pre) + lax.div(r, 2) * (xor(pre, 2) - pre) + pre
+        return (
+            rows_of(member, pre_part),
+            pl.ds(pl.multiple_of(4 * pre_part + member * later_part, 64), later_part),
+        )
+
+    @pl.loop(0, 4)
+    def _(r):
+        head_rows, tail_rows = position_rows(r)
+        value = dot_nt(lhs[rows_of(r, part), :], wbuf[:cols, :]).astype(BF)
+        do_v[head_rows, :] = value[:pre_part]
+        do_v[tail_rows, :] = value[pre_part:]
+
+    columns_grad(
+        mixed_v,
+        lhs,
+        cols,
+        D,
+        grad_v,
+        lambda rows: pltpu.make_async_copy(grad_v.at[:, :D], out_grad.at[rows, :], local_sem.at[5]),
+    )
+    put_out.begin(*late, 0)
+    loads = load_all(5, (w_qkv, wbuf.at[:, :width]))
+    for r in range(4):
+        head_rows, tail_rows = position_rows(jnp.int32(r))
+        loads += load_all(
+            8 + 2 * r,
+            (h1.at[r * part : r * part + pre_part, :], lhs.at[head_rows, :]),
+            (h1.at[r * part + pre_part : (r + 1) * part, :], lhs.at[tail_rows, :]),
+        )
+    pairs = cols // 128
+
+    def attention(first, last):
+        @pl.loop(first, last)
+        def _(pair):
+            attend_back_pair(
+                pair,
+                cols,
+                qkv_v,
+                do_v,
+                stats_v,
+                codes_q[...],
+                codes_k[...],
+                dq_v,
+                dk_v,
+                dv_v,
+                dqkv_v,
+            )
+
+    attention(0, pairs // 2)
+    for mask in late[1:-1]:
+        put_up.step(mask)
+    sum_f.far_copy.wait_recv()
+    sum_f.drain()
+
+    @pl.loop(0, part // chunk)
+    def _(i):
+        rows = rows_of(i, chunk)
+        live = active_ref[rows, :]
+        ffn = acc_v[rows, :] + far_v[rows, :].astype(F32) + down_bias[...]
+        branch = attn_v[rows, :]
+        result = x_v[rows, :].astype(F32) + live * (branch + ffn)
+        add_rows(sums, 2, live * result * result)
+        add_rows(sums, 3, live * branch * branch)
+        add_rows(sums, 4, live * ffn * ffn)
+        pass_v[rows, :] = result.astype(BF)
+
+    put_down.final(wide, res_down)
+    get_down.begin()
+    attention(pairs // 2, pairs)
+    get_down.forward()
+    wait_all(loads)
+    columns_grad(
+        lhs,
+        dqkv_v,
+        D,
+        width,
+        grad_v,
+        lambda rows: pltpu.make_async_copy(
+            grad_v.at[:, :width], qkv_grad.at[rows, :], local_sem.at[5]
+        ),
+    )
+    put_qkv.begin(*late, 0)
+    put_up.step(late[-1])
+    get_down.finish()
+    saves = load_all(6, (pass_v.at[:pre_part, :], prefix_out), (pass_v.at[pre_part:, :], later_out))
+    wait_all(saves)
+
+    def dh1_term(r, store):
+        head_rows, tail_rows = position_rows(jnp.int32(r))
+
+        @pl.loop(0, D // 512)
+        def _(j):
+            weights = wbuf[rows_of(j, 512), :width]
+            store(slice(0, pre_part), rows_of(j, 512), dot_nt(dqkv_v[head_rows, :], weights))
+            store(slice(pre_part, part), rows_of(j, 512), dot_nt(dqkv_v[tail_rows, :], weights))
+
+    sum_dh1.run(dh1_term, keep)
+
+    @pl.loop(0, length // chunk)
+    def _(i):
+        add_rows(qkv_sums, 0, dqkv_v[rows_of(i, chunk), :].astype(F32))
+
+    for mask in late:
+        put_out.step(mask)
+    sum_dh1.far_copy.wait_recv()
+
+    @pl.loop(0, part // chunk)
+    def _(i):
+        rows = rows_of(i, chunk)
+        grad = acc_v[rows, :] + far_v[rows, :].astype(F32)
+        _, normed, scaling = layer_norm_parts(x_v[rows, :].astype(F32), gain1[...], 0.0)
+        back = norm_back(grad, normed, scaling, gain1[...])
+        add_rows(sums, 0, grad * normed)
+        add_rows(sums, 1, grad)
+        value = cot_v[rows, :].astype(F32) + middle_v[rows, :] + back
+        terms_rows = value.astype(BF)
+        x_v[rows, :] = terms_rows
+
+    saves = load_all(6, (x_v.at[:pre_part, :], prefix_grad), (x_v.at[pre_part:, :], later_grad))
+    put_up.settle(wide)
+    put_up.final(wide, res_up)
+    get_up.begin()
+    put_qkv.step(late[0])
+    put_out.settle(wide)
+    put_out.final(wide, res_out)
+    wait_all(saves)
+    saves = load_all(6, (res_out, fin_out))
+    for mask in late[1:]:
+        put_qkv.step(mask)
+    get_up.forward()
+    put_qkv.settle(wide)
+    put_qkv.final(wide, res_qkv)
+    get_qkv.begin()
+    get_up.finish()
+    get_qkv.forward()
+    get_qkv.finish()
+    wait_all(saves)
+    for item in (put_up, put_out, put_qkv, get_down, get_up, get_qkv, sum_dh1, pool):
+        item.drain()
+
+
+def attend_back(seq_size, pre_part, later_part, *operands):
+    part = pre_part + later_part
+    length = 4 * part
+    width = operands[0].shape[1]
+    cols = width // 3
+    ff_cols = operands[2].shape[1]
+    own_d = D // seq_size
+    own_o = cols // seq_size
+    half = seq_size // 2
+    hbm = pl.BlockSpec(memory_space=pl.ANY)
+    vmem = pl.BlockSpec(memory_space=pltpu.VMEM)
+
+    def out(shape, kind=BF):
+        return jax.ShapeDtypeStruct(shape, kind)
+
+    outs = (
+        out((4 * own_d, ff_cols)),
+        out((4 * own_d, ff_cols)),
+        out((4 * own_d, width)),
+        out((own_o, D)),
+        out((half * own_d, ff_cols)),
+        out((half * own_d, ff_cols)),
+        out((half * own_o, D)),
+        out((half * own_o, D)),
+        out((half * own_d, width)),
+        out((half * own_d, width)),
+        out((cols, D)),
+        out((D, width)),
+        out((pre_part, D)),
+        out((later_part, D)),
+        out((pre_part, D)),
+        out((later_part, D)),
+        out((8, D), F32),
+        out((8, width), F32),
+    )
+    most = max(ff_cols, D, width)
+    dma = pltpu.SemaphoreType.DMA
+    return pl.pallas_call(
+        functools.partial(attend_back_kernel, (seq_size, pre_part, later_part)),
+        out_shape=outs,
+        in_specs=[hbm] * 19 + [vmem] * (len(operands) - 19),
+        out_specs=[hbm] * 16 + [vmem] * 2,
+        scratch_shapes=[
+            pltpu.VMEM((D, most), BF),
+            pltpu.VMEM((length, D), BF),
+            pltpu.VMEM((length, width), BF),
+            pltpu.VMEM((length, cols), F32),
+            pltpu.VMEM((length, cols), BF),
+            pltpu.VMEM((length, cols), BF),
+            pltpu.VMEM((length, width), BF),
+            pltpu.VMEM((length, 128), F32),
+            pltpu.VMEM((length, 128), F32),
+            pltpu.VMEM((length, 128), F32),
+            pltpu.VMEM((part, D), BF),
+            pltpu.VMEM((part, D), BF),
+            pltpu.VMEM((part, D), F32),
+            pltpu.VMEM((part, D), F32),
+            pltpu.VMEM((part, D), F32),
+            pltpu.VMEM((2, part, D), BF),
+            pltpu.VMEM((2, part, D), BF),
+            pltpu.VMEM((part, D), BF),
+            pltpu.VMEM((part, D), BF),
+            pltpu.VMEM((own_d, most), BF),
+            pltpu.VMEM((own_d, most), BF),
+            pltpu.VMEM((own_d, most), F32),
+            pltpu.VMEM((3, own_d, most), BF),
+            pltpu.VMEM((256, most), BF),
+            pltpu.VMEM((own_d, ff_cols), BF),
+            pltpu.VMEM((own_d, ff_cols), BF),
+            pltpu.VMEM((own_d, width), BF),
+            pltpu.VMEM((own_o, D), BF),
+            dma((3, half)),
+            dma((3, half)),
+            dma((3, half)),
+            dma((3, half)),
+            dma((3, 4)),
+            dma((3, 4)),
+            dma((2, 3)),
+            dma((2, 3)),
+            dma((20,)),
+        ],
+        compiler_params=pltpu.CompilerParams(
+            collective_id=2, has_side_effects=True, vmem_limit_bytes=63 * 2**20
+        ),
+        cost_estimate=pl.CostEstimate(
+            flops=2 * length * D * (2 * width + ff_cols),
+            bytes_accessed=8 * D * ff_cols,
+            transcendentals=length * length,
+        ),
+        name="attend_back",
+    )(*operands)
+
+
 class Seq:
     def __init__(self):
         self.size = lax.axis_size("seq")
@@ -746,17 +1533,6 @@
             blocks.append(self.swap(own, mask))
             blocks.append(self.swap(blocks[-1], 1))
         return blocks
-
-    def reduce(self, blocks):
-        total = None
-        masks = [mask for mask in range(2, self.size, 2)][::-1] + [0]
-        for mask in masks:
-            other = self.swap(blocks[mask + 1], 1)
-            part = blocks[mask].astype(F32) + other.astype(F32)
-            if mask:
-                part = self.swap(part.astype(BF), mask).astype(F32)
-            total = part if total is None else total + part
-        return total
 
     def reorder(self, value, axis):
         block = value.shape[axis] // self.size
@@ -777,12 +1553,6 @@
     far = over_pre(own, 2)
     near = over_pre(own, 1)
     return [own, near, far, over_pre(far, 1)]
-
-
-def scatter_pre(blocks):
-    a = blocks[0] + over_pre(blocks[1].astype(BF), 1).astype(F32)
-    b = blocks[2] + over_pre(blocks[3].astype(BF), 1).astype(F32)
-    return a + over_pre(b.astype(BF), 2).astype(F32)
 
 
 def sum_all(value):
@@ -909,86 +1679,56 @@
         codes_k,
     )
 
-    tokens = jnp.concatenate([prefix_in[0], later_in[0]], axis=0).astype(F32)
-    cotangent = jnp.concatenate([prefix_cot[0], later_cot[0]], axis=0).astype(F32)
-    ffn_grad = (active * cotangent).astype(BF)
-    _, first_normed, first_scaling = layer_norm_parts(tokens, gain1, bias1)
-    _, second_normed, second_scaling = layer_norm_parts(tokens + attn, gain2, bias2)
-    ffn_terms = lax.dot_general(
-        acted, w_down, (((1,), (1,)), ((), ())), preferred_element_type=F32
-    )
-    ffn = scatter_pre([ffn_terms[i * part : (i + 1) * part] for i in range(parts)]) + db
-    result = tokens + active * (attn + ffn)
-    square_sums = jnp.stack(
-        [
-            jnp.sum(active * result * result),
-            jnp.sum(active * attn * attn),
-            jnp.sum(active * ffn * ffn),
-            jnp.sum(active),
-        ]
-    )
-
-    acted_grad = jnp.dot(df, w_down, preferred_element_type=F32)
-    upper_grad = (acted_grad * slope.astype(F32)).astype(BF)
-    second_terms = lax.dot_general(
-        upper_grad, w_up, (((1,), (1,)), ((), ())), preferred_element_type=F32
-    )
-    up_grad = lax.dot_general(h2, upper_grad, (((0,), (0,)), ((), ())), preferred_element_type=F32)
-    up_grad = up_grad.astype(BF)
-    second_grad = scatter_pre([second_terms[i * part : (i + 1) * part] for i in range(parts)])
-    middle_grad = norm_back(second_grad, second_normed, second_scaling, gain2)
-    attn_grad = (active * cotangent + middle_grad).astype(BF)
-
-    dattn = jnp.concatenate(gather_pre(attn_grad), axis=0)
-    mixed_grad = lax.dot_general(
-        dattn, w_out, (((1,), (1,)), ((), ())), preferred_element_type=F32
-    ).astype(BF)
-    out_grad = lax.dot_general(mixed, dattn, (((0,), (0,)), ((), ())), preferred_element_type=F32)
-    out_grad = out_grad.astype(BF)
-
-    def by_member(blocks):
-        return absolute_pre(blocks, place)
-
-    do_blocks = by_member([mixed_grad[i * part : (i + 1) * part] for i in range(parts)])
-    do = jnp.concatenate([b[:pre_part] for b in do_blocks] + [b[pre_part:] for b in do_blocks], axis=0)
-    grads = jnp.concatenate(attend_back(qkv, do, stats, codes_q, codes_k), axis=1)
-    blocks = [
-        jnp.concatenate(
-            [
-                grads[i * pre_part : (i + 1) * pre_part],
-                grads[PRE + i * later_part : PRE + (i + 1) * later_part],
-            ],
-            axis=0,
-        )
-        for i in range(parts)
-    ]
-    project_grad = jnp.concatenate(by_member(blocks), axis=0)
-    qkv_grad = lax.dot_general(
-        h1, project_grad, (((0,), (0,)), ((), ())), preferred_element_type=F32
-    ).astype(BF)
-    first_terms = lax.dot_general(
-        project_grad, w_qkv, (((1,), (1,)), ((), ())), preferred_element_type=F32
-    )
-    first_grad = scatter_pre([first_terms[i * part : (i + 1) * part] for i in range(parts)])
-    input_grad = cotangent + middle_grad + norm_back(first_grad, first_normed, first_scaling, gain1)
-
-    def spread(grad):
-        rows = grad.shape[0] // seq_count
-        return seq.reduce(
-            [
-                lax.dynamic_slice_in_dim(grad, jnp.bitwise_xor(seq_place, i) * rows, rows, 0)
-                for i in range(seq_count)
-            ]
-        ).astype(BF)
-
-    def shared(block):
-        return absolute_pre(gather_pre(block), place)
-
-    down_full = jnp.concatenate(shared(spread(down_grad)), axis=1).astype(F32)
-    up_full = jnp.concatenate(shared(spread(up_grad)), axis=1).astype(F32)
-    out_own = lax.ppermute(spread(out_grad), ("pre", "seq"), [(b, a) for a, b in shuffle])
-    out_full = jnp.concatenate(shared(out_own), axis=0).astype(F32)
-    qkv_blocks = shared(spread(qkv_grad))
+    rows_in = (prefix_in[0], later_in[0], prefix_cot[0], later_cot[0], active)
+    near_down, wide_down, up_grad, dattn, middle_grad, sums2, up_sums = feed_back(
+        seq_count,
+        pre_part,
+        later_part,
+        w_down,
+        w_up,
+        df,
+        h2,
+        slope,
+        attn,
+        down_grad,
+        *rows_in,
+        gain2,
+    )
+    (fin_down, fin_up, fin_qkv, fin_out, *_, prefix_out, later_out, prefix_grad, later_grad, sums1, qkv_sums) = attend_back(
+        seq_count,
+        pre_part,
+        later_part,
+        w_qkv,
+        w_out,
+        w_down,
+        h1,
+        qkv,
+        stats,
+        mixed,
+        acted,
+        dattn,
+        middle_grad,
+        attn,
+        up_grad,
+        down_grad,
+        near_down,
+        wide_down,
+        *rows_in,
+        gain1,
+        db,
+        codes_q,
+        codes_k,
+    )
+
+    def shared(blocks):
+        rows = blocks.shape[0] // parts
+        return absolute_pre([blocks[i * rows : (i + 1) * rows] for i in range(parts)], place)
+
+    down_full = jnp.concatenate(shared(fin_down), axis=1).astype(F32)
+    up_full = jnp.concatenate(shared(fin_up), axis=1).astype(F32)
+    out_own = lax.ppermute(fin_out, ("pre", "seq"), [(b, a) for a, b in shuffle])
+    out_full = jnp.concatenate(absolute_pre(gather_pre(out_own), place), axis=0).astype(F32)
+    qkv_blocks = shared(fin_qkv)
     qkv_full = jnp.concatenate(
         [block[:, i * cols : (i + 1) * cols] for i in range(3) for block in qkv_blocks], axis=1
     ).astype(F32)
@@ -997,28 +1737,18 @@
         zeros = jnp.zeros((width * parts,), F32)
         return lax.dynamic_update_slice_in_dim(zeros, vector, place * width, 0)
 
-    column_sums = jnp.sum(project_grad.astype(F32), axis=0)
-    feature_sums = jnp.stack(
-        [
-            jnp.sum(first_grad * first_normed, axis=0),
-            jnp.sum(first_grad, axis=0),
-            jnp.sum(attn_grad.astype(F32), axis=0),
-            jnp.sum(second_grad * second_normed, axis=0),
-            jnp.sum(second_grad, axis=0),
-            jnp.sum(ffn_grad.astype(F32), axis=0),
-        ]
-    )
+    squares = jnp.stack([jnp.sum(sums1[2]), jnp.sum(sums1[3]), jnp.sum(sums1[4]), jnp.sum(active)])
     sums = [
-        feature_sums[0],
-        feature_sums[1],
-        placed(column_sums[:cols], cols),
-        placed(column_sums[2 * cols :], cols),
-        feature_sums[2],
-        feature_sums[3],
-        feature_sums[4],
-        feature_sums[5],
-        placed(jnp.sum(upper_grad.astype(F32), axis=0), ff_cols),
-        jnp.concatenate([square_sums, jnp.zeros((124,), F32)]),
+        sums1[0],
+        sums1[1],
+        placed(qkv_sums[0, :cols], cols),
+        placed(qkv_sums[0, 2 * cols :], cols),
+        sums2[0],
+        sums2[1],
+        sums2[2],
+        sums2[3],
+        placed(up_sums[0], ff_cols),
+        jnp.concatenate([squares, jnp.zeros((124,), F32)]),
     ]
     flat = sum_all(jnp.concatenate(sums).reshape(-1, 128)).reshape(-1)
     totals = [flat[i * D : (i + 1) * D] for i in range(8)]
@@ -1030,13 +1760,11 @@
         return lax.dynamic_slice_in_dim(vector, seq_place * width, width, 0)
 
     residual_rms = jnp.sqrt(total_squares[:3] / (total_squares[3] * D))
-    result = result.astype(BF)
-    input_grad = input_grad.astype(BF)
     return (
-        result[:pre_part][None],
-        result[pre_part:][None],
-        input_grad[:pre_part][None],
-        input_grad[pre_part:][None],
+        prefix_out[None],
+        later_out[None],
+        prefix_grad[None],
+        later_grad[None],
         own_share(totals[0]),
         own_share(totals[1]),
         qkv_full,

time: 1020 us -> 823 us (0.81); the launches traced: 1000 us -> 817 us
  Pallas kernels: 377 us -> 710 us
  waiting for transfers between devices: 305 us -> 9.89 us
  matrix products: 101 us -> 0 us
  other arithmetic: 66.2 us -> 22.8 us
  starting transfers between devices: 75.6 us -> 35.3 us
  local copies, waits for them, and re-layouts: 74.2 us -> 37.1 us
    pallas_call x1 -> x2, Pallas kernels: 36 us -> 369 us  [the longest x1 246 us: attend_back(): pl.pallas_call(functools.partial(attend_back_kernel, (seq_size, pre_part,...]
    ppermute x35 -> x7, waiting for transfers between devices: 250 us -> 0.02 us  [swap(): return lax.ppermute(value, 'seq', [(i, i ^ mask) for i in range(self.size)])]
    dot_general x8 -> x0, matrix products: 101 us -> none  [the longest x1 18.3 us: on_device(): lax.dot_general(upper_grad, w_up, (((1,), (1,)), ((), ())), preferred_ele...]
    ppermute x26 -> x5, waiting for transfers between devices: 47.8 us -> 4.19 us  [over_pre(): lax.ppermute(value, 'pre', [(i, i ^ mask) for i in range(lax.axis_size('p...]
    ppermute x26 -> x5, starting transfers between devices: 41.2 us -> 4.86 us  [over_pre(): lax.ppermute(value, 'pre', [(i, i ^ mask) for i in range(lax.axis_size('p...]
    convert_element_type x15 -> x4, other arithmetic: 39.8 us -> 12.7 us  [the longest x1 3.86 us: on_device(): down_full = jnp.concatenate(shared(fin_down), axis=1).astype(F32)]
    ppermute x35 -> x7, starting transfers between devices: 26.9 us -> 5.44 us  [swap(): return lax.ppermute(value, 'seq', [(i, i ^ mask) for i in range(self.size)])]
    unnamed x149 -> x59, local copies, waits for them, and re-layouts: 33.5 us -> 16.2 us
  transfers between devices with their start and end apart: 66 -> 17, of which waited for: 21 -> 3; matrix products, arithmetic and copies ran while one was open for 19% -> 5% of each run, Pallas kernels for 0% -> 0%
where the time goes in v3:
time: 823 us; the launch traced here: 817 us
  Pallas kernels  710 us (86%)
  local copies, waits for them, and re-layouts  37.1 us (5%)
  starting transfers between devices  35.3 us (4%)
  other arithmetic  22.8 us (3%)
  waiting for transfers between devices  9.89 us (1%)
    pallas_call x1, Pallas kernels, forward_pass(): pl.pallas_call(functools.partial(forward_kernel, (seq_size, pre_part, lat...  341 us
    pallas_call x1, Pallas kernels, attend_back(): pl.pallas_call(functools.partial(attend_back_kernel, (seq_size, pre_part,...  246 us
    pallas_call x1, Pallas kernels, feed_back(): pl.pallas_call(functools.partial(feed_back_kernel, (seq_size, pre_part, l...  123 us
  transfers between devices with their start and end apart: 17, of which 3 were waited for; matrix products, arithmetic and copies ran while one was open for 5% of the time, Pallas kernels for 0%

profile of v3, /device:TPU:5, one launch (start us, length us, event | category | flops | bytes accessed | tf_op | source)
XLA Modules:
  0.0 816.9 jit_solution(11841377672294139365)
XLA Ops:
  8.0 3.3 collective-permute-start.6
  11.9 1.0 constant_dynamic-slice_fusion.14
  12.9 5.4 collective-permute-start
  20.6 1.2 constant_dynamic-slice_fusion.17
  22.7 3.1 constant_dynamic-slice_fusion.12
  26.0 1.4 collective-permute-start.5
  29.5 1.1 broadcast_in_dim.73.codes_q
  36.9 341.1 %forward_pass.1 = (bf16[2048,1536]{1,0:T(8,128)(2,1)}, bf16[512,2048]{1,0:T(8,128)(2,1)}, bf16[2048,2048]{1,0:T(8,128)(2,1)}, bf16[2048,2048]{1,0:T(8,128)(2,1)}...) custom-call(bf16[256,1536]{1,0:T(8,128)(2,1)} %pad_maximum_fusion.ow, ...), custom_call_target="tpu_custom_call" | custom-call | flops 32212254720 | bytes 33554432 | tf_op jit(solution)/shard_map/forward_pass/pallas_call | solution.py:607
  378.0 122.6 %feed_back.1 = (bf16[1024,2048]{1,0:T(8,128)(2,1)}, bf16[1024,2048]{1,0:T(8,128)(2,1)}, bf16[2048,2048]{1,0:T(8,128)(2,1)}, bf16[1280,2048]{1,0:T(8,128)(2,1)}, ...) custom-call(bf16[2048,2048]{1,0:T(8,128)(2,1)} %get-tuple-element.51.w_down, ...), custom_call_target="tpu_custom_call" | custom-call | flops 32212254720 | bytes 33554432 | tf_op jit(solution)/shard_map/feed_back/pallas_call | solution.py:1033
  500.7 246.0 %attend_back.1 = (bf16[1024,2048]{1,0:T(8,128)(2,1)}, bf16[1024,2048]{1,0:T(8,128)(2,1)}, bf16[1024,1536]{1,0:T(8,128)(2,1)}, bf16[64,2048]{1,0:T(8,128)(2,1)}, ...) custom-call(bf16[2048,1536]{1,0:T(8,128)(2,1)} %get-tuple-element.49, ...), custom_call_target="tpu_custom_call" | custom-call | flops 26843545600 | bytes 33554432 | tf_op jit(solution)/shard_map/attend_back/pallas_call | solution.py:1466
  747.4 1.7 slice_reduce_fusion
  750.8 2.7 concatenate.47
  753.6 2.7 broadcast_select_fusion.11
  758.0 16.2 %collective-permute-start.13 = (bf16[64,2048]{1,0:T(8,128)(2,1)S(1)}, bf16[64,2048]{1,0:T(8,128)(2,1)S(1)}, u32[]{:S(2)}, u32[]{:S(2)}) collective-permute-start(bf16[64,2048]{1,0:T(8,128)(2,1)S(1)} %copy-done.8), channel_id=1, source_target_pairs={{0,0},{1,8},{2,16},{3,24},{4,1},{5,9},{6,17},{7,25},{8,2},{9,10},{... | collective-permute-start | bytes 786440 | tf_op jit(solution)/shard_map/ppermute | solution.py:1729
  774.7 3.9 maximum_convert_fusion.1
  778.6 3.8 maximum_convert_fusion
  782.6 4.2 collective-permute-done.9
  787.5 2.9 collective-permute-done.10
  791.2 2.8 collective-permute-done.11
  794.0 2.1 collective-permute-start.12
  796.1 3.5 convert_element_type.33
  799.5 2.7 collective-permute-start.14
  802.2 2.0 collective-permute-start.16
  811.8 1.6 maximum_convert_fusion.2
  (142 shorter events, 36.2 us)
Async XLA Ops:
  8.0 17.9 %collective-permute-start.6 = (bf16[24,128]{1,0:T(8,128)(2,1)S(1)}, bf16[24,128]{1,0:T(8,128)(2,1)S(1)}, u32[]{:S(2)}, u32[]{:S(2)}) collective-permute-start(bf16[24,128]{1,0:T(8,128)(2,1)S(1)} %bitcast.161), channel_id=1, source_target_pairs={{0,6},{1,7},{2,4},{3,5},{4,2},{5,3},{6,0},{7,1},{8,14},{9,15},{10,... | collective-permute-start | bytes 18440 | tf_op jit(solution)/shard_map/ppermute | solution.py:1528
  11.4 14.6 %collective-permute-start.4 = (bf16[24,128]{1,0:T(8,128)(2,1)S(1)}, bf16[24,128]{1,0:T(8,128)(2,1)S(1)}, u32[]{:S(2)}, u32[]{:S(2)}) collective-permute-start(bf16[24,128]{1,0:T(8,128)(2,1)S(1)} %bitcast.162), channel_id=1, source_target_pairs={{0,4},{1,5},{2,6},{3,7},{4,0},{5,1},{6,2},{7,3},{8,12},{9,13},{10,... | collective-permute-start | bytes 18440 | tf_op jit(solution)/shard_map/ppermute | solution.py:1528
  11.4 16.1 %collective-permute-start.2 = (bf16[24,128]{1,0:T(8,128)(2,1)S(1)}, bf16[24,128]{1,0:T(8,128)(2,1)S(1)}, u32[]{:S(2)}, u32[]{:S(2)}) collective-permute-start(bf16[24,128]{1,0:T(8,128)(2,1)S(1)} %bitcast.163), channel_id=1, source_target_pairs={{0,2},{1,3},{2,0},{3,1},{4,6},{5,7},{6,4},{7,5},{8,10},{9,11},{10,... | collective-permute-start | bytes 18440 | tf_op jit(solution)/shard_map/ppermute | solution.py:1528
  11.7 19.0 %collective-permute-start.1 = (bf16[24,128]{1,0:T(8,128)(2,1)S(1)}, bf16[24,128]{1,0:T(8,128)(2,1)S(1)}, u32[]{:S(2)}, u32[]{:S(2)}) collective-permute-start(bf16[24,128]{1,0:T(8,128)(2,1)S(1)} %bitcast.164), channel_id=1, source_target_pairs={{0,1},{1,0},{2,3},{3,2},{4,5},{5,4},{6,7},{7,6},{8,9},{9,8},{10,11... | collective-permute-start | bytes 18440 | tf_op jit(solution)/shard_map/ppermute | solution.py:1528
  12.9 23.3 %collective-permute-start = (bf16[64,2048]{1,0:T(8,128)(2,1)S(1)}, bf16[64,2048]{1,0:T(8,128)(2,1)S(1)}, u32[]{:S(2)}, u32[]{:S(2)}) collective-permute-start(bf16[64,2048]{1,0:T(8,128)(2,1)S(1)} %constant_dynamic-slice_fusion.14), channel_id=1, source_target_pairs={{0,0},{8,1},{16,2},{24,3},{1,4},{9,5},{17,6},{25,7},{2,8},{10,9},{... | collective-permute-start | bytes 786440 | tf_op jit(solution)/shard_map/ppermute | solution.py:1641
  25.9 4.8 collective-permute-start.7
  26.0 4.7 collective-permute-start.5
  27.5 3.3 collective-permute-start.3
  500.6 249.3 %copy-start.6 = (f32[8,2048]{1,0:T(8,128)S(1)}, f32[8,2048]{1,0:T(8,128)}, u32[]{:S(2)}) copy-start(f32[8,2048]{1,0:T(8,128)} %get-tuple-element.74) | copy-start | bytes 196612
  753.5 28.9 %collective-permute-start.8 = (f32[193,128]{1,0:T(8,128)S(1)}, f32[193,128]{1,0:T(8,128)S(1)}, u32[]{:S(2)}, u32[]{:S(2)}) collective-permute-start(f32[193,128]{1,0:T(8,128)S(1)} %bitcast.120), channel_id=1, source_target_pairs={{0,8},{8,0},{16,24},{24,16},{1,9},{9,1},{17,25},{25,17},{2,10},{10... | collective-permute-start | bytes 296456 | tf_op jit(solution)/shard_map/ppermute | solution.py:1549
  753.6 3.4 copy-start
  757.1 17.1 %copy-start.1 = (bf16[1024,1536]{1,0:T(8,128)(2,1)S(1)}, bf16[1024,1536]{1,0:T(8,128)(2,1)}, u32[]{:S(2)}) copy-start(bf16[1024,1536]{1,0:T(8,128)(2,1)} %get-tuple-element.76) | copy-start | bytes 9437188
  758.0 33.1 %collective-permute-start.13 = (bf16[64,2048]{1,0:T(8,128)(2,1)S(1)}, bf16[64,2048]{1,0:T(8,128)(2,1)S(1)}, u32[]{:S(2)}, u32[]{:S(2)}) collective-permute-start(bf16[64,2048]{1,0:T(8,128)(2,1)S(1)} %copy-done.8), channel_id=1, source_target_pairs={{0,0},{1,8},{2,16},{3,24},{4,1},{5,9},{6,17},{7,25},{8,2},{9,10},{... | collective-permute-start | bytes 786440 | tf_op jit(solution)/shard_map/ppermute | solution.py:1729
  782.5 4.3 collective-permute-start.9
  786.8 3.6 collective-permute-start.10
  790.4 3.6 collective-permute-start.11
  791.1 11.1 %collective-permute-start.15 = (bf16[64,2048]{1,0:T(8,128)(2,1)S(1)}, bf16[64,2048]{1,0:T(8,128)(2,1)S(1)}, u32[]{:S(2)}, u32[]{:S(2)}) collective-permute-start(bf16[64,2048]{1,0:T(8,128)(2,1)S(1)} %collective-permute-done.13), channel_id=1, source_target_pairs={{0,16},{8,24},{16,0},{24,8},{1,17},{9,25},{17,1},{25,9},{2,18},{10... | collective-permute-start | bytes 786440 | tf_op jit(solution)/shard_map/ppermute | solution.py:1549
  794.0 8.2 %collective-permute-start.12 = (f32[193,128]{1,0:T(8,128)S(1)}, f32[193,128]{1,0:T(8,128)S(1)}, u32[]{:S(2)}, u32[]{:S(2)}) collective-permute-start(f32[193,128]{1,0:T(8,128)S(1)} %add.121), channel_id=1, source_target_pairs={{0,4},{1,5},{2,6},{3,7},{4,0},{5,1},{6,2},{7,3},{8,12},{9,13},{10,... | collective-permute-start | bytes 296456 | tf_op jit(solution)/shard_map/ppermute | solution.py:1564
  799.5 13.8 %copy-start.5 = (bf16[128,2048]{1,0:T(8,128)(2,1)S(1)}, bf16[128,2048]{1,0:T(8,128)(2,1)}, u32[]{:S(2)}) copy-start(bf16[128,2048]{1,0:T(8,128)(2,1)} %get-tuple-element.68) | copy-start | bytes 1572868
  799.5 12.1 %collective-permute-start.14 = (bf16[64,2048]{1,0:T(8,128)(2,1)S(1)}, bf16[64,2048]{1,0:T(8,128)(2,1)S(1)}, u32[]{:S(2)}, u32[]{:S(2)}) collective-permute-start(bf16[64,2048]{1,0:T(8,128)(2,1)S(1)} %collective-permute-done.13), channel_id=1, source_target_pairs={{0,8},{8,0},{16,24},{24,16},{1,9},{9,1},{17,25},{25,17},{2,10},{10... | collective-permute-start | bytes 786440 | tf_op jit(solution)/shard_map/ppermute | solution.py:1549
  802.2 9.4 %collective-permute-start.16 = (bf16[64,2048]{1,0:T(8,128)(2,1)S(1)}, bf16[64,2048]{1,0:T(8,128)(2,1)S(1)}, u32[]{:S(2)}, u32[]{:S(2)}) collective-permute-start(bf16[64,2048]{1,0:T(8,128)(2,1)S(1)} %collective-permute-done.15), channel_id=1, source_target_pairs={{0,8},{8,0},{16,24},{24,16},{1,9},{9,1},{17,25},{25,17},{2,10},{10... | collective-permute-start | bytes 786440 | tf_op jit(solution)/shard_map/ppermute | solution.py:1549
  811.6 2.5 copy-start.3
  811.8 3.3 copy-start.4
  811.8 4.0 copy-start.2
  (2 other events, 1.7 us)

commit v4 on v3

--- a/solution.py
+++ b/solution.py
@@ -107,80 +107,171 @@
     )
 
 
-def greet(wide):
+def greet(masks, relay=None):
     barrier = pltpu.get_barrier_semaphore()
     seq = lax.axis_index("seq")
     pre = lax.axis_index("pre")
-    for mask in (1, *wide):
+
+    def signal(**target):
         pl.semaphore_signal(
-            barrier, inc=1, device_id={"seq": xor(seq, mask)}, device_id_type=pl.DeviceIdType.MESH
+            barrier, inc=1, device_id=target, device_id_type=pl.DeviceIdType.MESH
         )
+
+    for mask in masks:
+        signal(seq=xor(seq, mask))
     for mask in (1, 2):
-        pl.semaphore_signal(
-            barrier, inc=1, device_id={"pre": xor(pre, mask)}, device_id_type=pl.DeviceIdType.MESH
+        signal(pre=xor(pre, mask))
+    count = len(masks) + 2
+    if relay is not None:
+
+        @pl.when(relay.moves)
+        def _():
+            signal(seq=relay.there[0], pre=relay.there[1])
+            signal(seq=relay.back[0], pre=relay.back[1])
+
+        count = count + 2 * relay.moves.astype(jnp.int32)
+    pl.semaphore_wait(barrier, count)
+
+
+class Relay:
+    def __init__(self, size, send_sem, recv_sem, local_sem):
+        seq, pre = lax.axis_index("seq"), lax.axis_index("pre")
+        held = seq * 4 + pre
+        used = pre * size + seq
+        self.there = (lax.rem(held, size), lax.div(held, size))
+        self.back = (lax.div(used, 4), lax.rem(used, 4))
+        self.moves = held != used
+        self.sems = (send_sem, recv_sem, local_sem)
+
+    def copies(self, src, dst, target):
+        send_sem, recv_sem, local_sem = self.sems
+        return (
+            remote(src, dst, send_sem, recv_sem, seq=target[0], pre=target[1]),
+            pltpu.make_async_copy(src, dst, local_sem),
         )
-    pl.semaphore_wait(barrier, len(wide) + 3)
+
+    def begin(self, src, dst, target):
+        away, here = self.copies(src, dst, target)
+        pl.when(self.moves)(away.start)
+        pl.when(jnp.logical_not(self.moves))(here.start)
+
+    def finish(self, src, dst, target):
+        away, here = self.copies(src, dst, target)
+
+        @pl.when(self.moves)
+        def _():
+            away.wait_recv()
+            away.wait_send()
+
+        pl.when(jnp.logical_not(self.moves))(here.wait)
 
 
 def rows_of(index, count):
     return pl.ds(pl.multiple_of(index * count, count), count)
 
 
+def far_line(lines, line, turn):
+    low = lines - 1 - turn
+    low = low - (low <= line).astype(jnp.int32)
+    high = turn + (turn >= line).astype(jnp.int32)
+    return jnp.where(line < lines // 2, low, high)
+
+
+def early_rows(rows):
+    return (rows * 3 + 128) // 256 * 16
+
+
+class Copies:
+    def __init__(self):
+        self.items = []
+
+    def start(self, copy, when=None):
+        if when is None:
+            copy.start()
+        else:
+            pl.when(when)(copy.start)
+        self.items.append((copy, when))
+
+    def drain(self):
+        for copy, when in self.items:
+            if when is None:
+                copy.wait_send()
+            else:
+                pl.when(when)(copy.wait_send)
+
+
 class Gather:
-    def __init__(self, own, land, rows, send_sem, recv_sem, local_sem):
+    def __init__(self, own, land, rows, send_sem, recv_sem, local_sem, size):
         self.own, self.land, self.rows = own, land, rows
+        self.early = early_rows(rows)
         self.send_sem, self.recv_sem, self.local_sem = send_sem, recv_sem, local_sem
         self.seq = lax.axis_index("seq")
-        self.sent = []
+        self.lines = size // 2
+        self.line = lax.div(self.seq, jnp.int32(2))
+        self.twin = xor(self.seq, 1)
+        self.sent = Copies()
         self.local = None
 
-    def slot(self, place):
-        return self.land.at[rows_of(place, self.rows), :]
-
-    def begin(self, *masks):
-        for mask in masks:
-            copy = remote(
-                self.own,
-                self.slot(self.seq),
-                self.send_sem.at[mask],
-                self.recv_sem.at[mask],
-                seq=xor(self.seq, mask),
-            )
-            copy.start()
-            self.sent.append(copy)
-
-    def keep(self):
-        self.local = pltpu.make_async_copy(self.own, self.slot(self.seq), self.local_sem)
+    def view(self, place, kind):
+        first = {0: 0, 1: self.rows - self.early, 2: 0, 3: self.rows - self.early}[kind]
+        count = {0: self.rows, 1: self.early, 2: self.rows - self.early, 3: self.early}[kind]
+        return self.land.at[pl.ds(pl.multiple_of(place * self.rows + first, 16), count), :]
+
+    def copy(self, place, kind, send, recv, to, own=False):
+        there = self.view(place, kind)
+        src = there
+        if own:
+            first = self.rows - self.early if kind in (1, 3) else 0
+            count = there.shape[0]
+            src = self.own.at[first : first + count, :]
+        return remote(
+            src, there, self.send_sem.at[kind, send], self.recv_sem.at[kind, recv], seq=to
+        )
+
+    def beside(self, up):
+        return (self.line < self.lines - 1, self.seq + 2) if up else (self.line > 0, self.seq - 2)
+
+    def begin(self):
+        if self.early:
+            self.sent.start(self.copy(self.seq, 3, 0, 0, self.twin, True))
+        for up in (True, False):
+            there, to = self.beside(up)
+            spare = self.lines + (0 if up else 1)
+            self.sent.start(self.copy(self.seq, 0, spare, self.line, to, True), there)
+        self.sent.start(self.copy(self.seq, 2, self.line, self.line, self.twin, True))
+        self.local = pltpu.make_async_copy(self.own, self.view(self.seq, 0), self.local_sem)
         self.local.start()
 
-    def arrived(self, mask):
-        here = self.slot(xor(self.seq, mask))
-        remote(
-            here, here, self.send_sem.at[mask], self.recv_sem.at[mask], seq=xor(self.seq, mask)
-        ).wait_recv()
-
-    def forward(self, mask):
-        self.arrived(mask)
-        here = self.slot(xor(self.seq, mask))
-        copy = remote(
-            here,
-            here,
-            self.send_sem.at[mask + 1],
-            self.recv_sem.at[mask + 1],
-            seq=xor(self.seq, 1),
-        )
-        copy.start()
-        self.sent.append(copy)
-
-    def finish(self, wide):
+    def rest(self):
+        if not self.early:
+            return
+        self.copy(self.twin, 3, 0, 0, self.twin).wait_recv()
+        for up in (True, False):
+            there, to = self.beside(up)
+            spare = self.lines + (0 if up else 1)
+            self.sent.start(self.copy(self.twin, 1, spare, self.line, to), there)
+
+    def event(self, turn):
+        line = far_line(self.lines, self.line, jnp.int32(self.lines - 2 - turn))
+        step = jnp.where(line < self.line, 2, -2)
+        after = jnp.where(line < self.line, self.line < self.lines - 1, self.line > 0)
+        place = line * 2 + lax.rem(self.seq, jnp.int32(2))
+        other = xor(place, 1)
+        to = jnp.clip(self.seq + step, 0, 2 * self.lines - 1)
+        self.copy(place, 0, line, line, self.twin).wait_recv()
+        self.sent.start(self.copy(place, 0, line, line, to), after)
+        self.sent.start(self.copy(place, 2, line, line, self.twin))
+        if self.early:
+            self.copy(other, 1, line, line, self.twin).wait_recv()
+            self.sent.start(self.copy(other, 1, line, line, to), after)
+
+    def finish(self):
         self.local.wait()
-        self.arrived(1)
-        for mask in wide:
-            self.arrived(mask + 1)
+        for line in range(self.lines):
+            self.copy(line * 2, 2, line, line, self.twin).wait_recv()
 
     def drain(self):
-        for copy in self.sent:
-            copy.wait_send()
+        self.sent.drain()
 
 
 class Spread:
@@ -212,10 +303,16 @@
         copy.start()
         self.sent.append(copy)
 
-    def finish(self):
+    def finish_near(self):
         self.local.wait()
         self.copy(self.own, 1, 1).wait_recv()
+
+    def finish_far(self):
         self.copy(self.own, 3, 1).wait_recv()
+
+    def finish(self):
+        self.finish_near()
+        self.finish_far()
 
     def drain(self):
         for copy in self.sent:
@@ -289,23 +386,16 @@
 
 def forward_kernel(
     sizes,
-    own_qkv,
-    own_out,
-    own_up,
-    own_down,
+    small,
+    qkv_weight,
+    out_weight,
+    up_weight,
+    down_weight,
     prefix_in,
     later_in,
     prefix_cot,
     later_cot,
     active_ref,
-    gain1,
-    bias1,
-    out_bias,
-    gain2,
-    bias2,
-    shift,
-    factor,
-    up_bias,
     codes_q,
     codes_k,
     w_qkv,
@@ -322,6 +412,7 @@
     acted,
     slope,
     down_grad,
+    vectors,
     wbuf,
     lhs,
     qkv_v,
@@ -340,25 +431,40 @@
     acted_v,
     slope_v,
     grad_v,
+    own_qkv,
+    own_up,
+    own_down,
+    own_out,
+    small_v,
+    slope_bias,
     gather_send,
     gather_recv,
+    small_send,
+    small_recv,
     spread_send,
     spread_recv,
     sum_send,
     sum_recv,
+    relay_sem,
     local_sem,
 ):
     seq_size, pre_part, later_part = sizes
     part = pre_part + later_part
-    cols = own_qkv.shape[1] // 3
-    ff_cols = own_up.shape[1]
+    cols = qkv_weight.shape[1] // 12
+    ff_cols = up_weight.shape[1] // 4
+    own_d = D // seq_size
     wide = wide_masks(seq_size)
     pre = lax.axis_index("pre")
+    seq = lax.axis_index("seq")
     near_id = {"pre": xor(pre, 1)}
     far_id = {"pre": xor(pre, 2)}
 
     def gather(i, own, land):
-        return Gather(own, land, own.shape[0], gather_send.at[i], gather_recv.at[i], local_sem.at[i])
+        sems = (gather_send.at[i], gather_recv.at[i], local_sem.at[i])
+        return Gather(own, land, own.shape[0], *sems, seq_size)
+
+    def own_section(weight, first, columns):
+        return weight.at[:, pl.ds(pl.multiple_of(first + pre * columns, columns), columns)]
 
     get_qkv = gather(0, own_qkv, w_qkv)
     get_out = gather(1, own_out, w_out)
@@ -367,12 +473,41 @@
     get_h1 = Spread(h1_v, h1, part, spread_send.at[0], spread_recv.at[0], local_sem.at[4])
     get_df = Spread(df_v, df, part, spread_send.at[1], spread_recv.at[1], local_sem.at[5])
     get_h2 = Spread(h2_v, h2, part, spread_send.at[2], spread_recv.at[2], local_sem.at[6])
-
-    greet(wide)
-    get_qkv.begin(1, *wide)
-    get_qkv.keep()
-    get_out.begin(1, *wide)
-    get_out.keep()
+    relay = Relay(seq_size, relay_sem.at[0], relay_sem.at[1], relay_sem.at[2])
+    out_rows = own_d // 4
+    relayed = (out_weight.at[rows_of(pre, out_rows), :], own_out, relay.there)
+
+    cuts = [
+        pltpu.make_async_copy(
+            own_section(qkv_weight, i * D, cols),
+            own_qkv.at[:, i * cols : (i + 1) * cols],
+            local_sem.at[12 + i],
+        )
+        for i in range(3)
+    ]
+    late_cuts = [
+        pltpu.make_async_copy(own_section(weight, 0, ff_cols), own, local_sem.at[15 + i])
+        for i, (weight, own) in enumerate(((up_weight, own_up), (down_weight, own_down)))
+    ]
+    for cut in (*cuts, *late_cuts):
+        cut.start()
+    greet(range(1, seq_size), relay)
+    small_copies = [
+        remote(
+            small, small_v.at[seq], small_send.at[mask], small_recv.at[mask], seq=xor(seq, mask)
+        )
+        for mask in range(1, seq_size)
+    ]
+    for copy in small_copies:
+        copy.start()
+    keep_small = pltpu.make_async_copy(small, small_v.at[seq], local_sem.at[7])
+    keep_small.start()
+    relay.begin(*relayed)
+    for cut in cuts:
+        cut.wait()
+    get_qkv.begin()
+    for cut in late_cuts:
+        cut.wait()
     local_copies(
         [
             (prefix_in, x_v.at[:pre_part, :]),
@@ -382,12 +517,29 @@
         ],
         local_sem.at[8:12],
     )
+    keep_small.wait()
+    for copy in small_copies:
+        copy.wait_recv()
+    for member in range(seq_size):
+        vectors[:, member * own_d : (member + 1) * own_d] = small_v[member]
+    gain1, bias1, out_bias, gain2, bias2 = [vectors[i : i + 1, :] for i in (0, 1, 4, 5, 6)]
+    own_lanes = pl.ds(pl.multiple_of(pre * cols, cols), cols)
+    query_bias, value_bias = vectors[2:3, own_lanes], vectors[3:4, own_lanes]
+    up_shares = vectors[8:12, own_lanes]
+    up_bias = jnp.concatenate(
+        [
+            up_shares[k : k + 1, i * own_d : (i + 1) * own_d]
+            for i in range(seq_size // 4)
+            for k in range(4)
+        ],
+        axis=1,
+    )
     chunk = 32
 
     @pl.loop(0, part // chunk)
     def _(i):
         rows = rows_of(i, chunk)
-        value, _, _ = layer_norm_parts(x_v[rows, :].astype(F32), gain1[...], bias1[...])
+        value, _, _ = layer_norm_parts(x_v[rows, :].astype(F32), gain1, bias1)
         h1_v[rows, :] = value.astype(BF)
 
     get_h1.begin()
@@ -398,22 +550,25 @@
         df_v[rows, :] = (active_ref[rows, :] * cot_v[rows, :].astype(F32)).astype(BF)
 
     get_df.begin()
-    get_qkv.forward(wide[0])
-    get_h1.forward()
-    for mask in wide[1:-1]:
-        get_qkv.forward(mask)
-    get_up.begin(1, *wide)
-    get_up.keep()
-    get_qkv.forward(wide[-1])
+    slope_bias[...] = up_bias
+    turns = range(seq_size // 2 - 1)
+    get_qkv.rest()
+    for turn in turns:
+        get_qkv.event(turn)
+        if turn == 0:
+            relay.finish(*relayed)
+            get_out.begin()
+            get_h1.forward()
+        if turn == turns[-2]:
+            get_up.begin()
     get_h1.finish()
     get_df.forward()
+    get_out.rest()
     load = pltpu.make_async_copy(h1, lhs, local_sem.at[12])
     load.start()
-    get_qkv.finish(wide)
+    get_qkv.finish()
     local_copies([(w_qkv, wbuf.at[:, : 3 * cols])], local_sem.at[8:9])
     load.wait()
-    for mask in wide:
-        get_out.forward(mask)
 
     @pl.loop(0, 4)
     def _(r):
@@ -421,31 +576,37 @@
         head_rows = rows_of(member, pre_part)
         tail_rows = pl.ds(pl.multiple_of(4 * pre_part + member * later_part, 64), later_part)
 
-        @pl.loop(0, 3)
-        def _(j):
-            lanes = pl.ds(pl.multiple_of(j * cols, cols), cols)
+        for j in range(3):
+            lanes = slice(j * cols, (j + 1) * cols)
             value = dot_nn(lhs[rows_of(r, part), :], wbuf[:, lanes])
-            value = ((value + shift[:, lanes]) * factor[:, lanes]).astype(BF)
+            if j == 0:
+                value = (value + query_bias) * (1.0 / math.sqrt(HEAD_DIM))
+            if j == 2:
+                value = value + value_bias
+            value = value.astype(BF)
             qkv_v[head_rows, lanes] = value[:pre_part]
             qkv_v[tail_rows, lanes] = value[pre_part:]
 
     save_qkv = pltpu.make_async_copy(qkv_v, qkv, local_sem.at[13])
     save_qkv.start()
-    get_up.forward(wide[0])
+    for turn in turns:
+        get_out.event(turn)
+    get_up.rest()
     get_df.finish()
     pairs = cols // 128
 
-    @pl.loop(0, pairs)
-    def _(pair):
-        attend_pair(pair, cols, qkv_v, codes_q[...], codes_k[...], mixed_v, stats_v)
-
+    def attention(first, last):
+        @pl.loop(first, last)
+        def _(pair):
+            attend_pair(pair, cols, qkv_v, codes_q[...], codes_k[...], mixed_v, stats_v)
+
+    attention(0, pairs // 2)
+    get_up.event(0)
+    get_down.begin()
+    attention(pairs // 2, pairs)
     save_stats = pltpu.make_async_copy(stats_v, stats, local_sem.at[14])
     save_stats.start()
-    for mask in wide[1:-1]:
-        get_up.forward(mask)
-    get_down.begin(1, *wide)
-    get_down.keep()
-    get_out.finish(wide)
+    get_out.finish()
     local_copies([(w_out, wbuf.at[:cols, :])], local_sem.at[8:9])
 
     def position_rows(r):
@@ -494,7 +655,7 @@
     near[1].wait_recv()
 
     def own_term(lanes, head, tail):
-        bias = out_bias[:, lanes]
+        bias = vectors[4:5, lanes]
         attn_v[:pre_part, lanes] = head + near_v[1, :pre_part, lanes].astype(F32) + bias
         attn_v[pre_part:, lanes] = tail + near_v[1, pre_part:, lanes].astype(F32) + bias
 
@@ -505,7 +666,8 @@
         moves.append((mixed_v.at[head_rows, :], mixed.at[r * part : r * part + pre_part, :]))
         moves.append((mixed_v.at[tail_rows, :], mixed.at[r * part + pre_part : (r + 1) * part, :]))
     local_copies(moves, local_sem.at[16:24])
-    get_up.forward(wide[-1])
+    for turn in turns[1:]:
+        get_up.event(turn)
     far.wait_recv()
 
     @pl.loop(0, part // chunk)
@@ -513,33 +675,40 @@
         rows = rows_of(i, chunk)
         branch = attn_v[rows, :] + far_v[rows, :].astype(F32)
         attn_v[rows, :] = branch
-        value, _, _ = layer_norm_parts(x_v[rows, :].astype(F32) + branch, gain2[...], bias2[...])
+        value, _, _ = layer_norm_parts(x_v[rows, :].astype(F32) + branch, gain2, bias2)
         h2_v[rows, :] = value.astype(BF)
 
     get_h2.begin()
     save_attn = pltpu.make_async_copy(attn_v, attn, local_sem.at[15])
     save_attn.start()
-    get_down.forward(wide[0])
-    get_up.finish(wide)
+    get_down.rest()
+    get_up.finish()
     load = pltpu.make_async_copy(w_up, wbuf, local_sem.at[12])
     load.start()
-    get_h2.forward()
-    get_h2.finish()
-    local_copies([(h2, lhs)], local_sem.at[8:9])
+    get_h2.finish_near()
+    half = slice(0, 2 * part)
+    local_copies([(h2.at[half, :], lhs.at[half, :])], local_sem.at[8:9])
     load.wait()
 
-    @pl.loop(0, 4)
-    def _(r):
+    def up_rows(r):
         rows = rows_of(r, part)
 
         @pl.loop(0, ff_cols // 512)
         def _(j):
             lanes = rows_of(j, 512)
-            upper = dot_nn(lhs[rows, :], wbuf[:, lanes]) + up_bias[:, lanes]
+            upper = dot_nn(lhs[rows, :], wbuf[:, lanes]) + slope_bias[:, lanes]
             cumulative = 0.5 * (1.0 + lax.erf(upper * (1.0 / math.sqrt(2.0))))
             density = jnp.exp(-0.5 * upper * upper) * (1.0 / math.sqrt(2.0 * math.pi))
             acted_v[rows, lanes] = (upper * cumulative).astype(BF)
             slope_v[rows, lanes] = (cumulative + upper * density).astype(BF)
+
+    pl.loop(0, 2)(up_rows)
+    get_h2.forward()
+    get_down.event(0)
+    get_h2.finish_far()
+    half = slice(2 * part, 4 * part)
+    local_copies([(h2.at[half, :], lhs.at[half, :])], local_sem.at[8:9])
+    pl.loop(2, 4)(up_rows)
 
     saves = [
         pltpu.make_async_copy(acted_v, acted, local_sem.at[12]),
@@ -547,8 +716,8 @@
     ]
     for save in saves:
         save.start()
-    for mask in wide[1:-1]:
-        get_down.forward(mask)
+    for turn in turns[1:-1]:
+        get_down.event(turn)
     local_copies([(df, lhs)], local_sem.at[9:10])
 
     @pl.loop(0, D // 256)
@@ -564,23 +733,23 @@
         save.start()
         save.wait()
 
-    get_down.forward(wide[-1])
-    get_down.finish(wide)
+    get_down.event(turns[-1])
+    get_down.finish()
     for save in (*saves, save_qkv, save_stats, save_attn):
         save.wait()
     for item in (get_qkv, get_out, get_up, get_down, get_h1, get_df, get_h2):
         item.drain()
-    for copy in (*near, far):
+    for copy in (*near, far, *small_copies):
         copy.wait_send()
 
 
 def forward_pass(seq_size, pre_part, later_part, *operands):
-    own_qkv, own_out, own_up = operands[:3]
     part = pre_part + later_part
     length = 4 * part
-    width = own_qkv.shape[1]
+    width = 3 * D // 4
     cols = width // 3
-    ff_cols = own_up.shape[1]
+    ff_cols = FF // 4
+    own_d = D // seq_size
     hbm = pl.BlockSpec(memory_space=pl.ANY)
     vmem = pl.BlockSpec(memory_space=pltpu.VMEM)
 
@@ -602,13 +771,14 @@
         out((length, ff_cols)),
         out((length, ff_cols)),
         out((D, ff_cols)),
+        out((16, D), F32),
     )
     dma = pltpu.SemaphoreType.DMA
     return pl.pallas_call(
         functools.partial(forward_kernel, (seq_size, pre_part, later_part)),
         out_shape=outs,
-        in_specs=[hbm] * 8 + [vmem] * (len(operands) - 8),
-        out_specs=[hbm] * len(outs),
+        in_specs=[hbm] * 9 + [vmem] * (len(operands) - 9),
+        out_specs=[hbm] * (len(outs) - 1) + [vmem],
         scratch_shapes=[
             pltpu.VMEM((D, max(ff_cols, width)), BF),
             pltpu.VMEM((length, D), BF),
@@ -628,10 +798,19 @@
             pltpu.VMEM((length, ff_cols), BF),
             pltpu.VMEM((length, ff_cols), BF),
             pltpu.VMEM((256, ff_cols), BF),
-            dma((4, seq_size)),
-            dma((4, seq_size)),
+            pltpu.VMEM((own_d, width), BF),
+            pltpu.VMEM((own_d, ff_cols), BF),
+            pltpu.VMEM((own_d, ff_cols), BF),
+            pltpu.VMEM((own_d // 4, D), BF),
+            pltpu.VMEM((seq_size, 16, own_d), F32),
+            pltpu.VMEM((1, ff_cols), F32),
+            dma((4, 4, seq_size // 2 + 2)),
+            dma((4, 4, seq_size // 2)),
+            dma((seq_size,)),
+            dma((seq_size,)),
             dma((3, 4)),
             dma((3, 4)),
+            dma((3,)),
             dma((3,)),
             dma((3,)),
             dma((24,)),
@@ -715,12 +894,16 @@
         right = self.right.at[: self.rows, : self.width]
         return left, right
 
-    def step(self, mask):
+    def step(self, mask, early=None):
         left, right = self.views()
         own = pltpu.make_async_copy(self.block(mask), left, self.sem.at[0])
         own.start()
-        self.near_copy(mask).wait_recv()
-        other = pltpu.make_async_copy(self.near_slot(mask), right, self.sem.at[1])
+        if early is None:
+            self.near_copy(mask).wait_recv()
+            source = self.near_slot(mask)
+        else:
+            source = early.at[mask // 2 * self.rows : (mask // 2 + 1) * self.rows, :]
+        other = pltpu.make_async_copy(source, right, self.sem.at[1])
         other.start()
         index = self.pool.take()
         own.wait()
@@ -839,6 +1022,7 @@
     sizes,
     w_down,
     w_up,
+    acted,
     df,
     h2,
     slope,
@@ -849,27 +1033,34 @@
     prefix_cot,
     later_cot,
     active_ref,
-    gain2,
+    vectors,
     near_down,
     wide_down,
+    near_up,
     up_grad,
     dattn,
     middle_grad,
+    prefix_out,
+    later_out,
     sums,
     up_sums,
     wbuf,
     lhs,
+    acted_v,
     slope_v,
     du_v,
     x_v,
     cot_v,
     attn_v,
     acc_v,
+    ffn_v,
     dattn_v,
     terms_v,
     near_v,
     pass_v,
     far_v,
+    ffn_near_v,
+    ffn_far_v,
     left_v,
     right_v,
     total_v,
@@ -879,6 +1070,8 @@
     twin_recv,
     wide_send,
     wide_recv,
+    early_send,
+    early_recv,
     spread_send,
     spread_recv,
     sum_send,
@@ -889,6 +1082,7 @@
     part = pre_part + later_part
     length = 4 * part
     ff_cols = w_up.shape[1]
+    gain2 = vectors[5:6, :]
     wide = wide_masks(seq_size)
     late = sorted(wide, key=lambda m: (m == 2, m))
     pool = Pool(out_v, 3)
@@ -902,16 +1096,27 @@
         (twin_send, twin_recv, wide_send, wide_recv),
         work,
     )
+    put_up = Reduce(
+        up_grad,
+        near_up,
+        None,
+        D // seq_size,
+        ff_cols,
+        (early_send, early_recv, None, None),
+        work,
+    )
     get_dattn = Spread(dattn_v, dattn, part, spread_send, spread_recv, local_sem.at[2])
-    sum_dh2 = Sum(terms_v, near_v, pass_v, far_v, sum_send, sum_recv)
-
-    greet(wide)
+    sum_f = Sum(terms_v, ffn_near_v, pass_v, ffn_far_v, sum_send.at[0], sum_recv.at[0])
+    sum_dh2 = Sum(terms_v, near_v, pass_v, far_v, sum_send.at[1], sum_recv.at[1])
+
+    greet((1, *wide))
     put_down.begin(*late, 0)
     loads = [
         pltpu.make_async_copy(src, dst, local_sem.at[3 + i])
         for i, (src, dst) in enumerate(
             [
                 (w_down, wbuf),
+                (acted, acted_v),
                 (df, lhs),
                 (slope, slope_v),
                 (prefix_in, x_v.at[:pre_part, :]),
@@ -924,8 +1129,27 @@
     ]
     for load in loads:
         load.start()
-    for load in loads:
+    sums[...] = jnp.zeros_like(sums)
+    up_sums[...] = jnp.zeros_like(up_sums)
+    for load in loads[:2]:
         load.wait()
+
+    def f_term(r, store):
+        @pl.loop(0, D // 512)
+        def _(j):
+            store(
+                slice(0, part),
+                rows_of(j, 512),
+                dot_nt(acted_v[r * part : (r + 1) * part, :], wbuf[rows_of(j, 512), :]),
+            )
+
+    def keep_f(rows, lanes, value):
+        ffn_v[rows, lanes] = value
+
+    sum_f.run(f_term, keep_f)
+    for load in loads[2:]:
+        load.wait()
+    put_down.step(late[0])
 
     @pl.loop(0, 4)
     def _(r):
@@ -941,7 +1165,11 @@
     load.start()
     load_h2 = pltpu.make_async_copy(h2, lhs, local_sem.at[4])
     load_h2.start()
-    put_down.step(late[0])
+    for copy in sum_f.near_copies:
+        copy.wait_send()
+    for mask in late[1:-1]:
+        put_down.step(mask)
+    sum_f.far_copy.wait_send()
     load.wait()
 
     def dh2_term(r, store):
@@ -957,8 +1185,6 @@
         acc_v[rows, lanes] = value
 
     sum_dh2.run(dh2_term, keep_dh2)
-    for mask in late[1:-1]:
-        put_down.step(mask)
     load_h2.wait()
     columns_grad(
         lhs,
@@ -968,20 +1194,39 @@
         grad_v,
         lambda rows: pltpu.make_async_copy(grad_v, up_grad.at[rows, :], local_sem.at[3]),
     )
-    sums[...] = jnp.zeros_like(sums)
-    up_sums[...] = jnp.zeros_like(up_sums)
+    put_up.begin(late[0])
     if len(late) > 1:
         put_down.step(late[-1])
+    chunk = 32
+    sum_f.far_copy.wait_recv()
+
+    @pl.loop(0, part // chunk)
+    def _(i):
+        rows = rows_of(i, chunk)
+        live = active_ref[rows, :]
+        ffn = ffn_v[rows, :] + ffn_far_v[rows, :].astype(F32) + vectors[7:8, :]
+        branch = attn_v[rows, :]
+        result = x_v[rows, :].astype(F32) + live * (branch + ffn)
+        add_rows(sums, 4, live * result * result)
+        add_rows(sums, 5, live * branch * branch)
+        add_rows(sums, 6, live * ffn * ffn)
+        acted_v[rows, :] = result.astype(BF)
+
+    saves = [
+        pltpu.make_async_copy(acted_v.at[:pre_part, :], prefix_out, local_sem.at[4]),
+        pltpu.make_async_copy(acted_v.at[pre_part:part, :], later_out, local_sem.at[5]),
+    ]
+    for save in saves:
+        save.start()
     sum_dh2.far_copy.wait_recv()
-    chunk = 32
 
     @pl.loop(0, part // chunk)
     def _(i):
         rows = rows_of(i, chunk)
         grad = acc_v[rows, :] + far_v[rows, :].astype(F32)
         middle = x_v[rows, :].astype(F32) + attn_v[rows, :]
-        _, normed, scaling = layer_norm_parts(middle, gain2[...], 0.0)
-        back = norm_back(grad, normed, scaling, gain2[...])
+        _, normed, scaling = layer_norm_parts(middle, gain2, 0.0)
+        back = norm_back(grad, normed, scaling, gain2)
         acc_v[rows, :] = back
         direct = active_ref[rows, :] * cot_v[rows, :].astype(F32)
         value = (direct + back).astype(BF)
@@ -992,8 +1237,8 @@
         add_rows(sums, 3, direct)
 
     get_dattn.begin()
-    save = pltpu.make_async_copy(acc_v, middle_grad, local_sem.at[3])
-    save.start()
+    saves.append(pltpu.make_async_copy(acc_v, middle_grad, local_sem.at[3]))
+    saves[-1].start()
 
     @pl.loop(0, length // chunk)
     def _(i):
@@ -1002,8 +1247,10 @@
     get_dattn.forward()
     put_down.settle(wide)
     get_dattn.finish()
-    save.wait()
-    for item in (put_down, get_dattn, sum_dh2, pool):
+    for save in saves:
+        save.wait()
+    put_up.near_copy(late[0]).wait_recv()
+    for item in (put_down, put_up, get_dattn, sum_dh2, pool):
         item.drain()
 
 
@@ -1023,9 +1270,12 @@
     outs = (
         out((half * own_d, ff_cols)),
         out((half * own_d, ff_cols)),
+        out((half * own_d, ff_cols)),
         out((D, ff_cols)),
         out((length, D)),
         out((part, D), F32),
+        out((pre_part, D)),
+        out((later_part, D)),
         out((8, D), F32),
         out((8, ff_cols), F32),
     )
@@ -1033,21 +1283,25 @@
     return pl.pallas_call(
         functools.partial(feed_back_kernel, (seq_size, pre_part, later_part)),
         out_shape=outs,
-        in_specs=[hbm] * 11 + [vmem] * (len(operands) - 11),
-        out_specs=[hbm] * 5 + [vmem] * 2,
+        in_specs=[hbm] * 12 + [vmem] * (len(operands) - 12),
+        out_specs=[hbm] * 8 + [vmem] * 2,
         scratch_shapes=[
             pltpu.VMEM((D, ff_cols), BF),
             pltpu.VMEM((length, D), BF),
+            pltpu.VMEM((length, ff_cols), BF),
             pltpu.VMEM((length, ff_cols), BF),
             pltpu.VMEM((length, ff_cols), BF),
             pltpu.VMEM((part, D), BF),
             pltpu.VMEM((part, D), BF),
             pltpu.VMEM((part, D), F32),
             pltpu.VMEM((part, D), F32),
+            pltpu.VMEM((part, D), F32),
             pltpu.VMEM((part, D), BF),
             pltpu.VMEM((2, part, D), BF),
             pltpu.VMEM((2, part, D), BF),
             pltpu.VMEM((part, D), BF),
+            pltpu.VMEM((part, D), BF),
+            pltpu.VMEM((2, part, D), BF),
             pltpu.VMEM((part, D), BF),
             pltpu.VMEM((own_d, ff_cols), BF),
             pltpu.VMEM((own_d, ff_cols), BF),
@@ -1058,11 +1312,13 @@
             dma((half,)),
             dma((half,)),
             dma((half,)),
+            dma((half,)),
+            dma((half,)),
             dma((4,)),
             dma((4,)),
-            dma((3,)),
-            dma((3,)),
-            dma((12,)),
+            dma((2, 3)),
+            dma((2, 3)),
+            dma((16,)),
         ],
         compiler_params=pltpu.CompilerParams(
             collective_id=1, has_side_effects=True, vmem_limit_bytes=62 * 2**20
@@ -1121,26 +1377,25 @@
     sizes,
     w_qkv,
     w_out,
-    w_down,
     h1,
     qkv,
     stats,
     mixed,
-    acted,
     dattn,
     middle_grad,
-    attn,
     up_grad,
     down_grad,
     near_down,
     wide_down,
+    early_up,
     prefix_in,
     later_in,
     prefix_cot,
     later_cot,
     active_ref,
-    gain1,
-    down_bias,
+    vectors,
+    feed_sums,
+    up_sums,
     codes_q,
     codes_k,
     fin_down,
@@ -1155,12 +1410,9 @@
     wide_qkv,
     out_grad,
     qkv_grad,
-    prefix_out,
-    later_out,
     prefix_grad,
     later_grad,
     sums,
-    qkv_sums,
     wbuf,
     lhs,
     qkv_v,
@@ -1173,7 +1425,6 @@
     dv_v,
     x_v,
     cot_v,
-    attn_v,
     middle_v,
     acc_v,
     terms_v,
@@ -1189,6 +1440,12 @@
     res_up,
     res_qkv,
     res_out,
+    moved_out,
+    qkv_sums,
+    sums_land,
+    total_send,
+    total_recv,
+    relay_sem,
     twin_send,
     twin_recv,
     wide_send,
@@ -1204,7 +1461,7 @@
     length = 4 * part
     width = w_qkv.shape[1]
     cols = width // 3
-    ff_cols = w_down.shape[1]
+    ff_cols = up_grad.shape[1]
     own_d = D // seq_size
     own_o = cols // seq_size
     pre = lax.axis_index("pre")
@@ -1228,12 +1485,31 @@
     get_down = spread_of(0, res_down, fin_down)
     get_up = spread_of(1, res_up, fin_up)
     get_qkv = spread_of(2, res_qkv, fin_qkv)
-    sum_f = Sum(terms_v, near_v, pass_v, far_v, sum_send.at[0], sum_recv.at[0])
-    sum_dh1 = Sum(terms_v, near_v, pass_v, far_v, sum_send.at[1], sum_recv.at[1])
+    sum_dh1 = Sum(terms_v, near_v, pass_v, far_v, sum_send, sum_recv)
     chunk = 32
 
-    greet(wide)
-    put_up.begin(*late, 0)
+    relay = Relay(seq_size, relay_sem.at[0], relay_sem.at[1], relay_sem.at[2])
+    relayed = (res_out, moved_out, relay.back)
+    get_out = Spread(
+        moved_out, fin_out, own_o, spread_send.at[3], spread_recv.at[3], local_sem.at[20]
+    )
+    bits = [1 << i for i in range(seq_size.bit_length() - 1)]
+    greet(sorted({*wide, *bits}), relay)
+    put_up.begin(*late[1:])
+    stages = [
+        remote(sums, sums_land.at[i], total_send.at[i], total_recv.at[i], **target)
+        for i, target in enumerate(
+            [{"pre": xor(pre, 1)}, {"pre": xor(pre, 2)}]
+            + [{"seq": xor(lax.axis_index("seq"), bit)} for bit in bits]
+        )
+    ]
+
+    def add_stage(i, onward=True):
+        stages[i].wait_recv()
+        stages[i].wait_send()
+        sums[...] += sums_land[i]
+        if onward:
+            stages[i + 1].start()
 
     def load_all(first, *pairs):
         copies = [
@@ -1248,14 +1524,13 @@
         for copy in copies:
             copy.wait()
 
-    loads = load_all(5, (w_down, wbuf), (acted, lhs))
+    loads = load_all(5, (w_out, wbuf.at[:cols, :]), (dattn, lhs))
     more = load_all(
         8,
         (prefix_in, x_v.at[:pre_part, :]),
         (later_in, x_v.at[pre_part:, :]),
         (prefix_cot, cot_v.at[:pre_part, :]),
         (later_cot, cot_v.at[pre_part:, :]),
-        (attn, attn_v),
         (middle_grad, middle_v),
         (qkv, qkv_v),
         (stats, stats_v),
@@ -1263,25 +1538,14 @@
     )
     sums[...] = jnp.zeros_like(sums)
     qkv_sums[...] = jnp.zeros_like(qkv_sums)
-    wait_all(loads)
-
-    def f_term(r, store):
-        @pl.loop(0, D // 512)
-        def _(j):
-            store(
-                slice(0, part),
-                rows_of(j, 512),
-                dot_nt(lhs[r * part : (r + 1) * part, :], wbuf[rows_of(j, 512), :]),
-            )
-
+    put_up.step(late[0], early_up)
+    put_down.final(wide, res_down)
+    get_down.begin()
     def keep(rows, lanes, value):
         acc_v[rows, lanes] = value
 
-    sum_f.run(f_term, keep)
-    loads = load_all(5, (w_out, wbuf.at[:cols, :]), (dattn, lhs))
+    wait_all(loads)
     wait_all(more)
-    put_up.step(late[0])
-    wait_all(loads)
 
     def position_rows(r):
         member = lax.rem(r, 2) * (xor(pre, 1) - pre) + lax.div(r, 2) * (xor(pre, 2) - pre) + pre
@@ -1306,6 +1570,7 @@
         lambda rows: pltpu.make_async_copy(grad_v.at[:, :D], out_grad.at[rows, :], local_sem.at[5]),
     )
     put_out.begin(*late, 0)
+    put_up.begin(0)
     loads = load_all(5, (w_qkv, wbuf.at[:, :width]))
     for r in range(4):
         head_rows, tail_rows = position_rows(jnp.int32(r))
@@ -1333,28 +1598,15 @@
                 dqkv_v,
             )
 
-    attention(0, pairs // 2)
     for mask in late[1:-1]:
         put_up.step(mask)
-    sum_f.far_copy.wait_recv()
-    sum_f.drain()
-
-    @pl.loop(0, part // chunk)
-    def _(i):
-        rows = rows_of(i, chunk)
-        live = active_ref[rows, :]
-        ffn = acc_v[rows, :] + far_v[rows, :].astype(F32) + down_bias[...]
-        branch = attn_v[rows, :]
-        result = x_v[rows, :].astype(F32) + live * (branch + ffn)
-        add_rows(sums, 2, live * result * result)
-        add_rows(sums, 3, live * branch * branch)
-        add_rows(sums, 4, live * ffn * ffn)
-        pass_v[rows, :] = result.astype(BF)
-
-    put_down.final(wide, res_down)
-    get_down.begin()
+    attention(0, pairs // 2)
+    if len(late) > 1:
+        put_up.step(late[-1])
+    get_down.forward()
     attention(pairs // 2, pairs)
-    get_down.forward()
+    for mask in late:
+        put_out.step(mask)
     wait_all(loads)
     columns_grad(
         lhs,
@@ -1367,10 +1619,7 @@
         ),
     )
     put_qkv.begin(*late, 0)
-    put_up.step(late[-1])
     get_down.finish()
-    saves = load_all(6, (pass_v.at[:pre_part, :], prefix_out), (pass_v.at[pre_part:, :], later_out))
-    wait_all(saves)
 
     def dh1_term(r, store):
         head_rows, tail_rows = position_rows(jnp.int32(r))
@@ -1387,16 +1636,18 @@
     def _(i):
         add_rows(qkv_sums, 0, dqkv_v[rows_of(i, chunk), :].astype(F32))
 
-    for mask in late:
-        put_out.step(mask)
+    put_up.settle(wide)
+    put_up.final(wide, res_up)
+    get_up.begin()
+    put_qkv.step(late[0])
     sum_dh1.far_copy.wait_recv()
 
     @pl.loop(0, part // chunk)
     def _(i):
         rows = rows_of(i, chunk)
         grad = acc_v[rows, :] + far_v[rows, :].astype(F32)
-        _, normed, scaling = layer_norm_parts(x_v[rows, :].astype(F32), gain1[...], 0.0)
-        back = norm_back(grad, normed, scaling, gain1[...])
+        _, normed, scaling = layer_norm_parts(x_v[rows, :].astype(F32), vectors[0:1, :], 0.0)
+        back = norm_back(grad, normed, scaling, vectors[0:1, :])
         add_rows(sums, 0, grad * normed)
         add_rows(sums, 1, grad)
         value = cot_v[rows, :].astype(F32) + middle_v[rows, :] + back
@@ -1404,25 +1655,44 @@
         x_v[rows, :] = terms_rows
 
     saves = load_all(6, (x_v.at[:pre_part, :], prefix_grad), (x_v.at[pre_part:, :], later_grad))
-    put_up.settle(wide)
-    put_up.final(wide, res_up)
-    get_up.begin()
-    put_qkv.step(late[0])
+    own_lanes = pl.ds(pl.multiple_of(pre * cols, cols), cols)
+    sums[2:5, :] = feed_sums[4:7, :]
+    sums[5:9, :] = feed_sums[:4, :]
+    sums[9:10, own_lanes] = qkv_sums[0:1, :cols]
+    sums[10:11, own_lanes] = qkv_sums[0:1, 2 * cols :]
+    for k in range(4):
+        sums[11 + k : 12 + k, own_lanes] = jnp.concatenate(
+            [
+                up_sums[0:1, (i * 4 + k) * own_d : (i * 4 + k + 1) * own_d]
+                for i in range(seq_size // 4)
+            ],
+            axis=1,
+        )
+    sums[15:16, :] = jnp.zeros((1, D), F32) + jnp.sum(active_ref[...])
+    stages[0].start()
     put_out.settle(wide)
     put_out.final(wide, res_out)
+    relay.begin(*relayed)
+    add_stage(0)
     wait_all(saves)
-    saves = load_all(6, (res_out, fin_out))
     for mask in late[1:]:
         put_qkv.step(mask)
+    add_stage(1, False)
     get_up.forward()
+    relay.finish(*relayed)
+    get_out.begin()
     put_qkv.settle(wide)
     put_qkv.final(wide, res_qkv)
     get_qkv.begin()
+    stages[2].start()
+    get_out.forward()
     get_up.finish()
+    for i in range(2, len(stages)):
+        add_stage(i, i + 1 < len(stages))
+    get_out.finish()
     get_qkv.forward()
     get_qkv.finish()
-    wait_all(saves)
-    for item in (put_up, put_out, put_qkv, get_down, get_up, get_qkv, sum_dh1, pool):
+    for item in (put_up, put_out, put_qkv, get_down, get_up, get_out, get_qkv, sum_dh1, pool):
         item.drain()
 
 
@@ -1431,7 +1701,7 @@
     length = 4 * part
     width = operands[0].shape[1]
     cols = width // 3
-    ff_cols = operands[2].shape[1]
+    ff_cols = FF // 4
     own_d = D // seq_size
     own_o = cols // seq_size
     half = seq_size // 2
@@ -1445,7 +1715,7 @@
         out((4 * own_d, ff_cols)),
         out((4 * own_d, ff_cols)),
         out((4 * own_d, width)),
-        out((own_o, D)),
+        out((4 * own_o, D)),
         out((half * own_d, ff_cols)),
         out((half * own_d, ff_cols)),
         out((half * own_o, D)),
@@ -1456,18 +1726,16 @@
         out((D, width)),
         out((pre_part, D)),
         out((later_part, D)),
-        out((pre_part, D)),
-        out((later_part, D)),
-        out((8, D), F32),
-        out((8, width), F32),
+        out((16, D), F32),
     )
     most = max(ff_cols, D, width)
+    stages = 1 + seq_size.bit_length()
     dma = pltpu.SemaphoreType.DMA
     return pl.pallas_call(
         functools.partial(attend_back_kernel, (seq_size, pre_part, later_part)),
         out_shape=outs,
-        in_specs=[hbm] * 19 + [vmem] * (len(operands) - 19),
-        out_specs=[hbm] * 16 + [vmem] * 2,
+        in_specs=[hbm] * 17 + [vmem] * (len(operands) - 17),
+        out_specs=[hbm] * 14 + [vmem],
         scratch_shapes=[
             pltpu.VMEM((D, most), BF),
             pltpu.VMEM((length, D), BF),
@@ -1483,7 +1751,6 @@
             pltpu.VMEM((part, D), BF),
             pltpu.VMEM((part, D), F32),
             pltpu.VMEM((part, D), F32),
-            pltpu.VMEM((part, D), F32),
             pltpu.VMEM((2, part, D), BF),
             pltpu.VMEM((2, part, D), BF),
             pltpu.VMEM((part, D), BF),
@@ -1497,15 +1764,21 @@
             pltpu.VMEM((own_d, ff_cols), BF),
             pltpu.VMEM((own_d, width), BF),
             pltpu.VMEM((own_o, D), BF),
+            pltpu.VMEM((own_o, D), BF),
+            pltpu.VMEM((8, width), F32),
+            pltpu.VMEM((stages, 16, D), F32),
+            dma((stages,)),
+            dma((stages,)),
+            dma((3,)),
             dma((3, half)),
             dma((3, half)),
             dma((3, half)),
             dma((3, half)),
-            dma((3, 4)),
-            dma((3, 4)),
-            dma((2, 3)),
-            dma((2, 3)),
-            dma((20,)),
+            dma((4, 4)),
+            dma((4, 4)),
+            dma((3,)),
+            dma((3,)),
+            dma((24,)),
         ],
         compiler_params=pltpu.CompilerParams(
             collective_id=2, has_side_effects=True, vmem_limit_bytes=63 * 2**20
@@ -1517,53 +1790,6 @@
         ),
         name="attend_back",
     )(*operands)
-
-
-class Seq:
-    def __init__(self):
-        self.size = lax.axis_size("seq")
-        self.place = lax.axis_index("seq")
-
-    def swap(self, value, mask):
-        return lax.ppermute(value, "seq", [(i, i ^ mask) for i in range(self.size)])
-
-    def gather(self, own):
-        blocks = [own, self.swap(own, 1)]
-        for mask in range(2, self.size, 2):
-            blocks.append(self.swap(own, mask))
-            blocks.append(self.swap(blocks[-1], 1))
-        return blocks
-
-    def reorder(self, value, axis):
-        block = value.shape[axis] // self.size
-        return jnp.concatenate(
-            [
-                lax.dynamic_slice_in_dim(value, jnp.bitwise_xor(self.place, i) * block, block, axis)
-                for i in range(self.size)
-            ],
-            axis=axis,
-        )
-
-
-def over_pre(value, mask):
-    return lax.ppermute(value, "pre", [(i, i ^ mask) for i in range(lax.axis_size("pre"))])
-
-
-def gather_pre(own):
-    far = over_pre(own, 2)
-    near = over_pre(own, 1)
-    return [own, near, far, over_pre(far, 1)]
-
-
-def sum_all(value):
-    for mask in (1, 2):
-        value = value + over_pre(value, mask)
-    size = lax.axis_size("seq")
-    mask = 1
-    while mask < size:
-        value = value + lax.ppermute(value, "seq", [(i, i ^ mask) for i in range(size)])
-        mask *= 2
-    return value
 
 
 def absolute_pre(blocks, place):
@@ -1596,49 +1822,34 @@
     prefix_cot,
     later_cot,
 ):
-    scale = 1.0 / math.sqrt(HEAD_DIM)
     pre_part = prefix_in.shape[1]
     later_part = later_in.shape[1]
     part = pre_part + later_part
     parts = lax.axis_size("pre")
     place = lax.axis_index("pre")
-    seq = Seq()
-    seq_count = seq.size
-    seq_place = seq.place
+    seq_count = lax.axis_size("seq")
+    seq_place = lax.axis_index("seq")
     own_d = D // seq_count
     cols = D // parts
-    ff_cols = FF // parts
-    length = parts * part
-
-    packed = jnp.concatenate(
+
+    small = jnp.concatenate(
         [
-            first_gain,
-            first_bias,
-            query_bias,
-            value_bias,
-            out_bias,
-            second_gain,
-            second_bias,
-            down_bias,
-            up_bias,
+            jnp.stack(
+                [
+                    first_gain,
+                    first_bias,
+                    query_bias,
+                    value_bias,
+                    out_bias,
+                    second_gain,
+                    second_bias,
+                    down_bias,
+                ]
+            ),
+            up_bias.reshape(4, own_d),
+            jnp.zeros((4, own_d), BF),
         ]
-    ).reshape(-1, 128)
-    small = seq.reorder(jnp.stack(seq.gather(packed)).reshape(seq_count, -1), 0).astype(F32)
-    vectors = [small[:, i * own_d : (i + 1) * own_d].reshape(1, D) for i in range(8)]
-    full_up_bias = small[:, 8 * own_d :].reshape(1, FF)
-    (gain1, bias1, qb, vb, ob, gain2, bias2, db) = vectors
-
-    def section(weight, start, width):
-        return lax.dynamic_slice_in_dim(weight, start + place * width, width, 1)
-
-    own_qkv = jnp.concatenate([section(qkv_weight, i * D, cols) for i in range(3)], axis=1)
-    block_rows = own_d // parts
-    out_block = lax.dynamic_slice_in_dim(out_weight, place * block_rows, block_rows, 0)
-    shuffle = [
-        ((b % parts) * seq_count + b // parts, (b // seq_count) * seq_count + b % seq_count)
-        for b in range(parts * seq_count)
-    ]
-    own_out = lax.ppermute(out_block, ("pre", "seq"), shuffle)
+    ).astype(F32)
     doc_id, live = token_tables(doc_lengths, doc_exit, token_skip)
     live_here = lax.dynamic_slice_in_dim(live[0], place * later_part, later_part, 0)
     active = jnp.concatenate([jnp.ones((pre_part,), F32), live_here.astype(F32)])[:, None]
@@ -1647,75 +1858,61 @@
         [jnp.full((PRE,), -1, jnp.int32), jnp.where(live[0], doc_id[0], -2)]
     )[None, :]
 
-    def own_columns(vector, width):
-        return lax.dynamic_slice_in_dim(vector, place * width, width, 1)
-
-    shift = jnp.concatenate(
-        [own_columns(qb, cols), jnp.zeros((1, cols), F32), own_columns(vb, cols)], axis=1
-    )
-    factor = jnp.concatenate([jnp.full((1, cols), scale, F32), jnp.ones((1, 2 * cols), F32)], axis=1)
-    (w_qkv, w_out, w_up, w_down, h1, df, h2, qkv, mixed, stats, attn, acted, slope, down_grad) = forward_pass(
+    (w_qkv, w_out, w_up, w_down, h1, df, h2, qkv, mixed, stats, attn, acted, slope, down_grad, vectors) = forward_pass(
         seq_count,
         pre_part,
         later_part,
-        own_qkv,
-        own_out,
-        section(up_weight, 0, ff_cols),
-        section(down_weight, 0, ff_cols),
+        small,
+        qkv_weight,
+        out_weight,
+        up_weight,
+        down_weight,
         prefix_in[0],
         later_in[0],
         prefix_cot[0],
         later_cot[0],
         active,
-        gain1,
-        bias1,
-        ob,
-        gain2,
-        bias2,
-        shift,
-        factor,
-        own_columns(full_up_bias, ff_cols),
         codes_q,
         codes_k,
     )
 
     rows_in = (prefix_in[0], later_in[0], prefix_cot[0], later_cot[0], active)
-    near_down, wide_down, up_grad, dattn, middle_grad, sums2, up_sums = feed_back(
+    (near_down, wide_down, early_up, up_grad, dattn, middle_grad, prefix_out, later_out, feed_sums, up_sums) = feed_back(
         seq_count,
         pre_part,
         later_part,
         w_down,
         w_up,
+        acted,
         df,
         h2,
         slope,
         attn,
         down_grad,
         *rows_in,
-        gain2,
-    )
-    (fin_down, fin_up, fin_qkv, fin_out, *_, prefix_out, later_out, prefix_grad, later_grad, sums1, qkv_sums) = attend_back(
+        vectors,
+    )
+    (fin_down, fin_up, fin_qkv, fin_out, *_, prefix_grad, later_grad, sums) = attend_back(
         seq_count,
         pre_part,
         later_part,
         w_qkv,
         w_out,
-        w_down,
         h1,
         qkv,
         stats,
         mixed,
-        acted,
         dattn,
         middle_grad,
-        attn,
         up_grad,
         down_grad,
         near_down,
         wide_down,
+        early_up,
         *rows_in,
-        gain1,
-        db,
+        vectors,
+        feed_sums,
+        up_sums,
         codes_q,
         codes_k,
     )
@@ -1726,58 +1923,32 @@
 
     down_full = jnp.concatenate(shared(fin_down), axis=1).astype(F32)
     up_full = jnp.concatenate(shared(fin_up), axis=1).astype(F32)
-    out_own = lax.ppermute(fin_out, ("pre", "seq"), [(b, a) for a, b in shuffle])
-    out_full = jnp.concatenate(absolute_pre(gather_pre(out_own), place), axis=0).astype(F32)
+    out_full = jnp.concatenate(shared(fin_out), axis=0).astype(F32)
     qkv_blocks = shared(fin_qkv)
     qkv_full = jnp.concatenate(
         [block[:, i * cols : (i + 1) * cols] for i in range(3) for block in qkv_blocks], axis=1
     ).astype(F32)
 
-    def placed(vector, width):
-        zeros = jnp.zeros((width * parts,), F32)
-        return lax.dynamic_update_slice_in_dim(zeros, vector, place * width, 0)
-
-    squares = jnp.stack([jnp.sum(sums1[2]), jnp.sum(sums1[3]), jnp.sum(sums1[4]), jnp.sum(active)])
-    sums = [
-        sums1[0],
-        sums1[1],
-        placed(qkv_sums[0, :cols], cols),
-        placed(qkv_sums[0, 2 * cols :], cols),
-        sums2[0],
-        sums2[1],
-        sums2[2],
-        sums2[3],
-        placed(up_sums[0], ff_cols),
-        jnp.concatenate([squares, jnp.zeros((124,), F32)]),
-    ]
-    flat = sum_all(jnp.concatenate(sums).reshape(-1, 128)).reshape(-1)
-    totals = [flat[i * D : (i + 1) * D] for i in range(8)]
-    total_ub = flat[8 * D : 8 * D + FF]
-    total_squares = flat[8 * D + FF : 8 * D + FF + 4]
-
-    def own_share(vector):
-        width = vector.shape[0] // seq_count
-        return lax.dynamic_slice_in_dim(vector, seq_place * width, width, 0)
-
-    residual_rms = jnp.sqrt(total_squares[:3] / (total_squares[3] * D))
+    mine = lax.dynamic_slice_in_dim(sums, seq_place * own_d, own_d, 1)
+    residual_rms = jnp.sqrt(jnp.sum(sums[2:5], axis=1) / (sums[15, 0] * D))
     return (
         prefix_out[None],
         later_out[None],
         prefix_grad[None],
         later_grad[None],
-        own_share(totals[0]),
-        own_share(totals[1]),
+        mine[0],
+        mine[1],
         qkv_full,
-        own_share(totals[2]),
-        own_share(totals[3]),
+        mine[9],
+        mine[10],
         out_full,
-        own_share(totals[4]),
-        own_share(totals[5]),
-        own_share(totals[6]),
+        mine[5],
+        mine[6],
+        mine[7],
         up_full,
-        own_share(total_ub),
+        mine[11:15].reshape(-1),
         down_full,
-        own_share(totals[7]),
+        mine[8],
         residual_rms,
     )
 

time: 823 us -> 744 us (0.904); the launches traced: 817 us -> 730 us
  starting transfers between devices: 35.3 us -> 0 us
  Pallas kernels: 710 us -> 690 us
  local copies, waits for them, and re-layouts: 37.1 us -> 18.2 us
  waiting for transfers between devices: 9.89 us -> 0 us
    ppermute x17 -> x0, starting transfers between devices: 35.3 us -> none  [the longest x1 16.2 us: on_device(): lax.ppermute(fin_out, ('pre', 'seq'), [(b, a) for a, b in shuffle])]
    pallas_call x1, Pallas kernels: 341 us -> 317 us  [forward_pass(): pl.pallas_call(functools.partial(forward_kernel, (seq_size, pre_part, lat...]
    pallas_call x1, Pallas kernels: 123 us -> 136 us  [feed_back(): pl.pallas_call(functools.partial(feed_back_kernel, (seq_size, pre_part, l...]
    dynamic_slice x15 -> x0, local copies, waits for them, and re-layouts: 11.6 us -> none  [the longest x9 5.68 us: own_share(): return lax.dynamic_slice_in_dim(vector, seq_place * width, width, 0)]
    ppermute x17 -> x0, waiting for transfers between devices: 9.89 us -> none  [the longest x3 5.67 us: sum_all(): lax.ppermute(value, 'seq', [(i, i ^ mask) for i in range(size)])]
    pallas_call x1, Pallas kernels: 246 us -> 236 us  [attend_back(): pl.pallas_call(functools.partial(attend_back_kernel, (seq_size, pre_part,...]
    unnamed x59 -> x31, local copies, waits for them, and re-layouts: 16.2 us -> 6.8 us
  transfers between devices with their start and end apart: 17 -> 0, of which waited for: 3 -> 0; matrix products, arithmetic and copies ran while one was open for 5% -> 0% of each run, Pallas kernels for 0% -> 0%
where the time goes in v4:
time: 744 us; the launch traced here: 730 us
  Pallas kernels  690 us (93%)
  other arithmetic  19.8 us (3%)
  local copies, waits for them, and re-layouts  18.2 us (2%)
    pallas_call x1, Pallas kernels, forward_pass(): pl.pallas_call(functools.partial(forward_kernel, (seq_size, pre_part, lat...  317 us
    pallas_call x1, Pallas kernels, attend_back(): pl.pallas_call(functools.partial(attend_back_kernel, (seq_size, pre_part,...  236 us
    pallas_call x1, Pallas kernels, feed_back(): pl.pallas_call(functools.partial(feed_back_kernel, (seq_size, pre_part, l...  136 us

profile of v4, /device:TPU:5, one launch (start us, length us, event | category | flops | bytes accessed | tf_op | source)
XLA Modules:
  0.0 729.5 jit_solution(12040073535206791383)
XLA Ops:
  0.7 0.8 select_reduce_fusion
  1.5 0.7 compare_bitcast_fusion
  2.3 0.7 fusion.2
  3.1 0.8 reshape.212.active_ref
  4.5 1.1 broadcast_in_dim.68.codes_q
  5.6 0.7 reshape.209
  6.3 0.7 stack.24
  12.2 317.0 %forward_pass.1 = (bf16[2048,1536]{1,0:T(8,128)(2,1)}, bf16[512,2048]{1,0:T(8,128)(2,1)}, bf16[2048,2048]{1,0:T(8,128)(2,1)}, bf16[2048,2048]{1,0:T(8,128)(2,1)}...) custom-call(f32[16,256]{1,0:T(8,128)} %convert_element_type.30.small, ...), custom_call_target="tpu_custom_call" | custom-call | flops 32212254720 | bytes 33554432 | tf_op jit(solution)/shard_map/forward_pass/pallas_call | solution.py:777
  329.2 136.4 %feed_back.1 = (bf16[1024,2048]{1,0:T(8,128)(2,1)}, bf16[1024,2048]{1,0:T(8,128)(2,1)}, bf16[1024,2048]{1,0:T(8,128)(2,1)}, bf16[2048,2048]{1,0:T(8,128)(2,1)}, ...) custom-call(bf16[2048,2048]{1,0:T(8,128)(2,1)} %get-tuple-element.50, ...), custom_call_target="tpu_custom_call" | custom-call | flops 32212254720 | bytes 33554432 | tf_op jit(solution)/shard_map/feed_back/pallas_call | solution.py:1283
  465.5 236.3 %attend_back.1 = (bf16[1024,2048]{1,0:T(8,128)(2,1)}, bf16[1024,2048]{1,0:T(8,128)(2,1)}, bf16[1024,1536]{1,0:T(8,128)(2,1)}, bf16[256,2048]{1,0:T(8,128)(2,1)},...) custom-call(bf16[2048,1536]{1,0:T(8,128)(2,1)} %get-tuple-element.61, ...), custom_call_target="tpu_custom_call" | custom-call | flops 26843545600 | bytes 33554432 | tf_op jit(solution)/shard_map/attend_back/pallas_call | solution.py:1734
  701.8 1.2 slice.155
  703.7 1.0 slice_reduce_fusion
  705.2 2.7 broadcast_select_fusion.11
  707.8 0.8 copy-done
  709.0 7.0 maximum_convert_fusion
  716.0 1.6 maximum_convert_fusion.2
  717.6 1.0 copy-done.1
  719.3 3.4 convert_element_type.33
  722.7 1.6 fusion.3
  724.3 0.8 dynamic-slice_bitcast_fusion
  725.7 0.8 copy.64
  726.5 0.9 copy.65
  727.4 0.8 copy.66
  728.2 0.9 copy.67
  (48 shorter events, 8.3 us)
Async XLA Ops:
  705.2 3.4 copy-start
  709.0 7.0 copy-start.2
  715.9 2.6 copy-start.1
  719.3 6.4 copy-start.5
  719.3 7.2 copy-start.3
  719.3 8.1 %copy-start.6 = (bf16[128,2048]{1,0:T(8,128)(2,1)S(1)}, bf16[128,2048]{1,0:T(8,128)(2,1)}, u32[]{:S(2)}) copy-start(bf16[128,2048]{1,0:T(8,128)(2,1)} %get-tuple-element.75) | copy-start | bytes 1572868
  722.7 5.4 copy-start.4

commit v5 on v4

--- a/solution.py
+++ b/solution.py
@@ -830,133 +830,231 @@
 class Pool:
     def __init__(self, buffers, count):
         self.buffers, self.count = buffers, count
-        self.pending = [None] * count
+        self.pending = [Copies() for _ in range(count)]
         self.turn = 0
 
     def take(self):
         index = self.turn % self.count
         self.turn += 1
-        if self.pending[index] is not None:
-            self.pending[index].wait_send()
-            self.pending[index] = None
+        self.pending[index].drain()
+        self.pending[index] = Copies()
         return index
 
     def drain(self):
-        for copy in self.pending:
-            if copy is not None:
-                copy.wait_send()
+        for copies in self.pending:
+            copies.drain()
 
 
 class Reduce:
-    def __init__(self, grad, near, wide_land, rows, width, sems, work):
-        self.grad, self.near, self.wide_land = grad, near, wide_land
+    def __init__(self, grad, near, chain, tail, rows, width, sems, work, size, split=False):
+        self.grad, self.near, self.chain, self.tail = grad, near, chain, tail
         self.rows, self.width = rows, width
-        self.near_send, self.near_recv, self.wide_send, self.wide_recv = sems
-        self.left, self.right, self.total, self.out, self.pool, self.sem = work
+        self.early = early_rows(rows) if split else 0
+        self.first = rows - self.early
+        self.whole = rows + self.early
+        self.near_send, self.near_recv, self.chain_send, self.chain_recv, self.tail_sem = sems
+        self.left, self.right, self.third, self.fourth, self.out, self.pool, self.sem = work
         self.seq = lax.axis_index("seq")
-        self.sent = []
-
-    def block(self, mask):
-        return self.grad.at[rows_of(xor(self.seq, mask), self.rows), :]
-
-    def near_slot(self, mask):
-        return self.near.at[mask // 2 * self.rows : (mask // 2 + 1) * self.rows, :]
-
-    def wide_slot(self, mask):
-        return self.wide_land.at[mask // 2 * self.rows : (mask // 2 + 1) * self.rows, :]
-
-    def near_copy(self, mask):
+        self.lines = size // 2
+        self.line = lax.div(self.seq, jnp.int32(2))
+        self.side = lax.rem(self.seq, jnp.int32(2))
+        self.sent = Copies()
+
+    def target(self, turn):
+        if turn == self.lines - 1:
+            return self.line
+        return far_line(self.lines, self.line, jnp.int32(turn))
+
+    def block(self, line, other, first, count):
+        place = line * 2 + ((1 - self.side) if other else self.side)
+        return self.grad.at[pl.ds(pl.multiple_of(place * self.rows + first, 16), count), :]
+
+    def near_slot(self, line, near=None):
+        near = self.near if near is None else near
+        return near.at[pl.ds(pl.multiple_of(line * self.first, 16), self.first), :]
+
+    def chain_slot(self, slot):
+        return self.chain.at[pl.ds(pl.multiple_of(slot * self.whole, 16), self.whole), :]
+
+    def near_copy(self, turn):
+        line = self.target(turn)
         return remote(
-            self.block(mask + 1),
-            self.near_slot(mask),
-            self.near_send.at[mask // 2],
-            self.near_recv.at[mask // 2],
+            self.block(line, True, 0, self.first),
+            self.near_slot(line),
+            self.near_send.at[turn],
+            self.near_recv.at[line],
             seq=xor(self.seq, 1),
         )
 
-    def wide_copy(self, src, mask):
+    def chain_copy(self, src, turn, slot, to):
         return remote(
-            src,
-            self.wide_slot(mask),
-            self.wide_send.at[mask // 2],
-            self.wide_recv.at[mask // 2],
-            seq=xor(self.seq, mask),
+            src, self.chain_slot(slot), self.chain_send.at[turn], self.chain_recv.at[slot], seq=to
         )
 
-    def begin(self, *masks):
-        for mask in masks:
-            copy = self.near_copy(mask)
+    def begin(self, *turns):
+        for turn in turns:
+            self.sent.start(self.near_copy(turn))
+
+    def view(self, ref, first, count):
+        return ref.at[first : first + count, : self.width]
+
+    def load_own(self, line):
+        copies = [
+            pltpu.make_async_copy(
+                self.block(line, False, 0, self.rows), self.view(self.left, 0, self.rows), self.sem.at[0]
+            )
+        ]
+        if self.early:
+            copies.append(
+                pltpu.make_async_copy(
+                    self.block(line, True, self.first, self.early),
+                    self.view(self.left, self.rows, self.early),
+                    self.sem.at[1],
+                )
+            )
+        for copy in copies:
             copy.start()
-            self.sent.append(copy)
-
-    def views(self, index=None):
-        left = self.left.at[: self.rows, : self.width]
-        right = self.right.at[: self.rows, : self.width]
-        return left, right
-
-    def step(self, mask, early=None):
-        left, right = self.views()
-        own = pltpu.make_async_copy(self.block(mask), left, self.sem.at[0])
-        own.start()
-        if early is None:
-            self.near_copy(mask).wait_recv()
-            source = self.near_slot(mask)
+        return copies
+
+    def load(self, src, ref, count, sem):
+        copy = pltpu.make_async_copy(src, self.view(ref, 0, count), self.sem.at[sem])
+        copy.start()
+        return copy
+
+    def rows_loop(self, first, last, value, store):
+        if first == last:
+            return
+
+        @pl.loop(first // 16, last // 16)
+        def _(i):
+            at = (rows_of(i, 16), slice(0, self.width))
+            store(at, value(at))
+
+    def step(self, turn, when=None, early=None):
+        line = self.target(turn)
+        up = line > self.line
+        ahead = jnp.where(up, line - self.line, self.line - line)
+        base = jnp.where(up, 0, self.lines - 1)
+        more = jnp.where(up, self.line > 0, self.line < self.lines - 1)
+        slot_in = jnp.minimum(base + ahead, 2 * (self.lines - 1) - 1)
+        slot_out = base + ahead - 1
+        to = jnp.clip(self.seq + jnp.where(up, 2, -2), 0, 2 * self.lines - 1)
+        index = self.pool.take()
+        out = self.out.at[index]
+        leave = self.chain_copy(out.at[: self.whole, : self.width], turn, slot_out, to)
+
+        def store(at, value):
+            out[at] = value.astype(BF)
+
+        def body():
+            copies = self.load_own(line)
+            if early is None:
+                self.near_copy(turn).wait_recv()
+            copies.append(self.load(self.near_slot(line, early), self.right, self.first, 2))
+
+            def both(at):
+                return self.left[at].astype(F32) + self.right[at].astype(F32)
+
+            def own(at):
+                return self.left[at].astype(F32)
+
+            @pl.when(more)
+            def _():
+                self.chain_copy(out.at[: self.whole, : self.width], turn, slot_in, to).wait_recv()
+                third = self.load(self.chain_slot(slot_in), self.third, self.whole, 3)
+                for copy in (*copies, third):
+                    copy.wait()
+                self.rows_loop(
+                    0, self.first, lambda at: both(at) + self.third[at].astype(F32), store
+                )
+                self.rows_loop(
+                    self.first, self.whole, lambda at: own(at) + self.third[at].astype(F32), store
+                )
+
+            @pl.when(jnp.logical_not(more))
+            def _():
+                for copy in copies:
+                    copy.wait()
+                self.rows_loop(0, self.first, both, store)
+                self.rows_loop(self.first, self.whole, own, store)
+
+            leave.start()
+
+        if when is None:
+            body()
         else:
-            source = early.at[mask // 2 * self.rows : (mask // 2 + 1) * self.rows, :]
-        other = pltpu.make_async_copy(source, right, self.sem.at[1])
-        other.start()
+            pl.when(when)(body)
+        self.pool.pending[index].items.append((leave, when))
+
+    def sides(self):
+        return ((self.line > 0, 0), (self.line < self.lines - 1, self.lines - 1))
+
+    def settle(self):
+        self.near_copy(self.lines - 1).wait_recv()
+        for there, slot in self.sides():
+            pl.when(there)(
+                self.chain_copy(self.view(self.third, 0, self.whole), 0, slot, self.seq).wait_recv
+            )
+
+    def tail_copy(self, src):
+        return remote(src, self.tail, self.tail_sem.at[0], self.tail_sem.at[1], seq=xor(self.seq, 1))
+
+    def final(self, result):
+        copies = self.load_own(self.line)
+        copies.append(self.load(self.near_slot(self.line), self.right, self.first, 2))
+        side = jnp.where(self.line > 0, 0, self.lines - 1)
+        copies.append(self.load(self.chain_slot(side), self.third, self.whole, 3))
+        mid = (self.line > 0) & (self.line < self.lines - 1)
+        fourth = pltpu.make_async_copy(
+            self.chain_slot(self.lines - 1), self.view(self.fourth, 0, self.whole), self.sem.at[4]
+        )
+        pl.when(mid)(fourth.start)
         index = self.pool.take()
-        own.wait()
-        other.wait()
-        chunk = min(32, self.rows)
-
-        @pl.loop(0, self.rows // chunk)
+        out = self.out.at[index]
+
+        def put(at, value):
+            result[at] = value.astype(BF)
+
+        def put_tail(at, value):
+            out[at] = value.astype(BF)
+
+        def loops(refs):
+            def sum_of(at):
+                return functools.reduce(jnp.add, [ref[at].astype(F32) for ref in refs])
+
+            self.rows_loop(0, self.first, lambda at: sum_of(at) + self.right[at].astype(F32), put)
+            self.rows_loop(self.first, self.rows, sum_of, put)
+            self.rows_loop(self.rows, self.whole, sum_of, put_tail)
+
+        for copy in copies:
+            copy.wait()
+
+        @pl.when(mid)
+        def _():
+            fourth.wait()
+            loops((self.left, self.third, self.fourth))
+
+        pl.when(jnp.logical_not(mid))(lambda: loops((self.left, self.third)))
+        if self.early:
+            self.pool.pending[index].start(
+                self.tail_copy(out.at[self.rows : self.whole, : self.width])
+            )
+
+    def last(self, result):
+        if not self.early:
+            return
+        self.tail_copy(self.view(self.third, 0, self.early)).wait_recv()
+        self.load(self.tail, self.third, self.early, 3).wait()
+
+        @pl.loop(0, self.early // 16)
         def _(i):
-            at = (rows_of(i, chunk), slice(0, self.width))
-            value = self.left[at].astype(F32) + self.right[at].astype(F32)
-            self.out[index, at[0], at[1]] = value.astype(BF)
-
-        copy = self.wide_copy(self.out.at[index, : self.rows, : self.width], mask)
-        copy.start()
-        self.pool.pending[index] = copy
-
-    def settle(self, wide):
-        self.near_copy(0).wait_recv()
-        for mask in wide:
-            self.wide_copy(self.out.at[0, : self.rows, : self.width], mask).wait_recv()
-
-    def final(self, wide, result):
-        left, right = self.views()
-        chunk = min(32, self.rows)
-        local_copies([(self.block(0), left), (self.near_slot(0), right)], self.sem)
-        masks = list(wide)
-
-        @pl.loop(0, self.rows // chunk)
-        def _(i):
-            at = (rows_of(i, chunk), slice(0, self.width))
-            self.total[at] = self.left[at].astype(F32) + self.right[at].astype(F32)
-
-        while masks:
-            now, masks = masks[:2], masks[2:]
-            views = [(self.wide_slot(mask), view) for mask, view in zip(now, (left, right))]
-            local_copies(views, self.sem)
-            refs = (self.left, self.right)[: len(now)]
-            last = not masks
-
-            @pl.loop(0, self.rows // chunk)
-            def _(i):
-                at = (rows_of(i, chunk), slice(0, self.width))
-                value = self.total[at]
-                for ref in refs:
-                    value = value + ref[at].astype(F32)
-                if last:
-                    result[at] = value.astype(BF)
-                else:
-                    self.total[at] = value
+            lanes = slice(0, self.width)
+            rows = pl.ds(pl.multiple_of(self.first + i * 16, 16), 16)
+            value = result[rows, lanes].astype(F32) + self.third[rows_of(i, 16), lanes].astype(F32)
+            result[rows, lanes] = value.astype(BF)
 
     def drain(self):
-        for copy in self.sent:
-            copy.wait_send()
+        self.sent.drain()
 
 
 class Sum:
@@ -1035,7 +1133,7 @@
     active_ref,
     vectors,
     near_down,
-    wide_down,
+    chain_down,
     near_up,
     up_grad,
     dattn,
@@ -1063,13 +1161,13 @@
     ffn_far_v,
     left_v,
     right_v,
-    total_v,
+    third_v,
     out_v,
     grad_v,
     twin_send,
     twin_recv,
-    wide_send,
-    wide_recv,
+    chain_send,
+    chain_recv,
     early_send,
     early_recv,
     spread_send,
@@ -1084,33 +1182,41 @@
     ff_cols = w_up.shape[1]
     gain2 = vectors[5:6, :]
     wide = wide_masks(seq_size)
-    late = sorted(wide, key=lambda m: (m == 2, m))
+    lines = seq_size // 2
+    line = lax.div(lax.axis_index("seq"), jnp.int32(2))
+    end = (line == 0) | (line == lines - 1)
+    mid = jnp.logical_not(end)
+    turns = range(lines - 1)
     pool = Pool(out_v, 3)
-    work = (left_v, right_v, total_v, out_v, pool, local_sem.at[0:2])
+    work = (left_v, right_v, third_v, None, out_v, pool, local_sem.at[12:16])
     put_down = Reduce(
         down_grad,
         near_down,
-        wide_down,
+        chain_down,
+        None,
         D // seq_size,
         ff_cols,
-        (twin_send, twin_recv, wide_send, wide_recv),
+        (twin_send, twin_recv, chain_send, chain_recv, None),
         work,
+        seq_size,
     )
     put_up = Reduce(
         up_grad,
         near_up,
         None,
+        None,
         D // seq_size,
         ff_cols,
-        (early_send, early_recv, None, None),
+        (early_send, early_recv, None, None, None),
         work,
+        seq_size,
     )
     get_dattn = Spread(dattn_v, dattn, part, spread_send, spread_recv, local_sem.at[2])
     sum_f = Sum(terms_v, ffn_near_v, pass_v, ffn_far_v, sum_send.at[0], sum_recv.at[0])
     sum_dh2 = Sum(terms_v, near_v, pass_v, far_v, sum_send.at[1], sum_recv.at[1])
 
     greet((1, *wide))
-    put_down.begin(*late, 0)
+    put_down.begin(*turns, lines - 1)
     loads = [
         pltpu.make_async_copy(src, dst, local_sem.at[3 + i])
         for i, (src, dst) in enumerate(
@@ -1149,7 +1255,7 @@
     sum_f.run(f_term, keep_f)
     for load in loads[2:]:
         load.wait()
-    put_down.step(late[0])
+    put_down.step(0, end)
 
     @pl.loop(0, 4)
     def _(r):
@@ -1167,8 +1273,6 @@
     load_h2.start()
     for copy in sum_f.near_copies:
         copy.wait_send()
-    for mask in late[1:-1]:
-        put_down.step(mask)
     sum_f.far_copy.wait_send()
     load.wait()
 
@@ -1185,6 +1289,8 @@
         acc_v[rows, lanes] = value
 
     sum_dh2.run(dh2_term, keep_dh2)
+    put_down.step(1, end)
+    put_down.step(0, mid)
     load_h2.wait()
     columns_grad(
         lhs,
@@ -1194,9 +1300,9 @@
         grad_v,
         lambda rows: pltpu.make_async_copy(grad_v, up_grad.at[rows, :], local_sem.at[3]),
     )
-    put_up.begin(late[0])
-    if len(late) > 1:
-        put_down.step(late[-1])
+    put_up.begin(0)
+    for turn in turns[2:]:
+        put_down.step(turn, end)
     chunk = 32
     sum_f.far_copy.wait_recv()
 
@@ -1218,6 +1324,8 @@
     ]
     for save in saves:
         save.start()
+    for turn in turns[1:]:
+        put_down.step(turn, mid)
     sum_dh2.far_copy.wait_recv()
 
     @pl.loop(0, part // chunk)
@@ -1245,11 +1353,11 @@
         add_rows(up_sums, 0, du_v[rows_of(i, chunk), :].astype(F32))
 
     get_dattn.forward()
-    put_down.settle(wide)
+    put_down.settle()
     get_dattn.finish()
     for save in saves:
         save.wait()
-    put_up.near_copy(late[0]).wait_recv()
+    put_up.near_copy(0).wait_recv()
     for item in (put_down, put_up, get_dattn, sum_dh2, pool):
         item.drain()
 
@@ -1266,11 +1374,14 @@
     def out(shape, kind=BF):
         return jax.ShapeDtypeStruct(shape, kind)
 
-    half = seq_size // 2
+    lines = seq_size // 2
+    near_rows = lines * own_d
+    whole = own_d
+    chains = 2 * (lines - 1)
     outs = (
-        out((half * own_d, ff_cols)),
-        out((half * own_d, ff_cols)),
-        out((half * own_d, ff_cols)),
+        out((near_rows, ff_cols)),
+        out((chains * whole, ff_cols)),
+        out((near_rows, ff_cols)),
         out((D, ff_cols)),
         out((length, D)),
         out((part, D), F32),
@@ -1303,17 +1414,17 @@
             pltpu.VMEM((part, D), BF),
             pltpu.VMEM((2, part, D), BF),
             pltpu.VMEM((part, D), BF),
+            pltpu.VMEM((whole, ff_cols), BF),
             pltpu.VMEM((own_d, ff_cols), BF),
-            pltpu.VMEM((own_d, ff_cols), BF),
-            pltpu.VMEM((own_d, ff_cols), F32),
-            pltpu.VMEM((3, own_d, ff_cols), BF),
+            pltpu.VMEM((whole, ff_cols), BF),
+            pltpu.VMEM((3, whole, ff_cols), BF),
             pltpu.VMEM((256, ff_cols), BF),
-            dma((half,)),
-            dma((half,)),
-            dma((half,)),
-            dma((half,)),
-            dma((half,)),
-            dma((half,)),
+            dma((lines,)),
+            dma((lines,)),
+            dma((lines,)),
+            dma((chains,)),
+            dma((lines,)),
+            dma((lines,)),
             dma((4,)),
             dma((4,)),
             dma((2, 3)),
@@ -1386,7 +1497,7 @@
     up_grad,
     down_grad,
     near_down,
-    wide_down,
+    chain_down,
     early_up,
     prefix_in,
     later_in,
@@ -1402,12 +1513,16 @@
     fin_up,
     fin_qkv,
     fin_out,
+    tail_down,
     near_up,
-    wide_up,
+    chain_up,
+    tail_up,
     near_out,
-    wide_out,
+    chain_out,
+    tail_out,
     near_qkv,
-    wide_qkv,
+    chain_qkv,
+    tail_qkv,
     out_grad,
     qkv_grad,
     prefix_grad,
@@ -1433,7 +1548,8 @@
     far_v,
     left_v,
     right_v,
-    total_v,
+    third_v,
+    fourth_v,
     out_v,
     grad_v,
     res_down,
@@ -1448,8 +1564,9 @@
     relay_sem,
     twin_send,
     twin_recv,
-    wide_send,
-    wide_recv,
+    chain_send,
+    chain_recv,
+    tail_sem,
     spread_send,
     spread_recv,
     sum_send,
@@ -1466,18 +1583,23 @@
     own_o = cols // seq_size
     pre = lax.axis_index("pre")
     wide = wide_masks(seq_size)
-    late = sorted(wide, key=lambda m: (m == 2, m))
+    lines = seq_size // 2
+    line = lax.div(lax.axis_index("seq"), jnp.int32(2))
+    end = (line == 0) | (line == lines - 1)
+    mid = jnp.logical_not(end)
+    turns = range(lines - 1)
     pool = Pool(out_v, 3)
-    work = (left_v, right_v, total_v, out_v, pool, local_sem.at[0:2])
-
-    def reduce_of(i, grad, near, wide_land, rows, columns):
-        sems = (twin_send.at[i], twin_recv.at[i], wide_send.at[i], wide_recv.at[i])
-        return Reduce(grad, near, wide_land, rows, columns, sems, work)
-
-    put_down = reduce_of(0, down_grad, near_down, wide_down, own_d, ff_cols)
-    put_up = reduce_of(0, up_grad, near_up, wide_up, own_d, ff_cols)
-    put_out = reduce_of(1, out_grad, near_out, wide_out, own_o, D)
-    put_qkv = reduce_of(2, qkv_grad, near_qkv, wide_qkv, own_d, width)
+    work = (left_v, right_v, third_v, fourth_v, out_v, pool, local_sem.at[24:29])
+
+    def reduce_of(i, grad, near, chain, tail, rows, columns, split=False):
+        j = max(i, 1) - 1
+        sems = (twin_send.at[j], twin_recv.at[j], chain_send.at[j], chain_recv.at[j], tail_sem.at[i])
+        return Reduce(grad, near, chain, tail, rows, columns, sems, work, seq_size, split)
+
+    put_down = reduce_of(0, down_grad, near_down, chain_down, tail_down, own_d, ff_cols)
+    put_up = reduce_of(1, up_grad, near_up, chain_up, tail_up, own_d, ff_cols)
+    put_out = reduce_of(2, out_grad, near_out, chain_out, tail_out, own_o, D)
+    put_qkv = reduce_of(3, qkv_grad, near_qkv, chain_qkv, tail_qkv, own_d, width)
 
     def spread_of(i, own, land):
         return Spread(own, land, own_d, spread_send.at[i], spread_recv.at[i], local_sem.at[2 + i])
@@ -1495,7 +1617,7 @@
     )
     bits = [1 << i for i in range(seq_size.bit_length() - 1)]
     greet(sorted({*wide, *bits}), relay)
-    put_up.begin(*late[1:])
+    put_up.begin(*turns[1:])
     stages = [
         remote(sums, sums_land.at[i], total_send.at[i], total_recv.at[i], **target)
         for i, target in enumerate(
@@ -1538,8 +1660,8 @@
     )
     sums[...] = jnp.zeros_like(sums)
     qkv_sums[...] = jnp.zeros_like(qkv_sums)
-    put_up.step(late[0], early_up)
-    put_down.final(wide, res_down)
+    put_up.step(0, end, early_up)
+    put_down.final(res_down)
     get_down.begin()
     def keep(rows, lanes, value):
         acc_v[rows, lanes] = value
@@ -1569,8 +1691,9 @@
         grad_v,
         lambda rows: pltpu.make_async_copy(grad_v.at[:, :D], out_grad.at[rows, :], local_sem.at[5]),
     )
-    put_out.begin(*late, 0)
-    put_up.begin(0)
+    put_out.begin(*turns)
+    put_up.begin(lines - 1)
+    put_out.begin(lines - 1)
     loads = load_all(5, (w_qkv, wbuf.at[:, :width]))
     for r in range(4):
         head_rows, tail_rows = position_rows(jnp.int32(r))
@@ -1598,15 +1721,15 @@
                 dqkv_v,
             )
 
-    for mask in late[1:-1]:
-        put_up.step(mask)
+    put_up.step(0, mid, early_up)
     attention(0, pairs // 2)
-    if len(late) > 1:
-        put_up.step(late[-1])
+    put_up.step(1, end)
+    attention(pairs // 2, pairs)
+    for turn in turns[2:]:
+        put_up.step(turn, end)
+    for turn in turns[1:]:
+        put_up.step(turn, mid)
     get_down.forward()
-    attention(pairs // 2, pairs)
-    for mask in late:
-        put_out.step(mask)
     wait_all(loads)
     columns_grad(
         lhs,
@@ -1618,8 +1741,10 @@
             grad_v.at[:, :width], qkv_grad.at[rows, :], local_sem.at[5]
         ),
     )
-    put_qkv.begin(*late, 0)
+    put_qkv.begin(*turns, lines - 1)
     get_down.finish()
+    for turn in turns:
+        put_out.step(turn, end)
 
     def dh1_term(r, store):
         head_rows, tail_rows = position_rows(jnp.int32(r))
@@ -1636,10 +1761,15 @@
     def _(i):
         add_rows(qkv_sums, 0, dqkv_v[rows_of(i, chunk), :].astype(F32))
 
-    put_up.settle(wide)
-    put_up.final(wide, res_up)
+    put_qkv.step(0, end)
+    for turn in turns:
+        put_out.step(turn, mid)
+    put_up.settle()
+    put_up.final(res_up)
+    put_qkv.step(1, end)
+    put_up.last(res_up)
     get_up.begin()
-    put_qkv.step(late[0])
+    put_qkv.step(0, mid)
     sum_dh1.far_copy.wait_recv()
 
     @pl.loop(0, part // chunk)
@@ -1670,19 +1800,23 @@
         )
     sums[15:16, :] = jnp.zeros((1, D), F32) + jnp.sum(active_ref[...])
     stages[0].start()
-    put_out.settle(wide)
-    put_out.final(wide, res_out)
-    relay.begin(*relayed)
+    for turn in turns[2:]:
+        put_qkv.step(turn, end)
+    put_out.settle()
+    put_out.final(res_out)
     add_stage(0)
     wait_all(saves)
-    for mask in late[1:]:
-        put_qkv.step(mask)
+    put_out.last(res_out)
+    relay.begin(*relayed)
+    for turn in turns[1:]:
+        put_qkv.step(turn, mid)
     add_stage(1, False)
     get_up.forward()
     relay.finish(*relayed)
     get_out.begin()
-    put_qkv.settle(wide)
-    put_qkv.final(wide, res_qkv)
+    put_qkv.settle()
+    put_qkv.final(res_qkv)
+    put_qkv.last(res_qkv)
     get_qkv.begin()
     stages[2].start()
     get_out.forward()
@@ -1704,7 +1838,18 @@
     ff_cols = FF // 4
     own_d = D // seq_size
     own_o = cols // seq_size
-    half = seq_size // 2
+    lines = seq_size // 2
+    chains = 2 * (lines - 1)
+    early_d, early_o = 0, 0
+    least = 16
+
+    def landings(rows, early, columns):
+        return (
+            out((lines * (rows - early), columns)),
+            out((chains * (rows + early), columns)),
+            out((max(early, least), columns)),
+        )
+
     hbm = pl.BlockSpec(memory_space=pl.ANY)
     vmem = pl.BlockSpec(memory_space=pltpu.VMEM)
 
@@ -1716,12 +1861,10 @@
         out((4 * own_d, ff_cols)),
         out((4 * own_d, width)),
         out((4 * own_o, D)),
-        out((half * own_d, ff_cols)),
-        out((half * own_d, ff_cols)),
-        out((half * own_o, D)),
-        out((half * own_o, D)),
-        out((half * own_d, width)),
-        out((half * own_d, width)),
+        out((max(early_d, least), ff_cols)),
+        *landings(own_d, early_d, ff_cols),
+        *landings(own_o, early_o, D),
+        *landings(own_d, 0, width),
         out((cols, D)),
         out((D, width)),
         out((pre_part, D)),
@@ -1735,7 +1878,7 @@
         functools.partial(attend_back_kernel, (seq_size, pre_part, later_part)),
         out_shape=outs,
         in_specs=[hbm] * 17 + [vmem] * (len(operands) - 17),
-        out_specs=[hbm] * 14 + [vmem],
+        out_specs=[hbm] * (len(outs) - 1) + [vmem],
         scratch_shapes=[
             pltpu.VMEM((D, most), BF),
             pltpu.VMEM((length, D), BF),
@@ -1755,10 +1898,11 @@
             pltpu.VMEM((2, part, D), BF),
             pltpu.VMEM((part, D), BF),
             pltpu.VMEM((part, D), BF),
+            pltpu.VMEM((own_d + early_d, most), BF),
             pltpu.VMEM((own_d, most), BF),
-            pltpu.VMEM((own_d, most), BF),
-            pltpu.VMEM((own_d, most), F32),
-            pltpu.VMEM((3, own_d, most), BF),
+            pltpu.VMEM((own_d + early_d, most), BF),
+            pltpu.VMEM((own_d + early_d, most), BF),
+            pltpu.VMEM((3, own_d + early_d, most), BF),
             pltpu.VMEM((256, most), BF),
             pltpu.VMEM((own_d, ff_cols), BF),
             pltpu.VMEM((own_d, ff_cols), BF),
@@ -1770,15 +1914,16 @@
             dma((stages,)),
             dma((stages,)),
             dma((3,)),
-            dma((3, half)),
-            dma((3, half)),
-            dma((3, half)),
-            dma((3, half)),
+            dma((3, lines)),
+            dma((3, lines)),
+            dma((3, lines)),
+            dma((3, chains)),
+            dma((4, 2)),
             dma((4, 4)),
             dma((4, 4)),
             dma((3,)),
             dma((3,)),
-            dma((24,)),
+            dma((29,)),
         ],
         compiler_params=pltpu.CompilerParams(
             collective_id=2, has_side_effects=True, vmem_limit_bytes=63 * 2**20
@@ -1877,7 +2022,7 @@
     )
 
     rows_in = (prefix_in[0], later_in[0], prefix_cot[0], later_cot[0], active)
-    (near_down, wide_down, early_up, up_grad, dattn, middle_grad, prefix_out, later_out, feed_sums, up_sums) = feed_back(
+    (near_down, chain_down, early_up, up_grad, dattn, middle_grad, prefix_out, later_out, feed_sums, up_sums) = feed_back(
         seq_count,
         pre_part,
         later_part,
@@ -1907,7 +2052,7 @@
         up_grad,
         down_grad,
         near_down,
-        wide_down,
+        chain_down,
         early_up,
         *rows_in,
         vectors,

time: 744 us -> 710 us (0.954)
  Pallas kernels: 690 us -> 658 us
    pallas_call x1, Pallas kernels: 236 us -> 208 us  [attend_back(): pl.pallas_call(functools.partial(attend_back_kernel, (seq_size, pre_part,...]
where the time goes in v5:
time: 710 us; the launch traced here: 699 us
  Pallas kernels  658 us (93%)
  local copies, waits for them, and re-layouts  19.6 us (3%)
  other arithmetic  19.3 us (3%)
    pallas_call x1, Pallas kernels, forward_pass(): pl.pallas_call(functools.partial(forward_kernel, (seq_size, pre_part, lat...  317 us
    pallas_call x1, Pallas kernels, attend_back(): pl.pallas_call(functools.partial(attend_back_kernel, (seq_size, pre_part,...  208 us
    pallas_call x1, Pallas kernels, feed_back(): pl.pallas_call(functools.partial(feed_back_kernel, (seq_size, pre_part, l...  134 us

profile of v5, /device:TPU:5, one launch (start us, length us, event | category | flops | bytes accessed | tf_op | source)
XLA Modules:
  0.0 699.1 jit_solution(1230636936016381560)
XLA Ops:
  0.7 0.7 stack.24
  5.9 0.7 reshape.209
  7.3 0.8 select_reduce_fusion
  8.2 0.7 compare_bitcast_fusion
  8.9 0.7 fusion.2
  9.7 0.8 reshape.212.active_ref
  10.5 1.1 broadcast_in_dim.68.codes_q
  12.2 316.9 %forward_pass.1 = (bf16[2048,1536]{1,0:T(8,128)(2,1)}, bf16[512,2048]{1,0:T(8,128)(2,1)}, bf16[2048,2048]{1,0:T(8,128)(2,1)}, bf16[2048,2048]{1,0:T(8,128)(2,1)}...) custom-call(f32[16,256]{1,0:T(8,128)} %convert_element_type.30.small, ...), custom_call_target="tpu_custom_call" | custom-call | flops 32212254720 | bytes 33554432 | tf_op jit(solution)/shard_map/forward_pass/pallas_call | solution.py:777
  329.1 133.8 %feed_back.1 = (bf16[1024,2048]{1,0:T(8,128)(2,1)}, bf16[1536,2048]{1,0:T(8,128)(2,1)}, bf16[1024,2048]{1,0:T(8,128)(2,1)}, bf16[2048,2048]{1,0:T(8,128)(2,1)}, ...) custom-call(bf16[2048,2048]{1,0:T(8,128)(2,1)} %get-tuple-element.50, ...), custom_call_target="tpu_custom_call" | custom-call | flops 32212254720 | bytes 33554432 | tf_op jit(solution)/shard_map/feed_back/pallas_call | solution.py:1394
  462.9 207.6 %attend_back.1 = (bf16[1024,2048]{1,0:T(8,128)(2,1)}, bf16[1024,2048]{1,0:T(8,128)(2,1)}, bf16[1024,1536]{1,0:T(8,128)(2,1)}, bf16[256,2048]{1,0:T(8,128)(2,1)},...) custom-call(bf16[2048,1536]{1,0:T(8,128)(2,1)} %get-tuple-element.61, ...), custom_call_target="tpu_custom_call" | custom-call | flops 26843545600 | bytes 33554432 | tf_op jit(solution)/shard_map/attend_back/pallas_call | solution.py:1877
  670.5 1.6 fusion.3
  672.1 2.1 broadcast_select_fusion.20
  674.6 3.4 convert_element_type.33
  678.2 1.6 maximum_convert_fusion.2
  679.7 1.3 copy-done.1
  681.4 1.8 copy-done
  683.6 7.0 maximum_convert_fusion
  690.5 0.8 dynamic-slice_bitcast_fusion
  692.0 1.0 slice_reduce_fusion
  693.0 1.2 slice.155
  695.3 0.8 copy.64
  696.1 0.9 copy.65
  697.0 0.8 copy.66
  697.8 0.9 copy.67
  (48 shorter events, 8.4 us)
Async XLA Ops:
  674.6 3.5 copy-start.2
  678.1 2.9 copy-start.1
  681.0 2.2 copy-start
  683.6 11.8 %copy-start.5 = (bf16[128,2048]{1,0:T(8,128)(2,1)S(1)}, bf16[128,2048]{1,0:T(8,128)(2,1)}, u32[]{:S(2)}) copy-start(bf16[128,2048]{1,0:T(8,128)(2,1)} %get-tuple-element.59) | copy-start | bytes 1572868
  683.6 12.6 %copy-start.3 = (bf16[192,2048]{1,0:T(8,128)(2,1)S(1)}, bf16[192,2048]{1,0:T(8,128)(2,1)}, u32[]{:S(2)}) copy-start(bf16[192,2048]{1,0:T(8,128)(2,1)} %get-tuple-element.60) | copy-start | bytes 2359300
  683.6 13.4 %copy-start.6 = (bf16[128,2048]{1,0:T(8,128)(2,1)S(1)}, bf16[128,2048]{1,0:T(8,128)(2,1)}, u32[]{:S(2)}) copy-start(bf16[128,2048]{1,0:T(8,128)(2,1)} %get-tuple-element.75) | copy-start | bytes 1572868
  690.5 7.3 %copy-start.4 = (bf16[192,2048]{1,0:T(8,128)(2,1)S(1)}, bf16[192,2048]{1,0:T(8,128)(2,1)}, u32[]{:S(2)}) copy-start(bf16[192,2048]{1,0:T(8,128)(2,1)} %get-tuple-element.76) | copy-start | bytes 2359300

commit v6 on v5

--- a/solution.py
+++ b/solution.py
@@ -251,19 +251,40 @@
             spare = self.lines + (0 if up else 1)
             self.sent.start(self.copy(self.twin, 1, spare, self.line, to), there)
 
-    def event(self, turn):
+    def event(self, turn, when=None):
         line = far_line(self.lines, self.line, jnp.int32(self.lines - 2 - turn))
         step = jnp.where(line < self.line, 2, -2)
         after = jnp.where(line < self.line, self.line < self.lines - 1, self.line > 0)
         place = line * 2 + lax.rem(self.seq, jnp.int32(2))
         other = xor(place, 1)
         to = jnp.clip(self.seq + step, 0, 2 * self.lines - 1)
-        self.copy(place, 0, line, line, self.twin).wait_recv()
-        self.sent.start(self.copy(place, 0, line, line, to), after)
-        self.sent.start(self.copy(place, 2, line, line, self.twin))
-        if self.early:
-            self.copy(other, 1, line, line, self.twin).wait_recv()
-            self.sent.start(self.copy(other, 1, line, line, to), after)
+        onward = self.copy(place, 0, line, line, to)
+        aside = self.copy(place, 2, line, line, self.twin)
+        both = self.copy(other, 1, line, line, to) if self.early else None
+
+        def body():
+            self.copy(place, 0, line, line, self.twin).wait_recv()
+            pl.when(after)(onward.start)
+            aside.start()
+            if both is not None:
+                self.copy(other, 1, line, line, self.twin).wait_recv()
+                pl.when(after)(both.start)
+
+        if when is None:
+            body()
+        else:
+            pl.when(when)(body)
+            after = after & when
+        self.sent.items += [(onward, after), (aside, when)]
+        if both is not None:
+            self.sent.items.append((both, after))
+
+    def poll(self, turn):
+        last = self.lines - 2
+        end = (self.line == 0) | (self.line == self.lines - 1)
+        self.event(turn, end if turn else None)
+        if turn < last:
+            self.event(turn + 1, jnp.logical_not(end))
 
     def finish(self):
         self.local.wait()
@@ -554,7 +575,7 @@
     turns = range(seq_size // 2 - 1)
     get_qkv.rest()
     for turn in turns:
-        get_qkv.event(turn)
+        get_qkv.poll(turn)
         if turn == 0:
             relay.finish(*relayed)
             get_out.begin()
@@ -590,7 +611,7 @@
     save_qkv = pltpu.make_async_copy(qkv_v, qkv, local_sem.at[13])
     save_qkv.start()
     for turn in turns:
-        get_out.event(turn)
+        get_out.poll(turn)
     get_up.rest()
     get_df.finish()
     pairs = cols // 128
@@ -601,7 +622,7 @@
             attend_pair(pair, cols, qkv_v, codes_q[...], codes_k[...], mixed_v, stats_v)
 
     attention(0, pairs // 2)
-    get_up.event(0)
+    get_up.poll(0)
     get_down.begin()
     attention(pairs // 2, pairs)
     save_stats = pltpu.make_async_copy(stats_v, stats, local_sem.at[14])
@@ -667,7 +688,7 @@
         moves.append((mixed_v.at[tail_rows, :], mixed.at[r * part + pre_part : (r + 1) * part, :]))
     local_copies(moves, local_sem.at[16:24])
     for turn in turns[1:]:
-        get_up.event(turn)
+        get_up.poll(turn)
     far.wait_recv()
 
     @pl.loop(0, part // chunk)
@@ -703,9 +724,11 @@
             slope_v[rows, lanes] = (cumulative + upper * density).astype(BF)
 
     pl.loop(0, 2)(up_rows)
+    get_down.poll(0)
     get_h2.forward()
-    get_down.event(0)
     get_h2.finish_far()
+    for turn in turns[1:-1]:
+        get_down.poll(turn)
     half = slice(2 * part, 4 * part)
     local_copies([(h2.at[half, :], lhs.at[half, :])], local_sem.at[8:9])
     pl.loop(2, 4)(up_rows)
@@ -716,8 +739,7 @@
     ]
     for save in saves:
         save.start()
-    for turn in turns[1:-1]:
-        get_down.event(turn)
+    get_down.poll(turns[-1])
     local_copies([(df, lhs)], local_sem.at[9:10])
 
     @pl.loop(0, D // 256)
@@ -733,7 +755,6 @@
         save.start()
         save.wait()
 
-    get_down.event(turns[-1])
     get_down.finish()
     for save in (*saves, save_qkv, save_stats, save_attn):
         save.wait()
@@ -1937,12 +1958,57 @@
     )(*operands)
 
 
-def absolute_pre(blocks, place):
-    first = place % 2 == 0
-    low = place < 2
-    a = [jnp.where(first, blocks[0], blocks[1]), jnp.where(first, blocks[1], blocks[0])]
-    b = [jnp.where(first, blocks[2], blocks[3]), jnp.where(first, blocks[3], blocks[2])]
-    return [jnp.where(low, u, w) for u, w in zip(a, b)] + [jnp.where(low, w, u) for u, w in zip(a, b)]
+def assemble_kernel(place_ref, down, up, qkv, out, down_full, up_full, qkv_full, out_full):
+    qkv_full[...] = qkv[...].astype(F32)
+
+    @pl.when(pl.program_id(1) == 0)
+    def _():
+        down_full[...] = down[...].astype(F32)
+        up_full[...] = up[...].astype(F32)
+        out_full[...] = out[...].astype(F32)
+
+
+def assemble(place, down, up, qkv, out):
+    rows, ff_cols = down.shape[0] // 4, down.shape[1]
+    cols = qkv.shape[1] // 3
+    out_rows = out.shape[0] // 4
+
+    def member(slot, place_ref):
+        return jnp.bitwise_xor(slot, place_ref[0])
+
+    wide_in = pl.BlockSpec((rows, ff_cols), lambda slot, third, p: (slot, 0))
+    wide_out = pl.BlockSpec((rows, ff_cols), lambda slot, third, p: (0, member(slot, p)))
+    return pl.pallas_call(
+        assemble_kernel,
+        out_shape=(
+            jax.ShapeDtypeStruct((rows, 4 * ff_cols), F32),
+            jax.ShapeDtypeStruct((rows, 4 * ff_cols), F32),
+            jax.ShapeDtypeStruct((rows, 12 * cols), F32),
+            jax.ShapeDtypeStruct((4 * out_rows, out.shape[1]), F32),
+        ),
+        grid_spec=pltpu.PrefetchScalarGridSpec(
+            num_scalar_prefetch=1,
+            grid=(4, 3),
+            in_specs=[
+                wide_in,
+                wide_in,
+                pl.BlockSpec((rows, cols), lambda slot, third, p: (slot, third)),
+                pl.BlockSpec((out_rows, out.shape[1]), lambda slot, third, p: (slot, 0)),
+            ],
+            out_specs=[
+                wide_out,
+                wide_out,
+                pl.BlockSpec(
+                    (rows, cols), lambda slot, third, p: (0, third * 4 + member(slot, p))
+                ),
+                pl.BlockSpec(
+                    (out_rows, out.shape[1]), lambda slot, third, p: (member(slot, p), 0)
+                ),
+            ],
+        ),
+        compiler_params=pltpu.CompilerParams(vmem_limit_bytes=62 * 2**20),
+        name="assemble",
+    )(place, down, up, qkv, out)
 
 
 def on_device(
@@ -1977,24 +2043,21 @@
     own_d = D // seq_count
     cols = D // parts
 
-    small = jnp.concatenate(
-        [
-            jnp.stack(
-                [
-                    first_gain,
-                    first_bias,
-                    query_bias,
-                    value_bias,
-                    out_bias,
-                    second_gain,
-                    second_bias,
-                    down_bias,
-                ]
-            ),
-            up_bias.reshape(4, own_d),
-            jnp.zeros((4, own_d), BF),
-        ]
-    ).astype(F32)
+    vectors_in = [
+        first_gain,
+        first_bias,
+        query_bias,
+        value_bias,
+        out_bias,
+        second_gain,
+        second_bias,
+        down_bias,
+    ] + [up_bias[k * own_d : (k + 1) * own_d] for k in range(4)]
+    row = lax.broadcasted_iota(jnp.int32, (16, own_d), 0)
+    small = jnp.zeros((16, own_d), F32)
+    for i, vector in enumerate(vectors_in):
+        small = jnp.where(row == i, vector.astype(F32)[None, :], small)
+
     doc_id, live = token_tables(doc_lengths, doc_exit, token_skip)
     live_here = lax.dynamic_slice_in_dim(live[0], place * later_part, later_part, 0)
     active = jnp.concatenate([jnp.ones((pre_part,), F32), live_here.astype(F32)])[:, None]
@@ -2062,18 +2125,9 @@
         codes_k,
     )
 
-    def shared(blocks):
-        rows = blocks.shape[0] // parts
-        return absolute_pre([blocks[i * rows : (i + 1) * rows] for i in range(parts)], place)
-
-    down_full = jnp.concatenate(shared(fin_down), axis=1).astype(F32)
-    up_full = jnp.concatenate(shared(fin_up), axis=1).astype(F32)
-    out_full = jnp.concatenate(shared(fin_out), axis=0).astype(F32)
-    qkv_blocks = shared(fin_qkv)
-    qkv_full = jnp.concatenate(
-        [block[:, i * cols : (i + 1) * cols] for i in range(3) for block in qkv_blocks], axis=1
-    ).astype(F32)
-
+    down_full, up_full, qkv_full, out_full = assemble(
+        place.reshape(1).astype(jnp.int32), fin_down, fin_up, fin_qkv, fin_out
+    )
     mine = lax.dynamic_slice_in_dim(sums, seq_place * own_d, own_d, 1)
     residual_rms = jnp.sqrt(jnp.sum(sums[2:5], axis=1) / (sums[15, 0] * D))
     return (

time: 710 us -> 691 us (0.973)
  local copies, waits for them, and re-layouts: 19.6 us -> 10.2 us
  other arithmetic: 19.3 us -> 10.7 us
    pallas_call x1, Pallas kernels: 317 us -> 287 us  [forward_pass(): pl.pallas_call(functools.partial(forward_kernel, (seq_size, pre_part, lat...]
    pallas_call x0 -> x1, Pallas kernels: none -> 16.5 us  [assemble(): pl.pallas_call(assemble_kernel, out_shape=(jax.ShapeDtypeStruct((rows, 4...]
    pallas_call x1, Pallas kernels: 134 us -> 149 us  [feed_back(): pl.pallas_call(functools.partial(feed_back_kernel, (seq_size, pre_part, l...]
where the time goes in v6:
time: 691 us; the launch traced here: 681 us
  Pallas kernels  659 us (95%)
  other arithmetic  10.7 us (2%)
  local copies, waits for them, and re-layouts  10.2 us (1%)
    pallas_call x1, Pallas kernels, forward_pass(): pl.pallas_call(functools.partial(forward_kernel, (seq_size, pre_part, lat...  287 us
    pallas_call x1, Pallas kernels, attend_back(): pl.pallas_call(functools.partial(attend_back_kernel, (seq_size, pre_part,...  206 us
    pallas_call x1, Pallas kernels, feed_back(): pl.pallas_call(functools.partial(feed_back_kernel, (seq_size, pre_part, l...  149 us
    pallas_call x1, Pallas kernels, assemble(): pl.pallas_call(assemble_kernel, out_shape=(jax.ShapeDtypeStruct((rows, 4...  16.5 us

profile of v6, /device:TPU:5, one launch (start us, length us, event | category | flops | bytes accessed | tf_op | source)
XLA Modules:
  0.0 681.2 jit_solution(17864334642397552745)
XLA Ops:
  0.7 0.7 convert_element_type.62
  1.3 0.7 convert_element_type.61
  2.0 0.7 convert_element_type.60
  2.6 0.7 convert_element_type.59
  3.3 0.7 convert_element_type.58
  5.9 0.8 slice_convert_fusion.3
  6.8 0.7 select_select_fusion.small
  7.5 0.8 select_reduce_fusion
  8.4 0.7 compare_bitcast_fusion
  9.1 0.7 fusion.2
  10.0 0.8 reshape.224.active_ref
  10.8 1.1 broadcast_in_dim.155.codes_q
  12.4 287.2 %forward_pass.1 = (bf16[2048,1536]{1,0:T(8,128)(2,1)}, bf16[512,2048]{1,0:T(8,128)(2,1)}, bf16[2048,2048]{1,0:T(8,128)(2,1)}, bf16[2048,2048]{1,0:T(8,128)(2,1)}...) custom-call(f32[16,256]{1,0:T(8,128)} %select_select_fusion.small, ...), custom_call_target="tpu_custom_call" | custom-call | flops 32212254720 | bytes 33554432 | tf_op jit(solution)/shard_map/forward_pass/pallas_call | solution.py:798
  299.6 148.7 %feed_back.1 = (bf16[1024,2048]{1,0:T(8,128)(2,1)}, bf16[1536,2048]{1,0:T(8,128)(2,1)}, bf16[1024,2048]{1,0:T(8,128)(2,1)}, bf16[2048,2048]{1,0:T(8,128)(2,1)}, ...) custom-call(bf16[2048,2048]{1,0:T(8,128)(2,1)} %get-tuple-element.54, ...), custom_call_target="tpu_custom_call" | custom-call | flops 32212254720 | bytes 33554432 | tf_op jit(solution)/shard_map/feed_back/pallas_call | solution.py:1415
  448.3 206.3 %attend_back.1 = (bf16[1024,2048]{1,0:T(8,128)(2,1)}, bf16[1024,2048]{1,0:T(8,128)(2,1)}, bf16[1024,1536]{1,0:T(8,128)(2,1)}, bf16[256,2048]{1,0:T(8,128)(2,1)},...) custom-call(bf16[2048,1536]{1,0:T(8,128)(2,1)} %get-tuple-element.65, ...), custom_call_target="tpu_custom_call" | custom-call | flops 26843545600 | bytes 33554432 | tf_op jit(solution)/shard_map/attend_back/pallas_call | solution.py:1898
  654.7 1.6 fusion.3
  656.3 16.5 %assemble.1 = (f32[256,8192]{1,0:T(8,128)}, f32[256,8192]{1,0:T(8,128)}, f32[256,6144]{1,0:T(8,128)}, f32[256,2048]{1,0:T(8,128)}) custom-call(s32[1]{0:T(128)} %bitcast.12.place_ref, bf16[1024,2048]{1,0:T(8,128)(2,1)} %get-tuple-element.82.down, bf16[1024,2048]{1,0:T(8,128)(2,1)} %get-tuple-element.83.up, bf16[1024,1536]{1,0:T(8,128)(2,1)} %get-tuple-element.84.qkv, ...), custom_call_target="tpu_custom_call" | custom-call | tf_op jit(solution)/shard_map/assemble/pallas_call | solution.py:1981
  672.8 0.8 dynamic-slice_bitcast_fusion
  674.3 1.0 slice_reduce_fusion
  675.3 1.2 slice.59
  677.6 0.8 copy.53
  678.4 0.9 copy.54
  679.3 0.8 copy.55
  680.1 0.9 copy.56
  (28 shorter events, 4.0 us)
Async XLA Ops:
  656.3 21.3 %copy-start.2 = (bf16[128,2048]{1,0:T(8,128)(2,1)S(1)}, bf16[128,2048]{1,0:T(8,128)(2,1)}, u32[]{:S(2)}) copy-start(bf16[128,2048]{1,0:T(8,128)(2,1)} %get-tuple-element.63) | copy-start | bytes 1572868
  656.3 22.1 %copy-start = (bf16[192,2048]{1,0:T(8,128)(2,1)S(1)}, bf16[192,2048]{1,0:T(8,128)(2,1)}, u32[]{:S(2)}) copy-start(bf16[192,2048]{1,0:T(8,128)(2,1)} %get-tuple-element.64) | copy-start | bytes 2359300
  656.3 23.0 %copy-start.3 = (bf16[128,2048]{1,0:T(8,128)(2,1)S(1)}, bf16[128,2048]{1,0:T(8,128)(2,1)}, u32[]{:S(2)}) copy-start(bf16[128,2048]{1,0:T(8,128)(2,1)} %get-tuple-element.79) | copy-start | bytes 1572868
  672.8 7.3 %copy-start.1 = (bf16[192,2048]{1,0:T(8,128)(2,1)S(1)}, bf16[192,2048]{1,0:T(8,128)(2,1)}, u32[]{:S(2)}) copy-start(bf16[192,2048]{1,0:T(8,128)(2,1)} %get-tuple-element.80) | copy-start | bytes 2359300

commit v7 on v6

--- a/solution.py
+++ b/solution.py
@@ -1959,13 +1959,8 @@
 
 
 def assemble_kernel(place_ref, down, up, qkv, out, down_full, up_full, qkv_full, out_full):
-    qkv_full[...] = qkv[...].astype(F32)
-
-    @pl.when(pl.program_id(1) == 0)
-    def _():
-        down_full[...] = down[...].astype(F32)
-        up_full[...] = up[...].astype(F32)
-        out_full[...] = out[...].astype(F32)
+    for source, target in ((qkv, qkv_full), (down, down_full), (up, up_full), (out, out_full)):
+        target[...] = source[...].astype(F32)
 
 
 def assemble(place, down, up, qkv, out):
@@ -1976,8 +1971,10 @@
     def member(slot, place_ref):
         return jnp.bitwise_xor(slot, place_ref[0])
 
-    wide_in = pl.BlockSpec((rows, ff_cols), lambda slot, third, p: (slot, 0))
-    wide_out = pl.BlockSpec((rows, ff_cols), lambda slot, third, p: (0, member(slot, p)))
+    wide = ff_cols // 4
+    wide_in = pl.BlockSpec((rows, wide), lambda slot, q, p: (slot, q))
+    wide_out = pl.BlockSpec((rows, wide), lambda slot, q, p: (0, member(slot, p) * 4 + q))
+    out_cols = out.shape[1] // 4
     return pl.pallas_call(
         assemble_kernel,
         out_shape=(
@@ -1988,21 +1985,22 @@
         ),
         grid_spec=pltpu.PrefetchScalarGridSpec(
             num_scalar_prefetch=1,
-            grid=(4, 3),
+            grid=(4, 4),
             in_specs=[
                 wide_in,
                 wide_in,
-                pl.BlockSpec((rows, cols), lambda slot, third, p: (slot, third)),
-                pl.BlockSpec((out_rows, out.shape[1]), lambda slot, third, p: (slot, 0)),
+                pl.BlockSpec((rows, cols), lambda slot, q, p: (slot, jnp.minimum(q, 2))),
+                pl.BlockSpec((out_rows, out_cols), lambda slot, q, p: (slot, q)),
             ],
             out_specs=[
                 wide_out,
                 wide_out,
                 pl.BlockSpec(
-                    (rows, cols), lambda slot, third, p: (0, third * 4 + member(slot, p))
+                    (rows, cols),
+                    lambda slot, q, p: (0, jnp.minimum(q, 2) * 4 + member(slot, p)),
                 ),
                 pl.BlockSpec(
-                    (out_rows, out.shape[1]), lambda slot, third, p: (member(slot, p), 0)
+                    (out_rows, out_cols), lambda slot, q, p: (member(slot, p), q)
                 ),
             ],
         ),
@@ -2053,10 +2051,10 @@
         second_bias,
         down_bias,
     ] + [up_bias[k * own_d : (k + 1) * own_d] for k in range(4)]
-    row = lax.broadcasted_iota(jnp.int32, (16, own_d), 0)
-    small = jnp.zeros((16, own_d), F32)
+    flat = jnp.zeros((16 * own_d,), F32)
     for i, vector in enumerate(vectors_in):
-        small = jnp.where(row == i, vector.astype(F32)[None, :], small)
+        flat = flat + jnp.pad(vector.astype(F32), (i * own_d, (15 - i) * own_d))
+    small = flat.reshape(16, own_d)
 
     doc_id, live = token_tables(doc_lengths, doc_exit, token_skip)
     live_here = lax.dynamic_slice_in_dim(live[0], place * later_part, later_part, 0)

time: 691 us -> 686 us (level)
  no operation moved by 1% of the time
where the time goes in v7:
time: 686 us; the launch traced here: 676 us
  Pallas kernels  658 us (96%)
  local copies, waits for them, and re-layouts  11.6 us (2%)
    pallas_call x1, Pallas kernels, forward_pass(): pl.pallas_call(functools.partial(forward_kernel, (seq_size, pre_part, lat...  287 us
    pallas_call x1, Pallas kernels, attend_back(): pl.pallas_call(functools.partial(attend_back_kernel, (seq_size, pre_part,...  206 us
    pallas_call x1, Pallas kernels, feed_back(): pl.pallas_call(functools.partial(feed_back_kernel, (seq_size, pre_part, l...  149 us
    pallas_call x1, Pallas kernels, assemble(): pl.pallas_call(assemble_kernel, out_shape=(jax.ShapeDtypeStruct((rows, 4...  15.9 us

profile of v7, /device:TPU:5, one launch (start us, length us, event | category | flops | bytes accessed | tf_op | source)
XLA Modules:
  0.0 675.9 jit_solution(16086681165064967483)
XLA Ops:
  0.7 0.8 fusion.4
  1.5 0.8 convert_add_fusion
  2.3 0.6 reshape.212.small
  2.9 0.8 select_reduce_fusion
  3.8 0.7 compare_bitcast_fusion
  4.5 0.7 fusion.2
  5.2 0.1 dynamic-slice_reduce_fusion
  5.3 0.8 reshape.216.active_ref
  6.1 1.1 broadcast_in_dim.64.codes_q
  7.2 0.6 broadcast_in_dim.58.codes_k
  7.8 287.2 %forward_pass.1 = (bf16[2048,1536]{1,0:T(8,128)(2,1)}, bf16[512,2048]{1,0:T(8,128)(2,1)}, bf16[2048,2048]{1,0:T(8,128)(2,1)}, bf16[2048,2048]{1,0:T(8,128)(2,1)}...) custom-call(f32[16,256]{1,0:T(8,128)} %reshape.212.small, ...), custom_call_target="tpu_custom_call" | custom-call | flops 32212254720 | bytes 33554432 | tf_op jit(solution)/shard_map/forward_pass/pallas_call | solution.py:798
  295.0 148.7 %feed_back.1 = (bf16[1024,2048]{1,0:T(8,128)(2,1)}, bf16[1536,2048]{1,0:T(8,128)(2,1)}, bf16[1024,2048]{1,0:T(8,128)(2,1)}, bf16[2048,2048]{1,0:T(8,128)(2,1)}, ...) custom-call(bf16[2048,2048]{1,0:T(8,128)(2,1)} %get-tuple-element.54, ...), custom_call_target="tpu_custom_call" | custom-call | flops 32212254720 | bytes 33554432 | tf_op jit(solution)/shard_map/feed_back/pallas_call | solution.py:1415
  443.7 206.3 %attend_back.1 = (bf16[1024,2048]{1,0:T(8,128)(2,1)}, bf16[1024,2048]{1,0:T(8,128)(2,1)}, bf16[1024,1536]{1,0:T(8,128)(2,1)}, bf16[256,2048]{1,0:T(8,128)(2,1)},...) custom-call(bf16[2048,1536]{1,0:T(8,128)(2,1)} %get-tuple-element.65, ...), custom_call_target="tpu_custom_call" | custom-call | flops 26843545600 | bytes 33554432 | tf_op jit(solution)/shard_map/attend_back/pallas_call | solution.py:1898
  650.1 1.6 fusion.3
  651.7 15.9 %assemble.1 = (f32[256,8192]{1,0:T(8,128)}, f32[256,8192]{1,0:T(8,128)}, f32[256,6144]{1,0:T(8,128)}, f32[256,2048]{1,0:T(8,128)}) custom-call(s32[1]{0:T(128)} %bitcast.12.place_ref, bf16[1024,2048]{1,0:T(8,128)(2,1)} %get-tuple-element.82.down, bf16[1024,2048]{1,0:T(8,128)(2,1)} %get-tuple-element.83.up, bf16[1024,1536]{1,0:T(8,128)(2,1)} %get-tuple-element.84.qkv, ...), custom_call_target="tpu_custom_call" | custom-call | tf_op jit(solution)/shard_map/assemble/pallas_call | solution.py:1978
  667.6 0.8 dynamic-slice_bitcast_fusion
  668.4 0.6 copy.48
  669.0 1.0 slice_reduce_fusion
  670.0 1.2 slice.59
  671.8 0.5 divide_sqrt_fusion
  672.4 0.8 copy.53
  673.2 0.9 copy.54
  674.0 0.8 copy.55
  674.8 0.9 copy.56
  (15 shorter events, 0.2 us)
Async XLA Ops:
  651.7 20.7 %copy-start.2 = (bf16[128,2048]{1,0:T(8,128)(2,1)S(1)}, bf16[128,2048]{1,0:T(8,128)(2,1)}, u32[]{:S(2)}) copy-start(bf16[128,2048]{1,0:T(8,128)(2,1)} %get-tuple-element.63) | copy-start | bytes 1572868
  651.7 21.5 %copy-start = (bf16[192,2048]{1,0:T(8,128)(2,1)S(1)}, bf16[192,2048]{1,0:T(8,128)(2,1)}, u32[]{:S(2)}) copy-start(bf16[192,2048]{1,0:T(8,128)(2,1)} %get-tuple-element.64) | copy-start | bytes 2359300
  651.7 22.4 %copy-start.3 = (bf16[128,2048]{1,0:T(8,128)(2,1)S(1)}, bf16[128,2048]{1,0:T(8,128)(2,1)}, u32[]{:S(2)}) copy-start(bf16[128,2048]{1,0:T(8,128)(2,1)} %get-tuple-element.79) | copy-start | bytes 1572868
  667.6 7.3 %copy-start.1 = (bf16[192,2048]{1,0:T(8,128)(2,1)S(1)}, bf16[192,2048]{1,0:T(8,128)(2,1)}, u32[]{:S(2)}) copy-start(bf16[192,2048]{1,0:T(8,128)(2,1)} %get-tuple-element.80) | copy-start | bytes 2359300
